TPU v7x, 32 devices: a whole 2x2x4 slice. The times are simulated.
32 devices in a mesh: grp: 4 (over z), loc: 8 (over y, x, core).
Axes of the slice: x: 2, y: 2, z: 4, core: 2. Of those that a mesh axis runs over, the one named last changes fastest.
Arguments:
- fields: float32 [512, 4, 512], P(('grp', 'loc')), may hold values from 0 to 1
- target: int32 [512], P(('grp', 'loc')), may hold values from 0 to 127, as said below
- gradient_matrix: float32 [4, 4], replicated, may hold values from -0.05 to 0.4, as said below
- relaxation: float32 [4], replicated, may hold values from 0.04 to 0.2
- interaction: float32 [3, 4, 4], replicated, may hold values from -4 to 4
Outputs:
- evolved: float32 [512, 4, 512], P(('grp', 'loc'))
Inputs may be any that keep to these rules, and one draw needn't show every extreme that they name: Within each group, target maps the old slots one to one onto the new slots. One device sends at most 2 patches to each device of its group and receives at most 2 from each; every device sends exactly 2 patches to each device it sends to. The new slot number depends only on the group and the old slot number. `gradient_matrix`: diagonal entries lie between 0.2 and 0.4, the others between -0.05 and 0.05.
All inputs are finite; a program needn't handle non-finite values.
Results may differ from a plain program's by a relative error of at most 0.00002.
Values sent between devices are 32-bit elements; how exact they have to be, the bound alone decides.
No kernel may reach another device: no remote copies, remote signals or barrier semaphores. Data moves between devices by JAX's collectives and lax.ppermute only.
A program may use at most 64 MiB of HBM per device.

v0:
```python
import jax
import jax.numpy as jnp
from jax import lax
from jax.sharding import PartitionSpec as P

COMP = 4
B = 8
PX = 16
PZ = 1


def with_halo(block, sides, width):
    for axis, dim in sides:
        count = lax.axis_size(axis)
        forward = [(i, i + 1) for i in range(count - 1)]
        forward.append((count - 1, 0))
        backward = [(target, source) for source, target in forward]
        low = lax.ppermute(
            lax.slice_in_dim(block, block.shape[dim] - width, None, axis=dim), axis, forward
        )
        high = lax.ppermute(lax.slice_in_dim(block, 0, width, axis=dim), axis, backward)
        block = jnp.concatenate([low, block, high], axis=dim)
    return block


def reaction(components, interaction):
    count_comp = len(components)
    partials = [jnp.zeros_like(components[0]) for first_index in range(count_comp)]
    for first_index in range(count_comp):
        for second_index in range(first_index + 1, count_comp):
            first_conc = components[first_index]
            second_conc = components[second_index]
            spread_gap = first_conc - second_conc
            energy_poly = (
                interaction[0, first_index, second_index]
                + interaction[1, first_index, second_index] * spread_gap
                + interaction[2, first_index, second_index] * spread_gap * spread_gap
            )
            slope_term = (
                interaction[1, first_index, second_index]
                + 2.0 * interaction[2, first_index, second_index] * spread_gap
            )
            cross_term = first_conc * second_conc * slope_term
            partials[first_index] = partials[first_index] + second_conc * energy_poly + cross_term
            partials[second_index] = partials[second_index] + first_conc * energy_poly - cross_term
    return partials


def stacked_reaction(block_cells, interaction):
    return jnp.stack(
        reaction([block_cells[number] for number in range(block_cells.shape[0])], interaction)
    )


def second_difference(values, along):
    length = values.shape[along]

    def shifted(offset):
        return lax.slice_in_dim(values, 2 + offset, length - 2 + offset, axis=along)

    return (
        16.0 * (shifted(-1) + shifted(1)) - (shifted(-2) + shifted(2)) - 30.0 * shifted(0)
    ) / 12.0


def periodic_difference(values, along):
    return (
        16.0 * (jnp.roll(values, 1, along) + jnp.roll(values, -1, along))
        - (jnp.roll(values, 2, along) + jnp.roll(values, -2, along))
        - 30.0 * values
    ) / 12.0


def advance(padded_block, chemical, gradient_matrix, relaxation):
    center = padded_block[:, 2:-2, 2:-2]
    z_lap = second_difference(padded_block[:, :, 2:-2], 1)
    y_lap = second_difference(padded_block[:, 2:-2], 2)
    x_lap = periodic_difference(center, 3)
    laplace = z_lap + y_lap + x_lap
    smooth_terms = []
    for first_index in range(padded_block.shape[0]):
        running = gradient_matrix[first_index, 0] * laplace[0]
        for second_index in range(1, padded_block.shape[0]):
            running = running + gradient_matrix[first_index, second_index] * laplace[second_index]
        smooth_terms.append(running)
    return center - relaxation[:, None, None, None] * (chemical - jnp.stack(smooth_terms))


def deposit(patch_data, item_labels, slot_count):
    flat_data = patch_data.reshape((-1,) + patch_data.shape[2:])
    empty = jnp.zeros((slot_count,) + patch_data.shape[2:], patch_data.dtype)
    return empty.at[item_labels.reshape(-1)].set(flat_data, mode="drop")


def to_block(slot_array):
    shaped = slot_array.reshape(PZ, PX, COMP, B, B, B).transpose(2, 0, 3, 4, 1, 5)
    return shaped.reshape(COMP, PZ * B, B, PX * B)


def from_block(block_cells):
    shaped = block_cells.reshape(COMP, PZ, B, B, PX, B).transpose(1, 4, 0, 2, 3, 5)
    return shaped.reshape(PZ * PX, COMP, B * B * B)


def per_device(fields, target, gradient_matrix, relaxation, interaction):
    slot_count = fields.shape[0]
    cell_count = fields.shape[2]
    peer_count = lax.axis_size("loc")
    capacity = (slot_count + peer_count - 1) // peer_count
    home_loc = target // slot_count
    new_slot = target % slot_count
    same_home = (home_loc[:, None] == home_loc[None, :]).astype(jnp.int32)
    earlier = jnp.sum(jnp.tril(same_home, -1), axis=1)
    position = home_loc * capacity + earlier
    outbound = (
        jnp.zeros((peer_count * capacity, COMP, cell_count), jnp.float32).at[position].set(fields)
    )
    outbound = outbound.reshape(peer_count, capacity, COMP, cell_count)
    labels = jnp.full((peer_count * capacity,), slot_count, jnp.int32).at[position].set(new_slot)
    labels = labels.reshape(peer_count, capacity)
    patch_data, item_labels = (
        lax.all_to_all(outbound, "loc", split_axis=0, concat_axis=0, tiled=True),
        lax.all_to_all(labels, "loc", split_axis=0, concat_axis=0, tiled=True),
    )
    arrived = deposit(patch_data, item_labels, slot_count)
    current = to_block(arrived)
    for repeat in range(2):
        padded = with_halo(current, (("grp", 1), ("loc", 2)), 2)
        chemical = stacked_reaction(current, interaction)
        current = advance(padded, chemical, gradient_matrix, relaxation)
    return from_block(current)


def solution(mesh):
    placed = (P(("grp", "loc"), None, None), P(("grp", "loc")), P(), P(), P())
    return jax.shard_map(
        per_device,
        mesh=mesh,
        in_specs=placed,
        out_specs=P(("grp", "loc"), None, None),
        check_vma=False,
    )
```

profile of v0, /device:TPU:0, one launch (start us, length us, event | category | flops | bytes accessed | tf_op | source)
XLA Modules:
  0.0 174.3 jit_solution(15846009409256703852)
XLA Ops:
  2.2 5.2 %all-to-all-start = ((s32[8,1,2]{2,1,0:T(1,128)}), s32[8,1,2]{2,1,0:T(1,128)S(1)}, u32[]{:S(2)}, u32[]{:S(2)}) async-start(s32[8,1,2]{2,1,0:T(1,128)} %bitcast), calls=%async_computation | async-start | bytes 8192 | tf_op jit(solution)/shard_map/all_to_all | solution.py:123
  7.3 2.0 %fusion.95 = (f32[1,1]{1,0:T(1,128)}, f32[1,1]{1,0:T(1,128)}, f32[1,1]{1,0:T(1,128)}, f32[1,1]{1,0:T(1,128)}, f32[1,1]{1,0:T(1,128)}, /*index=5*/f32[1,1]{1,0:T(...) fusion(f32[4,4]{1,0:T(4,128)} %param.7), kind=kLoop, calls=%fused_computation.208 | loop fusion | bytes 128 | tf_op jit(solution)/shard_map/slice | solution.py:82
  15.4 2.4 %scatter_fusion = f32[16,4,512]{2,1,0:T(4,128)} fusion(f32[16,4,512]{2,1,0:T(4,128)} %broadcast.557.clone, s32[16]{0:T(128)S(1)} %compare_select_fusion.1, f32[16,4,512]{2,1,0:T(4,128)} %param.5), kind=kCustom, calls=%fused_computation.1 | custom fusion | bytes 393280 | tf_op jit(solution)/shard_map/scatter | solution.py:116
  17.8 4.2 %all-to-all-start.1 = ((f32[8,2,4,512]{3,2,1,0:T(4,128)}), f32[8,2,4,512]{3,2,1,0:T(4,128)S(1)}, u32[]{:S(2)}, u32[]{:S(2)}) async-start(f32[8,2,4,512]{3,2,1,0:T(4,128)} %bitcast.2), calls=%async_computation.1 | async-start | bytes 262144 | tf_op jit(solution)/shard_map/all_to_all | solution.py:122
  23.4 4.2 %all-to-all-done.1 = f32[8,2,4,512]{3,2,1,0:T(4,128)S(1)} async-done(((f32[8,2,4,512]{3,2,1,0:T(4,128)}), f32[8,2,4,512]{3,2,1,0:T(4,128)S(1)}, u32[]{:S(2)}, u32[]{:S(2)}) %all-to-all-start.1) | async-done | bytes 131104 | tf_op jit(solution)/shard_map/all_to_all | solution.py:122
  29.0 6.7 %add_add_fusion = f32[1,1,8,8,16,8]{4,5,3,2,0,1:T(8,128)} fusion(f32[]{:T(128)S(6)} %mul.1486, f32[]{:T(128)} %bitcast.24, f32[]{:T(128)} %bitcast.23, f32[]{:T(128)} %bitcast.22, f32[]{:T(128)S(6)} %mul.1462, f32[]{:T(128)} %bitcast.18, f32[]{:T(128)} %bitcast.17, f32[]{:T(128)} %bitcast.16, f32[]{:T(128)S(6)} %mul.1439, f32[]{:T(128)} %bitcast.12, ...), kind=kLoop, calls=%fused_computation.23 | loop fusion | flops 311296 | bytes 163888 | tf_op jit(solution)/shard_map/add | solution.py:44
  35.7 6.7 %add_add_fusion.1 = f32[1,1,8,8,16,8]{4,5,3,2,0,1:T(8,128)} fusion(f32[]{:T(128)S(6)} %mul.1473, f32[]{:T(128)} %bitcast.21, f32[]{:T(128)} %bitcast.20, f32[]{:T(128)} %bitcast.19, f32[]{:T(128)S(6)} %mul.1462, f32[]{:T(128)} %bitcast.18, f32[]{:T(128)} %bitcast.17, f32[]{:T(128)} %bitcast.16, f32[]{:T(128)S(6)} %mul.1428, f32[]{:T(128)} %bitcast.9, ...), kind=kLoop, calls=%fused_computation.25 | loop fusion | flops 311296 | bytes 163888 | tf_op jit(solution)/shard_map/add | solution.py:44
  42.4 6.5 %fusion.82 = (f32[1,1,8,8,16,8]{4,5,3,2,0,1:T(8,128)S(1)}, f32[1,1,8,8,16,8]{4,5,3,2,0,1:T(8,128)}) fusion(f32[4,1,8,8,16,8]{4,5,3,2,0,1:T(8,128)S(1)} %bitcast.86, f32[]{:T(128)S(6)} %mul.1450, f32[]{:T(128)} %bitcast.15, f32[]{:T(128)} %bitcast.14, f32[]{:T(128)} %bitcast.13, f32[]{:T(128)S(6)} %mul.1439, f32[]{:T(128)} %bitcast.12, f32[]{:T(128)} %bitcast.11, ...), kind=kLoop, calls=%fused_computation.195 | loop fusion | flops 311296 | bytes 196656 | tf_op jit(solution)/shard_map/slice | solution.py:51
  48.9 6.7 %fusion.81 = (f32[1,1,8,8,16,8]{4,5,3,2,0,1:T(8,128)S(1)}, f32[1,1,8,8,16,8]{4,5,3,2,0,1:T(8,128)}, f32[1,1,8,8,16,8]{4,5,3,2,0,1:T(8,128)S(1)}, f32[1,1,8,8,16,8]{4,5,3,2,0,1:T(8,128)S(1)}) fusion(f32[4,1,8,8,16,8]{4,5,3,2,0,1:T(8,128)S(1)} %bitcast.87, f32[]{:T(128)S(6)} %mul.1486, f32[]{:T(128)} %bitcast.24, f32[]{:T(128)} %bitcast.23, f32[]{:T(128)} %bitcast.22, ...), kind=kLoop, calls=%fused_computation.194 | loop fusion | flops 311296 | bytes 262192 | tf_op jit(solution)/shard_map/slice | solution.py:51
  57.6 5.7 %add_add_fusion.6 = f32[1,8,8,128]{3,2,1,0:T(8,128)S(1)} fusion(f32[1,8,8,128]{3,2,1,0:T(8,128)S(1)} %squeeze.113, f32[1,8,8,128]{3,2,1,0:T(8,128)S(1)} %squeeze.112, f32[1,8,8,128]{3,2,1,0:T(8,128)S(1)} %squeeze.110, f32[1,8,8,128]{3,2,1,0:T(8,128)S(1)} %squeeze.111, f32[]{:T(128)S(6)} %mul.1486, f32[]{:T(128)} %bitcast.24, f32[]{:T(128)} %bitcast.23, ...), kind=kLoop, calls=%fused_computation.151 | loop fusion | flops 311296 | bytes 163888 | tf_op jit(solution)/shard_map/add | solution.py:44
  63.3 5.7 %add_add_fusion.7 = f32[1,8,8,128]{3,2,1,0:T(8,128)S(1)} fusion(f32[1,8,8,128]{3,2,1,0:T(8,128)S(1)} %squeeze.113, f32[1,8,8,128]{3,2,1,0:T(8,128)S(1)} %squeeze.110, f32[1,8,8,128]{3,2,1,0:T(8,128)S(1)} %squeeze.112, f32[1,8,8,128]{3,2,1,0:T(8,128)S(1)} %squeeze.111, f32[]{:T(128)S(6)} %mul.1473, f32[]{:T(128)} %bitcast.21, f32[]{:T(128)} %bitcast.20, ...), kind=kLoop, calls=%fused_computation.153 | loop fusion | flops 311296 | bytes 163888 | tf_op jit(solution)/shard_map/add | solution.py:44
  72.7 5.6 %add_add_fusion.8 = f32[1,8,8,128]{3,2,1,0:T(8,128)S(1)} fusion(f32[1,8,8,128]{3,2,1,0:T(8,128)S(1)} %squeeze.113, f32[1,8,8,128]{3,2,1,0:T(8,128)S(1)} %squeeze.111, f32[1,8,8,128]{3,2,1,0:T(8,128)S(1)} %squeeze.112, f32[1,8,8,128]{3,2,1,0:T(8,128)S(1)} %squeeze.110, f32[]{:T(128)S(6)} %mul.1450, f32[]{:T(128)} %bitcast.15, f32[]{:T(128)} %bitcast.14, ...), kind=kLoop, calls=%fused_computation.160 | loop fusion | flops 311296 | bytes 163888 | tf_op jit(solution)/shard_map/add | solution.py:44
  78.3 2.3 %collective-permute-start.1 = (f32[4,2,8,128]{3,2,1,0:T(8,128)S(1)}, f32[4,2,8,128]{3,2,1,0:T(8,128)S(1)}, u32[]{:S(2)}, u32[]{:S(2)}) collective-permute-start(f32[4,2,8,128]{3,2,1,0:T(8,128)S(1)} %get-tuple-element.44), channel_id=1, source_target_pairs={{8,0},{16,8},{24,16},{0,24},{9,1},{17,9},{25,17},{1,25},{10,2},{18... | collective-permute-start | bytes 98312 | tf_op jit(solution)/shard_map/ppermute | solution.py:21
  82.4 2.6 %collective-permute-start.3 = (f32[4,12,2,128]{3,2,1,0:T(2,128)S(1)}, f32[4,12,2,128]{3,2,1,0:T(2,128)S(1)}, u32[]{:S(2)}, u32[]{:S(2)}) collective-permute-start(f32[4,12,2,128]{3,2,1,0:T(2,128)S(1)} %get-tuple-element.14), channel_id=1, source_target_pairs={{1,0},{2,1},{3,2},{4,3},{5,4},{6,5},{7,6},{0,7},{9,8},{10,9},{11,1... | collective-permute-start | bytes 147464 | tf_op jit(solution)/shard_map/ppermute | solution.py:21
  85.0 5.7 %add_subtract_fusion.2 = f32[1,8,8,128]{3,2,1,0:T(8,128)S(1)} fusion(f32[1,8,8,128]{3,2,1,0:T(8,128)S(1)} %squeeze.112, f32[1,8,8,128]{3,2,1,0:T(8,128)S(1)} %squeeze.110, f32[1,8,8,128]{3,2,1,0:T(8,128)S(1)} %squeeze.111, f32[1,8,8,128]{3,2,1,0:T(8,128)S(1)} %squeeze.113, f32[]{:T(128)S(6)} %mul.1486, f32[]{:T(128)} %bitcast.24, f32[]{:T(128)} %bitcast.23, ...), kind=kLoop, calls=%fused_computation.149 | loop fusion | flops 311296 | bytes 163888 | tf_op jit(solution)/shard_map/sub | solution.py:45
  91.0 4.9 %multiply_add_fusion.5 = (f32[1,8,8,128]{3,2,1,0:T(8,128)S(1)}, f32[1,8,8,128]{3,2,1,0:T(8,128)S(1)}) fusion(f32[4,8,8,128]{3,2,1,0:T(8,128)S(1)} %fusion.37, f32[]{:T(128)} %bitcast.36, f32[]{:T(128)} %bitcast.35, f32[]{:T(128)} %bitcast.34, f32[]{:T(128)} %bitcast.33, f32[]{:T(128)} %bitcast.40, f32[]{:T(128)} %bitcast.39, f32[]{:T(128)} %bitcast.38, ...), kind=kLoop, calls=%fused_computation.171 | loop fusion | flops 114688 | bytes 196640 | tf_op jit(solution)/shard_map/add | solution.py:84
  96.0 5.1 %multiply_add_fusion.7 = (f32[1,8,8,128]{3,2,1,0:T(8,128)S(1)}, f32[1,8,8,128]{3,2,1,0:T(8,128)S(1)}) fusion(f32[4,8,8,128]{3,2,1,0:T(8,128)S(1)} %fusion.37, f32[]{:T(128)} %bitcast.28, f32[]{:T(128)} %bitcast.27, f32[]{:T(128)} %bitcast.26, f32[]{:T(128)} %bitcast.25, f32[]{:T(128)} %bitcast.32, f32[]{:T(128)} %bitcast.31, f32[]{:T(128)} %bitcast.30, ...), kind=kLoop, calls=%fused_computation.173 | loop fusion | flops 114688 | bytes 196640 | tf_op jit(solution)/shard_map/add | solution.py:84
  101.1 5.7 %add_add_fusion.4 = f32[1,8,8,128]{3,2,1,0:T(8,128)S(1)} fusion(f32[4,8,8,128]{3,2,1,0:T(8,128)S(1)} %fusion.46, f32[]{:T(128)S(6)} %mul.1473, f32[]{:T(128)} %bitcast.21, f32[]{:T(128)} %bitcast.20, f32[]{:T(128)} %bitcast.19, f32[]{:T(128)S(6)} %mul.1462, f32[]{:T(128)} %bitcast.18, f32[]{:T(128)} %bitcast.17, f32[]{:T(128)} %bitcast.16, f32[]{:T(128)S(6)} %mul.1428, ...), kind=kLoop, calls=%fused_computation.132 | loop fusion | flops 311296 | bytes 163888 | tf_op jit(solution)/shard_map/add | solution.py:44
  106.9 6.2 %add_add_fusion.5 = f32[1,8,8,128]{3,2,1,0:T(8,128)} fusion(f32[4,8,8,128]{3,2,1,0:T(8,128)S(1)} %fusion.46, f32[]{:T(128)S(6)} %mul.1450, f32[]{:T(128)} %bitcast.15, f32[]{:T(128)} %bitcast.14, f32[]{:T(128)} %bitcast.13, f32[]{:T(128)S(6)} %mul.1439, f32[]{:T(128)} %bitcast.12, f32[]{:T(128)} %bitcast.11, f32[]{:T(128)} %bitcast.10, f32[]{:T(128)S(6)} %mul.1428, ...), kind=kLoop, calls=%fused_computation.139 | loop fusion | flops 311296 | bytes 163888 | tf_op jit(solution)/shard_map/add | solution.py:44
  117.6 2.5 %collective-permute-start.5 = (f32[4,2,8,128]{3,2,1,0:T(8,128)S(1)}, f32[4,2,8,128]{3,2,1,0:T(8,128)S(1)}, u32[]{:S(2)}, u32[]{:S(2)}) collective-permute-start(f32[4,2,8,128]{3,2,1,0:T(8,128)S(1)} %get-tuple-element.28), channel_id=1, source_target_pairs={{8,0},{16,8},{24,16},{0,24},{9,1},{17,9},{25,17},{1,25},{10,2},{18... | collective-permute-start | bytes 98312 | tf_op jit(solution)/shard_map/ppermute | solution.py:21
  120.1 6.3 %add_add_fusion.3 = f32[1,8,8,128]{3,2,1,0:T(8,128)} fusion(f32[4,8,8,128]{3,2,1,0:T(8,128)S(1)} %fusion.46, f32[]{:T(128)S(6)} %mul.1486, f32[]{:T(128)} %bitcast.24, f32[]{:T(128)} %bitcast.23, f32[]{:T(128)} %bitcast.22, f32[]{:T(128)S(6)} %mul.1462, f32[]{:T(128)} %bitcast.18, f32[]{:T(128)} %bitcast.17, f32[]{:T(128)} %bitcast.16, f32[]{:T(128)S(6)} %mul.1439, ...), kind=kLoop, calls=%fused_computation.130 | loop fusion | flops 311296 | bytes 163888 | tf_op jit(solution)/shard_map/add | solution.py:44
  127.1 2.6 %collective-permute-start.7 = (f32[4,12,2,128]{3,2,1,0:T(2,128)}, f32[4,12,2,128]{3,2,1,0:T(2,128)}, u32[]{:S(2)}, u32[]{:S(2)}) collective-permute-start(f32[4,12,2,128]{3,2,1,0:T(2,128)} %get-tuple-element.12), channel_id=1, source_target_pairs={{1,0},{2,1},{3,2},{4,3},{5,4},{6,5},{7,6},{0,7},{9,8},{10,9},{11,1... | collective-permute-start | bytes 147464 | tf_op jit(solution)/shard_map/ppermute | solution.py:21
  129.7 6.3 %add_subtract_fusion.1 = f32[1,8,8,128]{3,2,1,0:T(8,128)} fusion(f32[4,8,8,128]{3,2,1,0:T(8,128)S(1)} %fusion.46, f32[]{:T(128)S(6)} %mul.1486, f32[]{:T(128)} %bitcast.24, f32[]{:T(128)} %bitcast.23, f32[]{:T(128)} %bitcast.22, f32[]{:T(128)S(6)} %mul.1473, f32[]{:T(128)} %bitcast.21, f32[]{:T(128)} %bitcast.20, f32[]{:T(128)} %bitcast.19, f32[]{:T(128)S(6)} %mul.1450, ...), kind=kLoop, calls=%fused_computation.128 | loop fusion | flops 311296 | bytes 163888 | tf_op jit(solution)/shard_map/sub | solution.py:45
  137.3 1.9 %stack.67 = f32[1,1,8,8,16,8]{5,4,3,2,1,0:T(8,128)} reshape(f32[1,8,8,128]{3,2,1,0:T(8,128)} %add_subtract_fusion.1) | data formatting | bytes 65536 | tf_op jit(solution)/shard_map/stack | solution.py:50
  139.1 2.0 %copy.59 = f32[1,1,8,8,16,8]{4,5,3,2,0,1:T(8,128)} copy(f32[1,1,8,8,16,8]{5,4,3,2,1,0:T(8,128)} %stack.67) | data formatting | bytes 65536 | tf_op jit(solution)/shard_map/stack | solution.py:50
  141.1 1.8 %stack.66 = f32[1,1,8,8,16,8]{5,4,3,2,1,0:T(8,128)} reshape(f32[1,8,8,128]{3,2,1,0:T(8,128)} %add_add_fusion.3) | data formatting | bytes 65536 | tf_op jit(solution)/shard_map/stack | solution.py:50
  142.9 1.9 %copy.58 = f32[1,1,8,8,16,8]{4,5,3,2,0,1:T(8,128)} copy(f32[1,1,8,8,16,8]{5,4,3,2,1,0:T(8,128)} %stack.66) | data formatting | bytes 65536 | tf_op jit(solution)/shard_map/stack | solution.py:50
  145.9 1.9 %copy.56 = f32[1,1,8,8,16,8]{4,5,3,2,0,1:T(8,128)} copy(f32[1,1,8,8,16,8]{5,4,3,2,1,0:T(8,128)} %stack.64) | data formatting | bytes 65536 | tf_op jit(solution)/shard_map/stack | solution.py:50
  149.0 2.0 %copy.57 = f32[1,1,8,8,16,8]{4,5,3,2,0,1:T(8,128)} copy(f32[1,1,8,8,16,8]{5,4,3,2,1,0:T(8,128)} %stack.65) | data formatting | bytes 65536 | tf_op jit(solution)/shard_map/stack | solution.py:50
  156.1 4.9 %multiply_add_fusion.1 = (f32[1,8,8,128]{3,2,1,0:T(8,128)S(1)}, f32[1,8,8,128]{3,2,1,0:T(8,128)S(1)}) fusion(f32[4,8,8,128]{3,2,1,0:T(8,128)S(1)} %fusion.25, f32[]{:T(128)} %bitcast.36, f32[]{:T(128)} %bitcast.35, f32[]{:T(128)} %bitcast.34, f32[]{:T(128)} %bitcast.33, f32[]{:T(128)} %bitcast.40, f32[]{:T(128)} %bitcast.39, f32[]{:T(128)} %bitcast.38, ...), kind=kLoop, calls=%fused_computation.125 | loop fusion | flops 114688 | bytes 196640 | tf_op jit(solution)/shard_map/add | solution.py:84
  161.1 5.0 %multiply_add_fusion.3 = (f32[1,8,8,128]{3,2,1,0:T(8,128)S(1)}, f32[1,8,8,128]{3,2,1,0:T(8,128)S(1)}) fusion(f32[4,8,8,128]{3,2,1,0:T(8,128)S(1)} %fusion.25, f32[]{:T(128)} %bitcast.28, f32[]{:T(128)} %bitcast.27, f32[]{:T(128)} %bitcast.26, f32[]{:T(128)} %bitcast.25, f32[]{:T(128)} %bitcast.32, f32[]{:T(128)} %bitcast.31, f32[]{:T(128)} %bitcast.30, ...), kind=kLoop, calls=%fused_computation.127 | loop fusion | flops 114688 | bytes 196640 | tf_op jit(solution)/shard_map/add | solution.py:84
  171.0 2.4 %fusion.2 = f32[4,1,8,8,16,8]{4,5,3,2,0,1:T(8,128)S(1)} fusion(f32[4,1,8,8,16,8]{4,5,3,2,0,1:T(8,128)S(1)} %bitcast.89, f32[1,1,8,8,16,8]{4,5,3,2,0,1:T(8,128)S(1)} %copy-done.2, f32[1,1,8,8,16,8]{4,5,3,2,0,1:T(8,128)S(1)} %copy-done, f32[1,1,8,8,16,8]{4,5,3,2,0,1:T(8,128)S(1)} %copy-done.1, f32[1,1,8,8,16,8]{4,5,3,2,0,1:T(8,128)} %get-tuple-element.10, ...), kind=kLoop, calls=%fused_computation.6 | loop fusion | flops 589824 | bytes 786448 | tf_op jit(solution)/shard_map/sub | solution.py:86
  (96 shorter events, 34.5 us)
Async XLA Ops:
  2.2 15.7 %all-to-all-start = ((s32[8,1,2]{2,1,0:T(1,128)}), s32[8,1,2]{2,1,0:T(1,128)S(1)}, u32[]{:S(2)}, u32[]{:S(2)}) async-start(s32[8,1,2]{2,1,0:T(1,128)} %bitcast), calls=%async_computation | async-start | bytes 8192 | tf_op jit(solution)/shard_map/all_to_all | solution.py:123
  17.8 9.7 %all-to-all-start.1 = ((f32[8,2,4,512]{3,2,1,0:T(4,128)}), f32[8,2,4,512]{3,2,1,0:T(4,128)S(1)}, u32[]{:S(2)}, u32[]{:S(2)}) async-start(f32[8,2,4,512]{3,2,1,0:T(4,128)} %bitcast.2), calls=%async_computation.1 | async-start | bytes 262144 | tf_op jit(solution)/shard_map/all_to_all | solution.py:122
  71.0 30.1 %copy-start.10 = (f32[4]{0:T(128)S(1)}, f32[4]{0:T(128)}, u32[]{:S(2)}) copy-start(f32[4]{0:T(128)} %param.8) | copy-start | bytes 52
  71.1 9.5 %collective-permute-start = (f32[4,2,8,128]{3,2,1,0:T(8,128)S(1)}, f32[4,2,8,128]{3,2,1,0:T(8,128)S(1)}, u32[]{:S(2)}, u32[]{:S(2)}) collective-permute-start(f32[4,2,8,128]{3,2,1,0:T(8,128)S(1)} %get-tuple-element.45), channel_id=1, source_target_pairs={{0,8},{8,16},{16,24},{24,0},{1,9},{9,17},{17,25},{25,1},{2,10},{10... | collective-permute-start | bytes 98312 | tf_op jit(solution)/shard_map/ppermute | solution.py:18
  78.3 4.0 %collective-permute-start.1 = (f32[4,2,8,128]{3,2,1,0:T(8,128)S(1)}, f32[4,2,8,128]{3,2,1,0:T(8,128)S(1)}, u32[]{:S(2)}, u32[]{:S(2)}) collective-permute-start(f32[4,2,8,128]{3,2,1,0:T(8,128)S(1)} %get-tuple-element.44), channel_id=1, source_target_pairs={{8,0},{16,8},{24,16},{0,24},{9,1},{17,9},{25,17},{1,25},{10,2},{18... | collective-permute-start | bytes 98312 | tf_op jit(solution)/shard_map/ppermute | solution.py:21
  82.3 8.4 %collective-permute-start.2 = (f32[4,12,2,128]{3,2,1,0:T(2,128)S(1)}, f32[4,12,2,128]{3,2,1,0:T(2,128)S(1)}, u32[]{:S(2)}, u32[]{:S(2)}) collective-permute-start(f32[4,12,2,128]{3,2,1,0:T(2,128)S(1)} %get-tuple-element.13), channel_id=1, source_target_pairs={{0,1},{1,2},{2,3},{3,4},{4,5},{5,6},{6,7},{7,0},{8,9},{9,10},{10,1... | collective-permute-start | bytes 147464 | tf_op jit(solution)/shard_map/ppermute | solution.py:18
  82.4 8.4 %collective-permute-start.3 = (f32[4,12,2,128]{3,2,1,0:T(2,128)S(1)}, f32[4,12,2,128]{3,2,1,0:T(2,128)S(1)}, u32[]{:S(2)}, u32[]{:S(2)}) collective-permute-start(f32[4,12,2,128]{3,2,1,0:T(2,128)S(1)} %get-tuple-element.14), channel_id=1, source_target_pairs={{1,0},{2,1},{3,2},{4,3},{5,4},{6,5},{7,6},{0,7},{9,8},{10,9},{11,1... | collective-permute-start | bytes 147464 | tf_op jit(solution)/shard_map/ppermute | solution.py:21
  96.0 17.1 %copy-start.5 = (f32[1,8,8,128]{3,2,1,0:T(8,128)}, f32[1,8,8,128]{3,2,1,0:T(8,128)S(1)}, u32[]{:S(2)}) copy-start(f32[1,8,8,128]{3,2,1,0:T(8,128)S(1)} %get-tuple-element.32) | copy-start | bytes 98308
  113.1 23.9 %copy-start.6 = (f32[1,8,8,128]{3,2,1,0:T(8,128)S(1)}, f32[1,8,8,128]{3,2,1,0:T(8,128)}, u32[]{:S(2)}) copy-start(f32[1,8,8,128]{3,2,1,0:T(8,128)} %copy-done.5) | copy-start | bytes 98308
  116.0 10.3 %collective-permute-start.4 = (f32[4,2,8,128]{3,2,1,0:T(8,128)S(1)}, f32[4,2,8,128]{3,2,1,0:T(8,128)S(1)}, u32[]{:S(2)}, u32[]{:S(2)}) collective-permute-start(f32[4,2,8,128]{3,2,1,0:T(8,128)S(1)} %get-tuple-element.27), channel_id=1, source_target_pairs={{0,8},{8,16},{16,24},{24,0},{1,9},{9,17},{17,25},{25,1},{2,10},{10... | collective-permute-start | bytes 98312 | tf_op jit(solution)/shard_map/ppermute | solution.py:18
  117.6 8.8 %collective-permute-start.5 = (f32[4,2,8,128]{3,2,1,0:T(8,128)S(1)}, f32[4,2,8,128]{3,2,1,0:T(8,128)S(1)}, u32[]{:S(2)}, u32[]{:S(2)}) collective-permute-start(f32[4,2,8,128]{3,2,1,0:T(8,128)S(1)} %get-tuple-element.28), channel_id=1, source_target_pairs={{8,0},{16,8},{24,16},{0,24},{9,1},{17,9},{25,17},{1,25},{10,2},{18... | collective-permute-start | bytes 98312 | tf_op jit(solution)/shard_map/ppermute | solution.py:21
  126.4 16.5 %copy-start.7 = (f32[4,2,8,128]{3,2,1,0:T(8,128)}, f32[4,2,8,128]{3,2,1,0:T(8,128)S(1)}, u32[]{:S(2)}) copy-start(f32[4,2,8,128]{3,2,1,0:T(8,128)S(1)} %collective-permute-done.4) | copy-start | bytes 98308
  126.4 16.5 %copy-start.8 = (f32[4,2,8,128]{3,2,1,0:T(8,128)}, f32[4,2,8,128]{3,2,1,0:T(8,128)S(1)}, u32[]{:S(2)}) copy-start(f32[4,2,8,128]{3,2,1,0:T(8,128)S(1)} %collective-permute-done.5) | copy-start | bytes 98308
  127.1 27.4 %collective-permute-start.6 = (f32[4,12,2,128]{3,2,1,0:T(2,128)}, f32[4,12,2,128]{3,2,1,0:T(2,128)}, u32[]{:S(2)}, u32[]{:S(2)}) collective-permute-start(f32[4,12,2,128]{3,2,1,0:T(2,128)} %get-tuple-element.11), channel_id=1, source_target_pairs={{0,1},{1,2},{2,3},{3,4},{4,5},{5,6},{6,7},{7,0},{8,9},{9,10},{10,1... | collective-permute-start | bytes 147464 | tf_op jit(solution)/shard_map/ppermute | solution.py:18
  127.1 27.4 %collective-permute-start.7 = (f32[4,12,2,128]{3,2,1,0:T(2,128)}, f32[4,12,2,128]{3,2,1,0:T(2,128)}, u32[]{:S(2)}, u32[]{:S(2)}) collective-permute-start(f32[4,12,2,128]{3,2,1,0:T(2,128)} %get-tuple-element.12), channel_id=1, source_target_pairs={{1,0},{2,1},{3,2},{4,3},{5,4},{6,5},{7,6},{0,7},{9,8},{10,9},{11,1... | collective-permute-start | bytes 147464 | tf_op jit(solution)/shard_map/ppermute | solution.py:21
  137.3 7.6 %copy-start.9 = (f32[1,8,8,128]{3,2,1,0:T(8,128)S(1)}, f32[1,8,8,128]{3,2,1,0:T(8,128)}, u32[]{:S(2)}) copy-start(f32[1,8,8,128]{3,2,1,0:T(8,128)} %add_add_fusion.5) | copy-start | bytes 98308
  167.4 3.6 %copy-start = (f32[1,1,8,8,16,8]{4,5,3,2,0,1:T(8,128)S(1)}, f32[1,1,8,8,16,8]{4,5,3,2,0,1:T(8,128)}, u32[]{:S(2)}) copy-start(f32[1,1,8,8,16,8]{4,5,3,2,0,1:T(8,128)} %add_add_fusion) | copy-start | bytes 98308
  167.4 3.6 %copy-start.1 = (f32[1,1,8,8,16,8]{4,5,3,2,0,1:T(8,128)S(1)}, f32[1,1,8,8,16,8]{4,5,3,2,0,1:T(8,128)}, u32[]{:S(2)}) copy-start(f32[1,1,8,8,16,8]{4,5,3,2,0,1:T(8,128)} %add_add_fusion.1) | copy-start | bytes 98308
  167.4 3.6 %copy-start.2 = (f32[1,1,8,8,16,8]{4,5,3,2,0,1:T(8,128)S(1)}, f32[1,1,8,8,16,8]{4,5,3,2,0,1:T(8,128)}, u32[]{:S(2)}) copy-start(f32[1,1,8,8,16,8]{4,5,3,2,0,1:T(8,128)} %get-tuple-element.6) | copy-start | bytes 98308
  167.4 3.6 %copy-start.3 = (f32[1,1,8,8,16,8]{4,5,3,2,0,1:T(8,128)S(1)}, f32[1,1,8,8,16,8]{4,5,3,2,0,1:T(8,128)}, u32[]{:S(2)}) copy-start(f32[1,1,8,8,16,8]{4,5,3,2,0,1:T(8,128)} %copy.59) | copy-start | bytes 98308
  167.4 3.6 %copy-start.4 = (f32[1,1,8,8,16,8]{4,5,3,2,0,1:T(8,128)S(1)}, f32[1,1,8,8,16,8]{4,5,3,2,0,1:T(8,128)}, u32[]{:S(2)}) copy-start(f32[1,1,8,8,16,8]{4,5,3,2,0,1:T(8,128)} %copy.58) | copy-start | bytes 98308
where the time goes:
time: 176 us; the launch traced here: 174 us
  other arithmetic  100 us (57%)
  local copies, waits for them, and re-layouts  41.3 us (23%)
  starting transfers between devices  22.7 us (13%)
  waiting for transfers between devices  5.81 us (3%)
  between operations  4.15 us (2%)
    add x8, other arithmetic, reaction(): partials[first_index] + second_conc * energy_poly + cross_term  48.6 us
    add x4, other arithmetic, advance(): running + gradient_matrix[first_index, second_index] * laplace[second_index]  20 us
    another operation x8, local copies, waits for them, and re-layouts, stacked_reaction(): jnp.stack(reaction([block_cells[number] for number in range(block_cells.s...  13.7 us
    slice x2, other arithmetic, stacked_reaction(): block_cells[number]  13.2 us
    sub x2, other arithmetic, reaction(): partials[second_index] + first_conc * energy_poly - cross_term  12.1 us
    ppermute x4, starting transfers between devices, with_halo(): lax.ppermute(lax.slice_in_dim(block, 0, width, axis=dim), axis, backward)  10 us
    another operation x16, local copies, waits for them, and re-layouts, advance(): jnp.stack(smooth_terms)  9.53 us
    all_to_all x1, starting transfers between devices, per_device(): lax.all_to_all(labels, 'loc', split_axis=0, concat_axis=0, tiled=True)  5.17 us
  transfers between devices with their start and end apart: 10, of which 2 were waited for; matrix products, arithmetic and copies ran while one was open for 29% of the time, Pallas kernels for 0%

commit v1 on v0

v1 whole, which is shorter than its diff:
```python
import jax
import jax.numpy as jnp
from jax import lax
from jax.experimental import pallas as pl
from jax.experimental.pallas import tpu as pltpu
from jax.sharding import PartitionSpec as P

COMP = 4
LANES = 128
CHUNKS = 4
ROWS = CHUNKS * COMP
TOP = 8
DEPTH = 32

VMEM = pl.BlockSpec(memory_space=pltpu.VMEM)
SMEM = pl.BlockSpec(memory_space=pltpu.SMEM)


def lane_parts(shape):
    lane = lax.broadcasted_iota(jnp.int32, shape, 1)
    return lane // 64, (lane // 8) % 8, lane % 8


def pack_kernel(peers, cap, slots, target, fields, out, count, held, label):
    for peer in range(peers):
        count[peer] = 0
        for k in range(cap):
            held[peer * cap + k] = 0
            label[peer * cap + k] = slots
    for i in range(slots):
        goal = target[i]
        peer = lax.div(goal, slots)
        k = count[peer]
        count[peer] = k + 1
        held[peer * cap + k] = i
        label[peer * cap + k] = lax.rem(goal, slots)
    _, y, _ = lane_parts((COMP, LANES))
    row = lax.broadcasted_iota(jnp.int32, (8, LANES), 1)
    for peer in range(peers):
        after, before = (peer + 1) % peers, (peer - 1) % peers
        names = jnp.zeros((8, LANES), jnp.int32)
        for k in range(cap):
            own, high, low = held[peer * cap + k], held[after * cap + k], held[before * cap + k]
            names = jnp.where(row == k, label[peer * cap + k], names)
            names = jnp.where(row == cap + k, label[after * cap + k], names)
            names = jnp.where(row == 2 * cap + k, label[before * cap + k], names)
            for chunk in range(CHUNKS):
                part = slice(chunk * LANES, (chunk + 1) * LANES)
                at = k * ROWS + chunk * COMP
                out[peer, at : at + COMP, :] = fields[own, :, part]
                at += cap * ROWS
                out[peer, at : at + COMP, :] = jnp.where(y < 4, fields[high, :, part], fields[low, :, part])
        out[peer, 2 * cap * ROWS :, :] = names.astype(jnp.float32)


def place_kernel(peers, cap, slots, got, block, high, low, up, down):
    half = ROWS // 2
    _, y, _ = lane_parts((COMP, LANES))
    for peer in range(peers):
        names = got[peer, 2 * cap * ROWS : 2 * cap * ROWS + 1, :].astype(jnp.int32)
        for k in range(cap):
            slot = names[0, k]
            index = jnp.where(slot == slots, slots + 2, slot + 1)
            block[index] = got[peer, k * ROWS : (k + 1) * ROWS, :]
            joined = got[peer, (cap + k) * ROWS : (cap + k + 1) * ROWS, :]
            high[names[0, cap + k]] = joined
            low[names[0, 2 * cap + k]] = joined
    block[0] = block[slots]
    block[slots + 1] = block[1]
    up[: slots + 2] = block[: slots + 2, half:, :]
    down[: slots + 2] = block[: slots + 2, :half, :]
    last = ROWS - COMP
    for t in range(slots):
        at = (t % 2) * COMP
        up[slots + 2 + t // 2, at : at + COMP, :] = jnp.where(y < 4, high[t, last:, :], low[t, last:, :])
        down[slots + 2 + t // 2, at : at + COMP, :] = jnp.where(y < 4, high[t, :COMP, :], low[t, :COMP, :])


def turn(v, shift):
    return pltpu.roll(v, shift % LANES, 1)


def step(v, ahead, behind, above, below, beside, scalars):
    rates, mixing, pairs = scalars
    layer, y, x = lane_parts(v[0].shape)
    laps = []
    for c in range(COMP):
        near = turn(jnp.where(layer == 0, above[c], v[c]), 64) + turn(jnp.where(layer == 0, v[c], below[c]), 64)
        far = above[c] + below[c]
        other = turn(beside[c], 64)
        near += turn(jnp.where(y == 0, other, v[c]), -8) + turn(jnp.where(y == 7, other, v[c]), 8)
        far += turn(jnp.where(y < 2, other, v[c]), -16) + turn(jnp.where(y >= 6, other, v[c]), 16)
        plus, minus = turn(ahead[c], 8), turn(behind[c], -8)
        near += turn(jnp.where(x == 0, plus, v[c]), -1) + turn(jnp.where(x == 7, minus, v[c]), 1)
        far += turn(jnp.where(x < 2, plus, v[c]), -2) + turn(jnp.where(x >= 6, minus, v[c]), 2)
        laps.append(16.0 * near - far - 90.0 * v[c])
    drive = [None] * COMP
    for (i, j), (a, b, c) in pairs.items():
        gap = v[i] - v[j]
        bend = c * gap
        slope = b + bend
        energy = a + slope * gap
        cross = v[i] * v[j] * (slope + bend)
        first = v[j] * energy + cross
        second = v[i] * energy - cross
        drive[i] = first if drive[i] is None else drive[i] + first
        drive[j] = second if drive[j] is None else drive[j] + second
    result = []
    for i in range(COMP):
        total = v[i] - rates[i] * drive[i]
        for j in range(COMP):
            total += mixing[i][j] * laps[j]
        result.append(total)
    return result


def evolve_kernel(slots, block, high, low, below, above, gradient, relaxation, interaction, out, first, first_side, second, second_side):
    rows = slice(TOP, TOP + slots)
    rates = [relaxation[i] for i in range(COMP)]
    mixing = [[rates[i] * gradient[i, j] * (1.0 / 12.0) for j in range(COMP)] for i in range(COMP)]
    pairs = {
        (i, j): (interaction[0, i, j], interaction[1, i, j], interaction[2, i, j])
        for i in range(COMP)
        for j in range(i + 1, COMP)
    }
    scalars = rates, mixing, pairs
    half = ROWS // 2
    _, y, _ = lane_parts((slots, LANES))

    def ringed(ref, at, c, value):
        ref[at, c, rows, :] = value
        ref[at, c, TOP - 1 : TOP, :] = value[slots - 1 :]
        ref[at, c, TOP + slots : TOP + slots + 1, :] = value[:1]

    def column(ref, start, row):
        flat = ref.reshape(ref.shape[0] * ref.shape[1], LANES)
        return flat[pl.ds(start * ref.shape[1] + row, slots, stride=ref.shape[1]), :]

    def side_column(ref, c):
        flat = ref.reshape(ref.shape[0] * ref.shape[1], LANES)
        return flat[pl.ds((slots + 2) * half + c, slots, stride=COMP), :]

    for c in range(COMP):
        for chunk in range(CHUNKS):
            ringed(first, chunk + 2, c, column(block, 1, chunk * COMP + c))
            ringed(
                first_side,
                chunk + 1,
                c,
                jnp.where(y < 4, column(high, 0, chunk * COMP + c), column(low, 0, chunk * COMP + c)),
            )
        for chunk in range(2):
            ringed(first, chunk, c, column(below, 1, chunk * COMP + c))
            ringed(first, chunk + 6, c, column(above, 1, chunk * COMP + c))
        first_side[0, c, rows, :] = side_column(below, c)
        first_side[5, c, rows, :] = side_column(above, c)

    def take(ref, at, offset=0):
        return [ref[at, c, TOP + offset : TOP + offset + slots, :] for c in range(COMP)]

    def moved(ref, at, side):
        return step(take(ref, at), take(ref, at, 1), take(ref, at, -1), take(ref, at + 1), take(ref, at - 1), side, scalars)

    @pl.loop(0, CHUNKS + 2)
    def _(k):
        for c, value in enumerate(moved(first, k + 1, take(first_side, k))):
            ringed(second, k, c, value)

    @pl.loop(0, CHUNKS)
    def _(k):
        for c, value in enumerate(moved(first_side, k + 1, take(first, k + 2))):
            second_side[k, c, rows, :] = value

    @pl.loop(0, CHUNKS)
    def _(k):
        for c, value in enumerate(moved(second, k + 1, take(second_side, k))):
            out[:, c, pl.ds(pl.multiple_of(k * LANES, LANES), LANES)] = value


def per_device(fields, target, gradient_matrix, relaxation, interaction):
    slots = fields.shape[0]
    peers = lax.axis_size("loc")
    groups = lax.axis_size("grp")
    cap = (slots + peers - 1) // peers
    half = ROWS // 2
    f32 = jnp.float32

    def shape(*dims):
        return jax.ShapeDtypeStruct(dims, f32)

    sent = pl.pallas_call(
        lambda *refs: pack_kernel(peers, cap, slots, *refs),
        out_shape=shape(peers, 2 * cap * ROWS + 8, LANES),
        in_specs=[SMEM, VMEM],
        out_specs=VMEM,
        scratch_shapes=[
            pltpu.SMEM((peers,), jnp.int32),
            pltpu.SMEM((peers * cap,), jnp.int32),
            pltpu.SMEM((peers * cap,), jnp.int32),
        ],
        name="pack",
    )(target, fields)
    got = lax.all_to_all(sent, "loc", split_axis=0, concat_axis=0, tiled=True)
    block, high, low, up, down = pl.pallas_call(
        lambda *refs: place_kernel(peers, cap, slots, *refs),
        out_shape=(
            shape(slots + 3, ROWS, LANES),
            shape(slots + 1, ROWS, LANES),
            shape(slots + 1, ROWS, LANES),
            shape(slots + 2 + slots // 2, half, LANES),
            shape(slots + 2 + slots // 2, half, LANES),
        ),
        in_specs=[VMEM],
        out_specs=(VMEM,) * 5,
        name="place",
    )(got)
    forward = [(i, (i + 1) % groups) for i in range(groups)]
    backward = [(j, i) for i, j in forward]
    below = lax.ppermute(up, "grp", forward)
    above = lax.ppermute(down, "grp", backward)
    return pl.pallas_call(
        lambda *refs: evolve_kernel(slots, *refs),
        out_shape=shape(*fields.shape),
        in_specs=[VMEM] * 5 + [SMEM] * 3,
        out_specs=VMEM,
        scratch_shapes=[
            pltpu.VMEM((CHUNKS + 4, COMP, DEPTH, LANES), f32),
            pltpu.VMEM((CHUNKS + 2, COMP, DEPTH, LANES), f32),
            pltpu.VMEM((CHUNKS + 2, COMP, DEPTH, LANES), f32),
            pltpu.VMEM((CHUNKS, COMP, DEPTH, LANES), f32),
        ],
        name="evolve",
    )(block, high, low, below, above, gradient_matrix, relaxation, interaction)


def solution(mesh):
    placed = (P(("grp", "loc"), None, None), P(("grp", "loc")), P(), P(), P())
    return jax.shard_map(
        per_device,
        mesh=mesh,
        in_specs=placed,
        out_specs=P(("grp", "loc"), None, None),
        check_vma=False,
    )
```

time: 176 us -> 31.2 us (0.18)
  other arithmetic: 100 us -> 0 us
  local copies, waits for them, and re-layouts: 41.3 us -> 0.63 us
  starting transfers between devices: 22.7 us -> 3.82 us
  blocking collectives: 0 us -> 12.6 us
  Pallas kernels: 0 us -> 8.87 us
  between operations: 4.15 us -> 0.01 us
    add x14 -> x0, other arithmetic: 70.5 us -> none  [the longest x8 48.6 us: reaction(): partials[first_index] + second_conc * energy_poly + cross_term]
    another operation x26 -> x0, local copies, waits for them, and re-layouts: 23.9 us -> none  [the longest x8 13.7 us: stacked_reaction(): jnp.stack(reaction([block_cells[number] for number in range(block_cells.s...]
    sub x4 -> x0, other arithmetic: 14.5 us -> none  [the longest x2 12.1 us: reaction(): partials[second_index] + first_conc * energy_poly - cross_term]
    slice x3 -> x0, other arithmetic: 13.9 us -> none  [the longest x2 13.2 us: stacked_reaction(): block_cells[number]]
    all_to_all x0 -> x1, blocking collectives: none -> 12.6 us  [per_device(): got = lax.all_to_all(sent, 'loc', split_axis=0, concat_axis=0, tiled=True)]
    ppermute x8 -> x2, starting transfers between devices: 13.3 us -> 3.82 us  [the longest x1 2.03 us: per_device(): above = lax.ppermute(down, 'grp', backward)]
    all_to_all x2 -> x0, starting transfers between devices: 9.37 us -> none  [the longest x1 5.17 us: per_device(): lax.all_to_all(labels, 'loc', split_axis=0, concat_axis=0, tiled=True)]
    pallas_call x0 -> x3, Pallas kernels: none -> 8.87 us  [the longest x1 5.13 us: per_device(): pl.pallas_call(lambda *refs: evolve_kernel(slots, *refs), out_shape=shape...]
  transfers between devices with their start and end apart: 10 -> 2, of which waited for: 2 -> 2; matrix products, arithmetic and copies ran while one was open for 29% -> 0% of each run, Pallas kernels for 0% -> 0%
where the time goes in v1:
time: 31.2 us; the launch traced here: 30.9 us
  blocking collectives  12.6 us (40%)
  Pallas kernels  8.87 us (28%)
  waiting for transfers between devices  4.99 us (16%)
  starting transfers between devices  3.82 us (12%)
  local copies, waits for them, and re-layouts  0.63 us (2%)
    all_to_all x1, blocking collectives, per_device(): got = lax.all_to_all(sent, 'loc', split_axis=0, concat_axis=0, tiled=True)  12.6 us
    pallas_call x1, Pallas kernels, per_device(): pl.pallas_call(lambda *refs: evolve_kernel(slots, *refs), out_shape=shape...  5.13 us
    ppermute x1, waiting for transfers between devices, per_device(): below = lax.ppermute(up, 'grp', forward)  3.99 us
    ppermute x1, starting transfers between devices, per_device(): above = lax.ppermute(down, 'grp', backward)  2.03 us
    pallas_call x1, Pallas kernels, per_device(): pl.pallas_call(lambda *refs: place_kernel(peers, cap, slots, *refs), out_...  1.94 us
    pallas_call x1, Pallas kernels, per_device(): pl.pallas_call(lambda *refs: pack_kernel(peers, cap, slots, *refs), out_s...  1.79 us
    ppermute x1, starting transfers between devices, per_device(): below = lax.ppermute(up, 'grp', forward)  1.79 us
    ppermute x1, waiting for transfers between devices, per_device(): above = lax.ppermute(down, 'grp', backward)  1 us
  transfers between devices with their start and end apart: 2, of which 2 were waited for; matrix products, arithmetic and copies ran while one was open for 0% of the time, Pallas kernels for 0%

profile of v1, /device:TPU:0, one launch (start us, length us, event | category | flops | bytes accessed | tf_op | source)
XLA Modules:
  0.0 30.9 jit_solution(11348053142192448828)
XLA Ops:
  0.0 1.8 %pack.1 = f32[8,72,128]{2,1,0:T(8,128)} custom-call(s32[16]{0:T(128)} %refs_0_.1, f32[16,4,512]{2,1,0:T(4,128)} %refs_1_.1), custom_call_target="tpu_custom_call" | custom-call | tf_op jit(solution)/shard_map/pack/pallas_call | solution.py:191
  1.8 12.6 %all_to_all.5.refs_0_ = f32[8,72,128]{2,1,0:T(8,128)} all-to-all(f32[8,72,128]{2,1,0:T(8,128)} %pack.1), channel_id=1, replica_groups=mesh['grp'=4,'loc'=8] {'loc'}, dimensions={0} | all-to-all | bytes 589824 | tf_op jit(solution)/shard_map/all_to_all | solution.py:203
  14.4 1.9 %place.1 = (f32[19,16,128]{2,1,0:T(8,128)}, f32[17,16,128]{2,1,0:T(8,128)}, f32[17,16,128]{2,1,0:T(8,128)}, f32[26,8,128]{2,1,0:T(8,128)}, f32[26,8,128]{2,1,0:T(8,128)}) custom-call(f32[8,72,128]{2,1,0:T(8,128)} %all_to_all.5.refs_0_), custom_call_target="tpu_custom_call" | custom-call | tf_op jit(solution)/shard_map/place/pallas_call | solution.py:204
  16.3 1.8 %collective-permute-start = (f32[26,8,128]{2,1,0:T(8,128)}, f32[26,8,128]{2,1,0:T(8,128)S(1)}, u32[]{:S(2)}, u32[]{:S(2)}) collective-permute-start(f32[26,8,128]{2,1,0:T(8,128)} %get-tuple-element.13), channel_id=1, source_target_pairs={{0,8},{8,16},{16,24},{24,0},{1,9},{9,17},{17,25},{25,1},{2,10},{10... | collective-permute-start | bytes 319496 | tf_op jit(solution)/shard_map/ppermute | solution.py:219
  18.1 2.0 %collective-permute-start.1 = (f32[26,8,128]{2,1,0:T(8,128)}, f32[26,8,128]{2,1,0:T(8,128)S(1)}, u32[]{:S(2)}, u32[]{:S(2)}) collective-permute-start(f32[26,8,128]{2,1,0:T(8,128)} %get-tuple-element.14), channel_id=1, source_target_pairs={{8,0},{16,8},{24,16},{0,24},{9,1},{17,9},{25,17},{1,25},{10,2},{18... | collective-permute-start | bytes 319496 | tf_op jit(solution)/shard_map/ppermute | solution.py:220
  20.1 4.0 %collective-permute-done.refs_3_ = f32[26,8,128]{2,1,0:T(8,128)S(1)} collective-permute-done((f32[26,8,128]{2,1,0:T(8,128)}, f32[26,8,128]{2,1,0:T(8,128)S(1)}, u32[]{:S(2)}, u32[]{:S(2)}) %collective-permute-start) | collective-permute-done | bytes 106528 | tf_op jit(solution)/shard_map/ppermute | solution.py:219
  24.1 0.0 copy-start
  24.1 1.0 %collective-permute-done.1.refs_4_ = f32[26,8,128]{2,1,0:T(8,128)S(1)} collective-permute-done((f32[26,8,128]{2,1,0:T(8,128)}, f32[26,8,128]{2,1,0:T(8,128)S(1)}, u32[]{:S(2)}, u32[]{:S(2)}) %collective-permute-start.1) | collective-permute-done | bytes 106528 | tf_op jit(solution)/shard_map/ppermute | solution.py:220
  25.1 0.0 copy-start.1
  25.1 0.0 copy-done
  25.1 0.6 %copy-done.1 = f32[26,8,128]{2,1,0:T(8,128)} copy-done((f32[26,8,128]{2,1,0:T(8,128)}, f32[26,8,128]{2,1,0:T(8,128)S(1)}, u32[]{:S(2)}) %copy-start.1) | copy-done | bytes 106520
  25.8 5.1 %evolve.1 = f32[16,4,512]{2,1,0:T(4,128)} custom-call(f32[19,16,128]{2,1,0:T(8,128)} %get-tuple-element.10.refs_0_, f32[17,16,128]{2,1,0:T(8,128)} %get-tuple-element.11.refs_1_, f32[17,16,128]{2,1,0:T(8,128)} %get-tuple-element.12.refs_2_, f32[26,8,128]{2,1,0:T(8,128)} %copy-done, f32[26,8,128]{2,1,0:T(8,128)} %copy-done.1, f32[4,4]{1,0:T(4,128)} %refs_5_.1, ...), custom_call_target="tpu_custom_call" | custom-call | tf_op jit(solution)/shard_map/evolve/pallas_call | solution.py:221
Async XLA Ops:
  16.3 7.8 %collective-permute-start = (f32[26,8,128]{2,1,0:T(8,128)}, f32[26,8,128]{2,1,0:T(8,128)S(1)}, u32[]{:S(2)}, u32[]{:S(2)}) collective-permute-start(f32[26,8,128]{2,1,0:T(8,128)} %get-tuple-element.13), channel_id=1, source_target_pairs={{0,8},{8,16},{16,24},{24,0},{1,9},{9,17},{17,25},{25,1},{2,10},{10... | collective-permute-start | bytes 319496 | tf_op jit(solution)/shard_map/ppermute | solution.py:219
  18.1 7.0 %collective-permute-start.1 = (f32[26,8,128]{2,1,0:T(8,128)}, f32[26,8,128]{2,1,0:T(8,128)S(1)}, u32[]{:S(2)}, u32[]{:S(2)}) collective-permute-start(f32[26,8,128]{2,1,0:T(8,128)} %get-tuple-element.14), channel_id=1, source_target_pairs={{8,0},{16,8},{24,16},{0,24},{9,1},{17,9},{25,17},{1,25},{10,2},{18... | collective-permute-start | bytes 319496 | tf_op jit(solution)/shard_map/ppermute | solution.py:220
  24.1 1.0 %copy-start = (f32[26,8,128]{2,1,0:T(8,128)}, f32[26,8,128]{2,1,0:T(8,128)S(1)}, u32[]{:S(2)}) copy-start(f32[26,8,128]{2,1,0:T(8,128)S(1)} %collective-permute-done.refs_3_) | copy-start | bytes 319492
  25.1 0.6 %copy-start.1 = (f32[26,8,128]{2,1,0:T(8,128)}, f32[26,8,128]{2,1,0:T(8,128)S(1)}, u32[]{:S(2)}) copy-start(f32[26,8,128]{2,1,0:T(8,128)S(1)} %collective-permute-done.1.refs_4_) | copy-start | bytes 319492

commit v2 on v1

v2 whole, which is shorter than its diff:
```python
import jax
import jax.numpy as jnp
from jax import lax
from jax.experimental import pallas as pl
from jax.experimental.pallas import tpu as pltpu
from jax.sharding import PartitionSpec as P

COMP = 4
LANES = 128
CHUNKS = 4
ROWS = CHUNKS * COMP
HALF = ROWS // 2
TOP = 8
DEPTH = 32
PAIRS = [(i, j) for i in range(COMP) for j in range(i + 1, COMP)]
TABLE = COMP + COMP * COMP + 3 * len(PAIRS)

VMEM = pl.BlockSpec(memory_space=pltpu.VMEM)
SMEM = pl.BlockSpec(memory_space=pltpu.SMEM)


def lane_parts(shape):
    lane = lax.broadcasted_iota(jnp.int32, shape, 1)
    return lane // 64, (lane // 8) % 8, lane % 8


def turn(v, shift):
    return pltpu.roll(v, shift % LANES, 1)


def pack_kernel(peers, cap, slots, target, other_target, fields, other_fields, *refs):
    outs, (count, held, label) = refs[: peers // 2], refs[peers // 2 :]
    for core, goals in enumerate((target[...], other_target[...])):
        for peer in range(peers):
            count[core * peers + peer] = 0
            for k in range(cap):
                held[(core * peers + peer) * cap + k] = 0
                label[(core * peers + peer) * cap + k] = slots
        for i in range(slots):
            goal = goals[0, i]
            peer = core * peers + lax.div(goal, slots)
            k = count[peer]
            count[peer] = k + 1
            held[peer * cap + k] = i
            label[peer * cap + k] = lax.rem(goal, slots)
    _, y, _ = lane_parts((COMP, LANES))
    row = lax.broadcasted_iota(jnp.int32, (8, LANES), 1)
    me = lax.axis_index("loc")
    for j, out in enumerate(outs):
        peer = me ^ (2 * j)
        places = [lax.rem(peer + d, peers) * cap for d in (0, 1, peers - 1)]
        names = jnp.zeros((8, LANES), jnp.int32)
        for core, source in enumerate((fields, other_fields)):
            for k in range(cap):
                own, high, low = [held[core * peers * cap + at + k] for at in places]
                entry = core * cap + k
                for n, at in enumerate(places):
                    names = jnp.where(row == 2 * cap * n + entry, label[core * peers * cap + at + k], names)
                for chunk in range(CHUNKS):
                    part = slice(chunk * LANES, (chunk + 1) * LANES)
                    at = entry * ROWS + chunk * COMP
                    out[at : at + COMP, :] = source[own, :, part]
                    at += 2 * cap * ROWS
                    out[at : at + COMP, :] = jnp.where(y < 4, source[high, :, part], source[low, :, part])
        out[4 * cap * ROWS :, :] = names.astype(jnp.float32)


def entries(cap, got):
    for message in got:
        names = message[4 * cap * ROWS : 4 * cap * ROWS + 1, :].astype(jnp.int32)
        for k in range(2 * cap):
            yield message, k * ROWS, (2 * cap + k) * ROWS, names[0, k], names[0, 2 * cap + k], names[0, 4 * cap + k]


def faces_kernel(cap, slots, *refs):
    got, (up, down, high, low) = refs[:-4], refs[-4:]
    _, y, _ = lane_parts((2 * COMP, LANES))
    for message, whole, joined, slot, high_slot, low_slot in entries(cap, got):
        down[slot] = message[whole : whole + HALF, :]
        up[slot] = message[whole + HALF : whole + ROWS, :]
        for part, at in ((0, 0), (COMP, ROWS - COMP)):
            rows = message[joined + at : joined + at + COMP, :]
            high[high_slot, part : part + COMP, :] = rows
            low[low_slot, part : part + COMP, :] = rows
    pairs = slots // 2
    for q in range(pairs):
        one, two = [jnp.where(y < 4, high[t], low[t]) for t in (q, q + pairs)]
        two = jnp.where(y < 4, turn(two, 16), turn(two, -16))
        both = jnp.where((y >= 2) & (y < 6), two, one)
        at = (q % 2) * COMP
        down[slots + 1 + q // 2, at : at + COMP, :] = both[:COMP]
        up[slots + 1 + q // 2, at : at + COMP, :] = both[COMP:]


def stage_kernel(fields, target, gradient, relaxation, interaction, out, goals, table):
    out[...] = fields[...]
    goals[...] = target[...]
    for i in range(COMP):
        rate = relaxation[i]
        table[i] = rate
        for j in range(COMP):
            table[COMP + i * COMP + j] = rate * gradient[i, j] * (1.0 / 12.0)
    at = COMP + COMP * COMP
    for i, j in PAIRS:
        for order in range(3):
            table[at] = interaction[order, i, j]
            at += 1


def coefficients(table):
    rates = [table[i] for i in range(COMP)]
    mixing = [[table[COMP + i * COMP + j] for j in range(COMP)] for i in range(COMP)]
    at = COMP + COMP * COMP
    pairs = {pair: [table[at + 3 * n + order] for order in range(3)] for n, pair in enumerate(PAIRS)}
    return rates, mixing, pairs


def mixed(start, laps, mixing):
    result = []
    for i in range(COMP):
        total = start[i]
        for j in range(COMP):
            total += mixing[i][j] * laps[j]
        result.append(total)
    return result


def step(v, ahead, behind, above, below, beside, scalars):
    rates, mixing, pairs = scalars
    layer, y, x = lane_parts(v[0].shape)
    laps = []
    for c in range(COMP):
        near = turn(jnp.where(layer == 0, above[c], v[c]), 64) + turn(jnp.where(layer == 0, v[c], below[c]), 64)
        far = above[c] + below[c]
        other = turn(beside[c], 64)
        near += turn(jnp.where(y == 0, other, v[c]), -8) + turn(jnp.where(y == 7, other, v[c]), 8)
        far += turn(jnp.where(y < 2, other, v[c]), -16) + turn(jnp.where(y >= 6, other, v[c]), 16)
        plus, minus = turn(ahead[c], 8), turn(behind[c], -8)
        near += turn(jnp.where(x == 0, plus, v[c]), -1) + turn(jnp.where(x == 7, minus, v[c]), 1)
        far += turn(jnp.where(x < 2, plus, v[c]), -2) + turn(jnp.where(x >= 6, minus, v[c]), 2)
        laps.append(16.0 * near - far - 90.0 * v[c])
    drive = [None] * COMP
    for (i, j), (a, b, c) in pairs.items():
        gap = v[i] - v[j]
        bend = c * gap
        slope = b + bend
        energy = a + slope * gap
        cross = v[i] * v[j] * (slope + bend)
        first = v[j] * energy + cross
        second = v[i] * energy - cross
        drive[i] = first if drive[i] is None else drive[i] + first
        drive[j] = second if drive[j] is None else drive[j] + second
    return mixed([v[i] - rates[i] * drive[i] for i in range(COMP)], laps, mixing)


def store(slots, ref, at, values):
    for c, value in enumerate(values):
        ref[at, c, TOP : TOP + slots, :] = value
        ref[at, c, TOP - 1 : TOP, :] = value[slots - 1 :]
        ref[at, c, TOP + slots : TOP + slots + 1, :] = value[:1]


def load(slots, ref, at, offset=0):
    return [ref[at, c, TOP + offset : TOP + offset + slots, :] for c in range(COMP)]


def moved(slots, work, at, above, below, beside, scalars):
    ahead, behind = load(slots, work, at, 1), load(slots, work, at, -1)
    around = [load(slots, work, n) for n in (above, below, beside)]
    return step(load(slots, work, at), ahead, behind, *around, scalars)


def column(ref, start, count, stride):
    flat = ref.reshape(ref.shape[0] * ref.shape[1], LANES)
    return flat[pl.ds(start, count, stride=stride), :]


SPAN = CHUNKS + 2
BLOCK, SIDE, BLOCK_NEXT, SIDE_NEXT, FINAL, BELOW, ABOVE = [n * SPAN for n in range(5)] + [4 * SPAN + 2, 4 * SPAN + 3]
ENTRIES = ABOVE + 1


def inner_kernel(cap, slots, peers, *refs):
    got, (table, work, block, high, low) = refs[: peers // 2], refs[peers // 2 :]
    scalars = coefficients(table)
    _, y, _ = lane_parts((slots, LANES))
    for message, whole, joined, slot, high_slot, low_slot in entries(cap, got):
        block[slot] = message[whole : whole + ROWS, :]
        rows = message[joined : joined + ROWS, :]
        high[high_slot] = rows
        low[low_slot] = rows
    for base in range(0, FINAL, SPAN):
        for at in (base, base + SPAN - 1):
            work[at] = jnp.zeros(work.shape[1:], work.dtype)

    @pl.loop(0, CHUNKS)
    def _(k):
        rows = [k * COMP + c for c in range(COMP)]
        store(slots, work, BLOCK + 1 + k, [column(block, r, slots, ROWS) for r in rows])
        sides = [jnp.where(y < 4, column(high, r, slots, ROWS), column(low, r, slots, ROWS)) for r in rows]
        store(slots, work, SIDE + 1 + k, sides)

    @pl.loop(0, 2 * CHUNKS + 2)
    def _(n):
        late = n >= 2 * CHUNKS
        side = n // CHUNKS
        k = n % CHUNKS
        at = jnp.where(late, BLOCK_NEXT + 2 + k, side * SPAN + 1 + k)
        above = jnp.where(n == 2 * CHUNKS + 1, BLOCK_NEXT + SPAN - 1, at + 1)
        below = jnp.where(n == 2 * CHUNKS, BLOCK_NEXT, at - 1)
        beside = jnp.where(late, SIDE_NEXT + 2 + k, (1 - side) * SPAN + 1 + k)
        to = jnp.where(late, FINAL + k, BLOCK_NEXT + side * SPAN + 1 + k)
        store(slots, work, to, moved(slots, work, at, above, below, beside, scalars))


def finish(slots, end, ref, table, work, target):
    scalars = coefficients(table)
    mixing = scalars[1]
    pairs = slots // 2
    _, y, _ = lane_parts((pairs, LANES))
    layer, _, _ = lane_parts((slots, LANES))
    outside, edge = end * (SPAN - 1), 1 + end * (CHUNKS - 1)
    near, distant, side = [], [], []
    for c in range(COMP):
        near.append(column(ref, (1 - end) * COMP + c, slots, HALF))
        distant.append(column(ref, end * COMP + c, slots, HALF))
        both = column(ref, (slots + 1) * HALF + c, pairs, COMP)
        side.append(jnp.concatenate([both, jnp.where(y < 4, turn(both, -16), turn(both, 16))], axis=0))
    store(slots, work, BLOCK + outside, near)
    store(slots, work, ABOVE if end else BELOW, distant)
    store(slots, work, SIDE + outside, side)

    @pl.loop(0, 3)
    def _(kind):
        source = jnp.where(kind == 2, BLOCK_NEXT + edge, kind * SPAN + outside)
        to = jnp.where(kind == 2, FINAL + end, BLOCK_NEXT + kind * SPAN + edge)
        laps = [16.0 * turn(jnp.where(layer == 1 - end, b, 0.0), 64) - b for b in load(slots, work, source)]
        store(slots, work, to, mixed(load(slots, work, to), laps, mixing))

    @pl.loop(0, 2)
    def _(late):
        at = jnp.where(late, BLOCK_NEXT + edge, BLOCK + outside)
        beyond = jnp.where(late, BLOCK_NEXT + outside, ABOVE if end else BELOW)
        within = at + 1 - 2 * end
        beside = jnp.where(late, SIDE_NEXT + edge, SIDE + outside)
        to = jnp.where(late, BLOCK + end, BLOCK_NEXT + outside)
        above, below = (beyond, within) if end else (within, beyond)
        store(slots, work, to, moved(slots, work, at, above, below, beside, scalars))

    results = [load(slots, work, FINAL + 1), load(slots, work, BLOCK + 1)] if end else [load(slots, work, BLOCK), load(slots, work, FINAL)]

    for k, values in enumerate(results):
        for c, value in enumerate(values):
            target[:, c, k * LANES : (k + 1) * LANES] = value


def lower_kernel(slots, ref, table, _, half, work):
    finish(slots, 0, ref, table, work, half)


def upper_kernel(slots, ref, table, lower, _, out, work, half, sems):
    length = half.shape[2]
    first = pltpu.make_async_copy(lower, out.at[:, :, :length], sems.at[0])
    first.start()
    finish(slots, 1, ref, table, work, half)
    last = pltpu.make_async_copy(half, out.at[:, :, length:], sems.at[1])
    last.start()
    first.wait()
    last.wait()


def per_device(fields, target, gradient_matrix, relaxation, interaction):
    slots = fields.shape[0]
    peers = lax.axis_size("loc")
    groups = lax.axis_size("grp")
    cap = (slots + peers - 1) // peers
    chips = peers // 2
    f32 = jnp.float32
    params = pltpu.CompilerParams(vmem_limit_bytes=8 << 20)

    def shape(*dims):
        return pltpu.VMEM(dims, f32)

    def inside(*arrays):
        return [pltpu.with_memory_space_constraint(a, pltpu.VMEM) for a in arrays]

    def cross(array, flip):
        return lax.ppermute(array, "loc", [(i, i ^ flip) for i in range(peers)])

    target = target.reshape(1, slots)
    staged, goals, table = pl.pallas_call(
        stage_kernel,
        out_shape=(shape(*fields.shape), pltpu.VMEM(target.shape, jnp.int32), pltpu.SMEM((TABLE,), f32)),
        in_specs=[VMEM] * 2 + [SMEM] * 3,
        out_specs=(VMEM, VMEM, SMEM),
        name="stage",
    )(fields, target, gradient_matrix, relaxation, interaction)
    table = pltpu.with_memory_space_constraint(table, pltpu.SMEM)
    other_fields, other_target = cross(fields, 1), cross(target, 1)
    sent = pl.pallas_call(
        lambda *refs: pack_kernel(peers, cap, slots, *refs),
        out_shape=(shape(4 * cap * ROWS + 8, LANES),) * chips,
        in_specs=[VMEM] * 4,
        out_specs=(VMEM,) * chips,
        scratch_shapes=[pltpu.SMEM((2 * peers * n,), jnp.int32) for n in (1, cap, cap)],
        name="pack",
        compiler_params=params,
    )(*inside(goals, other_target, staged, other_fields))
    got = inside(sent[0], *[cross(sent[j], 2 * j) for j in range(1, chips)])
    up, down = pl.pallas_call(
        lambda *refs: faces_kernel(cap, slots, *refs),
        out_shape=(shape(slots + 1 + slots // 4, HALF, LANES),) * 2,
        in_specs=[VMEM] * chips,
        out_specs=(VMEM,) * 2,
        scratch_shapes=[pltpu.VMEM((slots + 1, HALF, LANES), f32)] * 2,
        name="faces",
        compiler_params=params,
    )(*got)
    forward = [(i, (i + 1) % groups) for i in range(groups)]
    backward = [(j, i) for i, j in forward]
    below = lax.ppermute(up, "grp", forward)
    above = lax.ppermute(down, "grp", backward)
    work = pl.pallas_call(
        lambda *refs: inner_kernel(cap, slots, peers, *refs),
        out_shape=shape(ENTRIES, COMP, DEPTH, LANES),
        in_specs=[VMEM] * chips + [SMEM],
        out_specs=VMEM,
        scratch_shapes=[pltpu.VMEM((slots + 1, ROWS, LANES), f32)] * 3,
        name="inner",
        compiler_params=params,
    )(*got, table)
    half = (slots, COMP, fields.shape[2] // 2)
    lower, work = pl.pallas_call(
        lambda *refs: lower_kernel(slots, *refs),
        out_shape=(shape(*half), shape(*work.shape)),
        in_specs=[VMEM, SMEM, VMEM],
        out_specs=(VMEM,) * 2,
        input_output_aliases={2: 1},
        name="lower",
        compiler_params=params,
    )(*inside(below), table, *inside(work))
    return pl.pallas_call(
        lambda *refs: upper_kernel(slots, *refs),
        out_shape=(jax.ShapeDtypeStruct(fields.shape, f32), shape(*work.shape)),
        in_specs=[VMEM, SMEM, VMEM, VMEM],
        out_specs=(pl.BlockSpec(memory_space=pl.ANY), VMEM),
        input_output_aliases={3: 1},
        scratch_shapes=[pltpu.VMEM(half, f32), pltpu.SemaphoreType.DMA((2,))],
        name="upper",
        compiler_params=params,
    )(*inside(above), table, *inside(lower, work))[0]


def solution(mesh):
    placed = (P(("grp", "loc"), None, None), P(("grp", "loc")), P(), P(), P())
    return jax.shard_map(
        per_device,
        mesh=mesh,
        in_specs=placed,
        out_specs=P(("grp", "loc"), None, None),
        check_vma=False,
    )
```

time: 31.2 us -> 21 us (0.67)
  blocking collectives: 12.6 us -> 0 us
  starting transfers between devices: 3.82 us -> 8.78 us
  Pallas kernels: 8.87 us -> 6.56 us
  local copies, waits for them, and re-layouts: 0.63 us -> 0 us
  waiting for transfers between devices: 4.99 us -> 5.41 us
    all_to_all x1 -> x0, blocking collectives: 12.6 us -> none  [per_device(): got = lax.all_to_all(sent, 'loc', split_axis=0, concat_axis=0, tiled=True)]
    ppermute x0 -> x5, waiting for transfers between devices: none -> 5.4 us  [cross(): return lax.ppermute(array, 'loc', [(i, i ^ flip) for i in range(peers)])]
    ppermute x0 -> x5, starting transfers between devices: none -> 4.9 us  [cross(): return lax.ppermute(array, 'loc', [(i, i ^ flip) for i in range(peers)])]
    ppermute x1, waiting for transfers between devices: 3.99 us -> 0.01 us  [per_device(): below = lax.ppermute(up, 'grp', forward)]
    pallas_call x1, Pallas kernels: 1.79 us -> 0.42 us  [per_device(): pl.pallas_call(lambda *refs: pack_kernel(peers, cap, slots, *refs), out_s...]
    ppermute x1, waiting for transfers between devices: 1 us -> 0.01 us  [per_device(): above = lax.ppermute(down, 'grp', backward)]
    pallas_call x2 -> x5, Pallas kernels: 7.07 us -> 6.14 us  [the longest x1 2.61 us: per_device(): pl.pallas_call(lambda *refs: inner_kernel(cap, slots, peers, *refs), out_...]
    unnamed x4 -> x0, local copies, waits for them, and re-layouts: 0.63 us -> none
  transfers between devices with their start and end apart: 2 -> 7, of which waited for: 2 -> 4; matrix products, arithmetic and copies ran while one was open for 0% -> 0% of each run, Pallas kernels for 0% -> 21%
where the time goes in v2:
time: 21 us; the launch traced here: 20.8 us
  starting transfers between devices  8.78 us (42%)
  Pallas kernels  6.56 us (31%)
  waiting for transfers between devices  5.41 us (26%)
    ppermute x5, waiting for transfers between devices, cross(): return lax.ppermute(array, 'loc', [(i, i ^ flip) for i in range(peers)])  5.4 us
    ppermute x5, starting transfers between devices, cross(): return lax.ppermute(array, 'loc', [(i, i ^ flip) for i in range(peers)])  4.9 us
    pallas_call x1, Pallas kernels, per_device(): pl.pallas_call(lambda *refs: inner_kernel(cap, slots, peers, *refs), out_...  2.61 us
    ppermute x1, starting transfers between devices, per_device(): above = lax.ppermute(down, 'grp', backward)  2.25 us
    ppermute x1, starting transfers between devices, per_device(): below = lax.ppermute(up, 'grp', forward)  1.63 us
    pallas_call x1, Pallas kernels, per_device(): pl.pallas_call(lambda *refs: upper_kernel(slots, *refs), out_shape=(jax.S...  1.48 us
    pallas_call x1, Pallas kernels, per_device(): pl.pallas_call(stage_kernel, out_shape=(shape(*fields.shape), pltpu.VMEM(...  0.97 us
    pallas_call x1, Pallas kernels, per_device(): pl.pallas_call(lambda *refs: lower_kernel(slots, *refs), out_shape=(shape...  0.83 us
  transfers between devices with their start and end apart: 7, of which 4 were waited for; matrix products, arithmetic and copies ran while one was open for 0% of the time, Pallas kernels for 21%

profile of v2, /device:TPU:0, one launch (start us, length us, event | category | flops | bytes accessed | tf_op | source)
XLA Modules:
  0.0 20.8 jit_solution(16325448485643532239)
XLA Ops:
  0.0 0.5 %collective-permute-start.1 = (f32[16,4,512]{2,1,0:T(4,128)}, f32[16,4,512]{2,1,0:T(4,128)S(1)}, u32[]{:S(2)}, u32[]{:S(2)}) collective-permute-start(f32[16,4,512]{2,1,0:T(4,128)} %fields.1), channel_id=1, source_target_pairs={{0,1},{1,0},{2,3},{3,2},{4,5},{5,4},{6,7},{7,6},{8,9},{9,8},{10,11... | collective-permute-start | bytes 393224 | tf_op jit(solution)/shard_map/ppermute | solution.py:288
  0.5 0.1 collective-permute-start
  0.5 1.0 %stage.1 = (f32[16,4,512]{2,1,0:T(4,128)S(1)}, s32[1,16]{1,0:T(1,128)S(1)}, f32[38]{0:T(128)S(4)}) custom-call(f32[16,4,512]{2,1,0:T(4,128)} %fields.1, s32[1,16]{1,0:T(1,128)} %bitcast.2, f32[4,4]{1,0:T(4,128)} %gradient.1, f32[4]{0:T(128)} %relaxation.1, f32[3,4,4]{2,1,0:T(4,128)} %interaction.1), custom_call_target="tpu_custom_call" | custom-call | tf_op jit(solution)/shard_map/stage/pallas_call | solution.py:291
  1.5 0.2 %collective-permute-done.refs_1_ = s32[1,16]{1,0:T(1,128)S(1)} collective-permute-done((s32[1,16]{1,0:T(1,128)}, s32[1,16]{1,0:T(1,128)S(1)}, u32[]{:S(2)}, u32[]{:S(2)}) %collective-permute-start) | collective-permute-done | bytes 96 | tf_op jit(solution)/shard_map/ppermute | solution.py:288
  1.7 0.0 collective-permute-done.1.refs_3_
  1.7 0.4 %pack.1 = (f32[136,128]{1,0:T(8,128)S(1)}, f32[136,128]{1,0:T(8,128)S(1)}, f32[136,128]{1,0:T(8,128)S(1)}, f32[136,128]{1,0:T(8,128)S(1)}) custom-call(s32[1,16]{1,0:T(1,128)S(1)} %get-tuple-element.17.refs_0_, s32[1,16]{1,0:T(1,128)S(1)} %collective-permute-done.refs_1_, f32[16,4,512]{2,1,0:T(4,128)S(1)} %get-tuple-element.18.refs_2_, ...), custom_call_target="tpu_custom_call" | custom-call | tf_op jit(solution)/shard_map/pack/pallas_call | solution.py:300
  2.1 2.9 %collective-permute-start.2 = (f32[136,128]{1,0:T(8,128)S(1)}, f32[136,128]{1,0:T(8,128)S(1)}, u32[]{:S(2)}, u32[]{:S(2)}) collective-permute-start(f32[136,128]{1,0:T(8,128)S(1)} %get-tuple-element.20), channel_id=1, source_target_pairs={{0,2},{1,3},{2,0},{3,1},{4,6},{5,7},{6,4},{7,5},{8,10},{9,11},{10,... | collective-permute-start | bytes 208904 | tf_op jit(solution)/shard_map/ppermute | solution.py:288
  5.0 1.5 %collective-permute-start.3 = (f32[136,128]{1,0:T(8,128)S(1)}, f32[136,128]{1,0:T(8,128)S(1)}, u32[]{:S(2)}, u32[]{:S(2)}) collective-permute-start(f32[136,128]{1,0:T(8,128)S(1)} %get-tuple-element.21), channel_id=1, source_target_pairs={{0,4},{1,5},{2,6},{3,7},{4,0},{5,1},{6,2},{7,3},{8,12},{9,13},{10,... | collective-permute-start | bytes 208904 | tf_op jit(solution)/shard_map/ppermute | solution.py:288
  6.5 0.0 collective-permute-start.4
  6.5 1.0 %collective-permute-done.2.refs_1_ = f32[136,128]{1,0:T(8,128)S(1)} collective-permute-done((f32[136,128]{1,0:T(8,128)S(1)}, f32[136,128]{1,0:T(8,128)S(1)}, u32[]{:S(2)}, u32[]{:S(2)}) %collective-permute-start.2) | collective-permute-done | bytes 69664 | tf_op jit(solution)/shard_map/ppermute | solution.py:288
  7.5 1.8 %collective-permute-done.3.refs_2_ = f32[136,128]{1,0:T(8,128)S(1)} collective-permute-done((f32[136,128]{1,0:T(8,128)S(1)}, f32[136,128]{1,0:T(8,128)S(1)}, u32[]{:S(2)}, u32[]{:S(2)}) %collective-permute-start.3) | collective-permute-done | bytes 69664 | tf_op jit(solution)/shard_map/ppermute | solution.py:288
  9.3 2.4 %collective-permute-done.4.refs_3_ = f32[136,128]{1,0:T(8,128)S(1)} collective-permute-done((f32[136,128]{1,0:T(8,128)S(1)}, f32[136,128]{1,0:T(8,128)S(1)}, u32[]{:S(2)}, u32[]{:S(2)}) %collective-permute-start.4) | collective-permute-done | bytes 69664 | tf_op jit(solution)/shard_map/ppermute | solution.py:288
  11.7 0.2 %faces.1 = (f32[21,8,128]{2,1,0:T(8,128)S(1)}, f32[21,8,128]{2,1,0:T(8,128)S(1)}) custom-call(f32[136,128]{1,0:T(8,128)S(1)} %get-tuple-element.19.refs_0_, f32[136,128]{1,0:T(8,128)S(1)} %collective-permute-done.2.refs_1_, f32[136,128]{1,0:T(8,128)S(1)} %collective-permute-done.3.refs_2_, f32[136,128]{1,0:T(8,128)S(1)} %collective-permute-done.4.refs_3_), custom_call_target="tpu_custom_call" | custom-call | tf_op jit(solution)/shard_map/faces/pallas_call | solution.py:310
  12.0 1.6 %collective-permute-start.6 = (f32[21,8,128]{2,1,0:T(8,128)S(1)}, f32[21,8,128]{2,1,0:T(8,128)S(1)}, u32[]{:S(2)}, u32[]{:S(2)}) collective-permute-start(f32[21,8,128]{2,1,0:T(8,128)S(1)} %get-tuple-element.25), channel_id=1, source_target_pairs={{0,8},{8,16},{16,24},{24,0},{1,9},{9,17},{17,25},{25,1},{2,10},{10... | collective-permute-start | bytes 258056 | tf_op jit(solution)/shard_map/ppermute | solution.py:321
  13.6 2.2 %collective-permute-start.5 = (f32[21,8,128]{2,1,0:T(8,128)S(1)}, f32[21,8,128]{2,1,0:T(8,128)S(1)}, u32[]{:S(2)}, u32[]{:S(2)}) collective-permute-start(f32[21,8,128]{2,1,0:T(8,128)S(1)} %get-tuple-element.23), channel_id=1, source_target_pairs={{8,0},{16,8},{24,16},{0,24},{9,1},{17,9},{25,17},{1,25},{10,2},{18... | collective-permute-start | bytes 258056 | tf_op jit(solution)/shard_map/ppermute | solution.py:322
  15.8 2.6 %inner.1.refs_2_ = f32[28,4,32,128]{3,2,1,0:T(8,128)S(1)} custom-call(f32[136,128]{1,0:T(8,128)S(1)} %get-tuple-element.19.refs_0_, f32[136,128]{1,0:T(8,128)S(1)} %collective-permute-done.2.refs_1_, f32[136,128]{1,0:T(8,128)S(1)} %collective-permute-done.3.refs_2_, f32[136,128]{1,0:T(8,128)S(1)} %collective-permute-done.4.refs_3_, ...), custom_call_target="tpu_custom_call" | custom-call | tf_op jit(solution)/shard_map/inner/pallas_call | solution.py:323
  18.5 0.0 collective-permute-done.6.refs_0_
  18.5 0.8 %lower.1 = (f32[16,4,256]{2,1,0:T(4,128)S(1)}, f32[28,4,32,128]{3,2,1,0:T(8,128)S(1)}) custom-call(f32[21,8,128]{2,1,0:T(8,128)S(1)} %collective-permute-done.6.refs_0_, f32[38]{0:T(128)S(4)} %get-tuple-element.24.refs_4_.refs_1_, f32[28,4,32,128]{3,2,1,0:T(8,128)S(1)} %inner.1.refs_2_), custom_call_target="tpu_custom_call", output_to_operand_aliasing={{1}: (2, {})} | custom-call | tf_op jit(solution)/shard_map/lower/pallas_call | solution.py:333
  19.3 0.0 collective-permute-done.5.refs_0_
  19.3 1.5 %upper.1 = (f32[16,4,512]{2,1,0:T(4,128)}, f32[28,4,32,128]{3,2,1,0:T(8,128)S(1)}) custom-call(f32[21,8,128]{2,1,0:T(8,128)S(1)} %collective-permute-done.5.refs_0_, f32[38]{0:T(128)S(4)} %get-tuple-element.24.refs_4_.refs_1_, f32[16,4,256]{2,1,0:T(4,128)S(1)} %get-tuple-element.26.refs_2_, ...), custom_call_target="tpu_custom_call", output_to_operand_aliasing={{1}: (3, {})} | custom-call | tf_op jit(solution)/shard_map/upper/pallas_call | solution.py:342
Async XLA Ops:
  0.0 1.7 %collective-permute-start.1 = (f32[16,4,512]{2,1,0:T(4,128)}, f32[16,4,512]{2,1,0:T(4,128)S(1)}, u32[]{:S(2)}, u32[]{:S(2)}) collective-permute-start(f32[16,4,512]{2,1,0:T(4,128)} %fields.1), channel_id=1, source_target_pairs={{0,1},{1,0},{2,3},{3,2},{4,5},{5,4},{6,7},{7,6},{8,9},{9,8},{10,11... | collective-permute-start | bytes 393224 | tf_op jit(solution)/shard_map/ppermute | solution.py:288
  0.5 1.3 %collective-permute-start = (s32[1,16]{1,0:T(1,128)}, s32[1,16]{1,0:T(1,128)S(1)}, u32[]{:S(2)}, u32[]{:S(2)}) collective-permute-start(s32[1,16]{1,0:T(1,128)} %bitcast.1), channel_id=1, source_target_pairs={{0,1},{1,0},{2,3},{3,2},{4,5},{5,4},{6,7},{7,6},{8,9},{9,8},{10,11... | collective-permute-start | bytes 200 | tf_op jit(solution)/shard_map/ppermute | solution.py:288
  2.1 5.4 %collective-permute-start.2 = (f32[136,128]{1,0:T(8,128)S(1)}, f32[136,128]{1,0:T(8,128)S(1)}, u32[]{:S(2)}, u32[]{:S(2)}) collective-permute-start(f32[136,128]{1,0:T(8,128)S(1)} %get-tuple-element.20), channel_id=1, source_target_pairs={{0,2},{1,3},{2,0},{3,1},{4,6},{5,7},{6,4},{7,5},{8,10},{9,11},{10,... | collective-permute-start | bytes 208904 | tf_op jit(solution)/shard_map/ppermute | solution.py:288
  5.0 4.3 %collective-permute-start.3 = (f32[136,128]{1,0:T(8,128)S(1)}, f32[136,128]{1,0:T(8,128)S(1)}, u32[]{:S(2)}, u32[]{:S(2)}) collective-permute-start(f32[136,128]{1,0:T(8,128)S(1)} %get-tuple-element.21), channel_id=1, source_target_pairs={{0,4},{1,5},{2,6},{3,7},{4,0},{5,1},{6,2},{7,3},{8,12},{9,13},{10,... | collective-permute-start | bytes 208904 | tf_op jit(solution)/shard_map/ppermute | solution.py:288
  6.5 5.2 %collective-permute-start.4 = (f32[136,128]{1,0:T(8,128)S(1)}, f32[136,128]{1,0:T(8,128)S(1)}, u32[]{:S(2)}, u32[]{:S(2)}) collective-permute-start(f32[136,128]{1,0:T(8,128)S(1)} %get-tuple-element.22), channel_id=1, source_target_pairs={{0,6},{1,7},{2,4},{3,5},{4,2},{5,3},{6,0},{7,1},{8,14},{9,15},{10,... | collective-permute-start | bytes 208904 | tf_op jit(solution)/shard_map/ppermute | solution.py:288
  12.0 6.5 %collective-permute-start.6 = (f32[21,8,128]{2,1,0:T(8,128)S(1)}, f32[21,8,128]{2,1,0:T(8,128)S(1)}, u32[]{:S(2)}, u32[]{:S(2)}) collective-permute-start(f32[21,8,128]{2,1,0:T(8,128)S(1)} %get-tuple-element.25), channel_id=1, source_target_pairs={{0,8},{8,16},{16,24},{24,0},{1,9},{9,17},{17,25},{25,1},{2,10},{10... | collective-permute-start | bytes 258056 | tf_op jit(solution)/shard_map/ppermute | solution.py:321
  13.6 5.7 %collective-permute-start.5 = (f32[21,8,128]{2,1,0:T(8,128)S(1)}, f32[21,8,128]{2,1,0:T(8,128)S(1)}, u32[]{:S(2)}, u32[]{:S(2)}) collective-permute-start(f32[21,8,128]{2,1,0:T(8,128)S(1)} %get-tuple-element.23), channel_id=1, source_target_pairs={{8,0},{16,8},{24,16},{0,24},{9,1},{17,9},{25,17},{1,25},{10,2},{18... | collective-permute-start | bytes 258056 | tf_op jit(solution)/shard_map/ppermute | solution.py:322

commit v3 on v2

v3 whole, which is shorter than its diff:
```python
import jax
import jax.numpy as jnp
from jax import lax
from jax.experimental import pallas as pl
from jax.experimental.pallas import tpu as pltpu
from jax.sharding import PartitionSpec as P

COMP = 4
LANES = 128
CHUNKS = 4
ROWS = CHUNKS * COMP
HALF = ROWS // 2
TOP = 8
DEPTH = 32
PAIRS = [(i, j) for i in range(COMP) for j in range(i + 1, COMP)]
TABLE = COMP + COMP * COMP + 3 * len(PAIRS)

VMEM = pl.BlockSpec(memory_space=pltpu.VMEM)
SMEM = pl.BlockSpec(memory_space=pltpu.SMEM)


def lane_parts(shape):
    lane = lax.broadcasted_iota(jnp.int32, shape, 1)
    return lane // 64, (lane // 8) % 8, lane % 8


def turn(v, shift):
    return pltpu.roll(v, shift % LANES, 1)


def route_kernel(peers, cap, slots, target, other_target, held, label, count):
    for core, goals in enumerate((target[...], other_target[...])):
        for peer in range(peers):
            count[core * peers + peer] = 0
            for k in range(cap):
                held[(core * peers + peer) * cap + k] = 0
                label[(core * peers + peer) * cap + k] = slots
        for i in range(slots):
            goal = goals[0, i]
            peer = core * peers + lax.div(goal, slots)
            k = count[peer]
            count[peer] = k + 1
            held[peer * cap + k] = i
            label[peer * cap + k] = lax.rem(goal, slots)


def pack_kernel(peers, cap, flip, held, label, fields, other_fields, out, *weights):
    _, y, _ = lane_parts((COMP, LANES))
    row = lax.broadcasted_iota(jnp.int32, (8, LANES), 1)
    peer = lax.axis_index("loc") ^ flip
    places = [lax.rem(peer + d, peers) * cap for d in (0, 1, peers - 1)]
    names = jnp.zeros((8, LANES), jnp.int32)
    for core, source in enumerate((fields, other_fields)):
        for k in range(cap):
            own, high, low = [held[core * peers * cap + at + k] for at in places]
            entry = core * cap + k
            for n, at in enumerate(places):
                names = jnp.where(row == 2 * cap * n + entry, label[core * peers * cap + at + k], names)
            for chunk in range(CHUNKS):
                part = slice(chunk * LANES, (chunk + 1) * LANES)
                at = entry * ROWS + chunk * COMP
                out[at : at + COMP, :] = source[own, :, part]
                at += 2 * cap * ROWS
                out[at : at + COMP, :] = jnp.where(y < 4, source[high, :, part], source[low, :, part])
    out[4 * cap * ROWS :, :] = names.astype(jnp.float32)
    if weights:
        fill_weights(weights[0])


def fill_weights(out):
    shape = (LANES, LANES)
    z, y, x = lane_parts(shape)
    source = lax.broadcasted_iota(jnp.int32, shape, 0)
    dz, dy, dx = source // 64 - z, (source // 8) % 8 - y, source % 8 - x

    def stencil(d):
        return jnp.where(jnp.abs(d) == 1, 16.0, jnp.where(jnp.abs(d) == 2, -1.0, 0.0))

    def only(mask, value):
        return jnp.where(mask, value, 0.0)

    swap = only((dz != 0) & (dy == 0) & (dx == 0), 16.0)
    along_y, along_x = (dz == 0) & (dx == 0), (dz == 0) & (dy == 0)
    parts = (
        swap + only(along_y, stencil(dy)) + only(along_x, stencil(dx)),
        only(along_y, stencil(dy + 8) + stencil(dy - 8)),
        only(along_x, stencil(dx + 8) + stencil(dx - 8)),
        swap,
    )
    for n, part in enumerate(parts):
        out[n * LANES : (n + 1) * LANES, :] = part.astype(out.dtype)


def entries(cap, got):
    for message in got:
        names = message[4 * cap * ROWS : 4 * cap * ROWS + 1, :].astype(jnp.int32)
        for k in range(2 * cap):
            yield message, k * ROWS, (2 * cap + k) * ROWS, names[0, k], names[0, 2 * cap + k], names[0, 4 * cap + k]


def faces_kernel(cap, slots, *refs):
    got, (up, down, high, low) = refs[:-4], refs[-4:]
    _, y, _ = lane_parts((2 * COMP, LANES))
    for message, whole, joined, slot, high_slot, low_slot in entries(cap, got):
        down[slot] = message[whole : whole + HALF, :]
        up[slot] = message[whole + HALF : whole + ROWS, :]
        for part, at in ((0, 0), (COMP, ROWS - COMP)):
            rows = message[joined + at : joined + at + COMP, :]
            high[high_slot, part : part + COMP, :] = rows
            low[low_slot, part : part + COMP, :] = rows
    pairs = slots // 2
    for q in range(pairs):
        one, two = [jnp.where(y < 4, high[t], low[t]) for t in (q, q + pairs)]
        two = jnp.where(y < 4, turn(two, 16), turn(two, -16))
        both = jnp.where((y >= 2) & (y < 6), two, one)
        at = (q % 2) * COMP
        down[slots + q // 2, at : at + COMP, :] = both[:COMP]
        up[slots + q // 2, at : at + COMP, :] = both[COMP:]


def stage_kernel(fields, target, gradient, relaxation, interaction, out, goals, table):
    out[...] = fields[...]
    goals[...] = target[...]
    for i in range(COMP):
        rate = relaxation[i]
        table[i] = rate
        for j in range(COMP):
            table[COMP + i * COMP + j] = rate * gradient[i, j] * (1.0 / 12.0)
    at = COMP + COMP * COMP
    for i, j in PAIRS:
        for order in range(3):
            table[at] = interaction[order, i, j]
            at += 1


def coefficients(table):
    rates = [table[i] for i in range(COMP)]
    mixing = [[table[COMP + i * COMP + j] for j in range(COMP)] for i in range(COMP)]
    at = COMP + COMP * COMP
    pairs = {pair: [table[at + 3 * n + order] for order in range(3)] for n, pair in enumerate(PAIRS)}
    return rates, mixing, pairs


def mixed(start, laps, mixing):
    result = []
    for i in range(COMP):
        total = start[i]
        for j in range(COMP):
            total += mixing[i][j] * laps[j]
        result.append(total)
    return result


def pieces(values):
    rest = jnp.concatenate(values, axis=0)
    result = []
    for n in range(3):
        piece = rest.astype(jnp.bfloat16)
        result.append(piece)
        rest = rest - piece.astype(jnp.float32)
    return result


def steps(chunks, weights, scalars):
    rates, mixing, pairs = scalars
    layer, _, x = lane_parts(chunks[0][0][0].shape)
    slots = chunks[0][0][0].shape[0]
    rows = []
    for v, ahead, behind, above, below, beside in chunks:
        ends = [jnp.where(x < 4, a, b) for a, b in zip(ahead, behind)]
        layers = [jnp.where(layer == 0, a, b) for a, b in zip(above, below)]
        rows += [jnp.concatenate(p, axis=1) for p in zip(*[pieces(part) for part in (v, beside, ends, layers)])]
    sums = jnp.dot(jnp.concatenate(rows, axis=0), weights[...], preferred_element_type=jnp.float32)
    count = COMP * slots
    results = []
    for n, (v, _, _, above, below, _) in enumerate(chunks):
        near = sum(sums[(3 * n + m) * count : (3 * n + m + 1) * count] for m in range(3))
        laps = [near[c * slots : (c + 1) * slots] - (above[c] + below[c]) - 90.0 * v[c] for c in range(COMP)]
        drive = [None] * COMP
        for (i, j), (a, b, c) in pairs.items():
            gap = v[i] - v[j]
            bend = c * gap
            slope = b + bend
            energy = a + slope * gap
            cross = v[i] * v[j] * (slope + bend)
            first = v[j] * energy + cross
            second = v[i] * energy - cross
            drive[i] = first if drive[i] is None else drive[i] + first
            drive[j] = second if drive[j] is None else drive[j] + second
        results.append(mixed([v[i] - rates[i] * drive[i] for i in range(COMP)], laps, mixing))
    return results


def store(slots, ref, at, values):
    for c, value in enumerate(values):
        ref[at, c, TOP : TOP + slots, :] = value
        ref[at, c, TOP - 1 : TOP, :] = value[slots - 1 :]
        ref[at, c, TOP + slots : TOP + slots + 1, :] = value[:1]


def load(slots, ref, at, offset=0):
    return [ref[at, c, TOP + offset : TOP + offset + slots, :] for c in range(COMP)]


def move(slots, work, places, weights, scalars):
    chunks = []
    for at, above, below, beside, _ in places:
        around = [load(slots, work, n) for n in (above, below, beside)]
        chunks.append((load(slots, work, at), load(slots, work, at, 1), load(slots, work, at, -1), *around))
    for place, values in zip(places, steps(chunks, weights, scalars)):
        store(slots, work, place[-1], values)


def column(ref, start, count, stride):
    flat = ref.reshape(ref.shape[0] * ref.shape[1], LANES)
    return flat[pl.ds(start, count, stride=stride), :]


SPAN = CHUNKS + 2
BLOCK, SIDE, BLOCK_NEXT, SIDE_NEXT, FINAL, BEYOND = [n * SPAN for n in range(5)] + [4 * SPAN + 2]
ENTRIES = BEYOND + 2


def inner_kernel(cap, slots, peers, *refs):
    got, (table, weights, work, block, high, low) = refs[: peers // 2], refs[peers // 2 :]
    scalars = coefficients(table)
    _, y, _ = lane_parts((slots, LANES))
    for message, whole, joined, slot, high_slot, low_slot in entries(cap, got):
        block[slot] = message[whole : whole + ROWS, :]
        rows = message[joined : joined + ROWS, :]
        high[high_slot] = rows
        low[low_slot] = rows
    for base in range(0, FINAL, SPAN):
        for at in (base, base + SPAN - 1):
            work[at] = jnp.zeros(work.shape[1:], work.dtype)

    @pl.loop(0, CHUNKS)
    def _(k):
        rows = [k * COMP + c for c in range(COMP)]
        store(slots, work, BLOCK + 1 + k, [column(block, r, slots, ROWS) for r in rows])
        sides = [jnp.where(y < 4, column(high, r, slots, ROWS), column(low, r, slots, ROWS)) for r in rows]
        store(slots, work, SIDE + 1 + k, sides)

    @pl.loop(0, 2)
    def _(side):
        places = []
        for k in range(1, CHUNKS + 1):
            at = side * SPAN + k
            places.append((at, at + 1, at - 1, (1 - side) * SPAN + k, BLOCK_NEXT + at))
        move(slots, work, places, weights, scalars)

    second, third = BLOCK_NEXT + 2, BLOCK_NEXT + 3
    places = [
        (second, third, BLOCK_NEXT, SIDE_NEXT + 2, FINAL),
        (third, BLOCK_NEXT + SPAN - 1, second, SIDE_NEXT + 3, FINAL + 1),
    ]
    move(slots, work, places, weights, scalars)


def outer_kernel(slots, below, above, table, weights, _, out, work, middle, ends, sems):
    scalars = coefficients(table)
    mixing = scalars[1]
    pairs = slots // 2
    last = SPAN - 1
    _, y, _ = lane_parts((pairs, LANES))
    layer, _, _ = lane_parts((slots, LANES))

    def add(start, beyond, end):
        laps = [16.0 * turn(jnp.where(layer == 1 - end, b, 0.0), 64) - b for b in beyond]
        return mixed(start, laps, mixing)

    for end, ref in enumerate((below, above)):
        near, distant, side = [], [], []
        for c in range(COMP):
            near.append(column(ref, (1 - end) * COMP + c, slots, HALF))
            distant.append(column(ref, end * COMP + c, slots, HALF))
            both = column(ref, slots * HALF + c, pairs, COMP)
            side.append(jnp.concatenate([both, jnp.where(y < 4, turn(both, -16), turn(both, 16))], axis=0))
        edge = 1 + end * (CHUNKS - 1)
        store(slots, work, BLOCK + end * last, near)
        store(slots, work, BEYOND + end, distant)
        store(slots, work, SIDE + end * last, side)
        first = add(load(slots, work, BLOCK_NEXT + edge), near, end)
        store(slots, work, SIDE_NEXT + edge, add(load(slots, work, SIDE_NEXT + edge), side, end))
        store(slots, work, BLOCK_NEXT + edge, first)
        for c, value in enumerate(add(load(slots, work, FINAL + end), first, end)):
            middle[:, c, end * LANES : (end + 1) * LANES] = value

    copies = [pltpu.make_async_copy(middle, out.at[:, :, LANES : 3 * LANES], sems.at[2])]
    copies[0].start()

    @pl.loop(0, 2)
    def _(late):
        places = []
        for end in range(2):
            outside = end * last
            at = jnp.where(late == 1, BLOCK_NEXT + 1 + end * (CHUNKS - 1), BLOCK + outside)
            beyond = jnp.where(late == 1, BLOCK_NEXT + outside, BEYOND + end)
            beside = jnp.where(late == 1, SIDE_NEXT + 1 + end * (CHUNKS - 1), SIDE + outside)
            to = jnp.where(late == 1, BLOCK, BLOCK_NEXT) + outside
            up, down = (beyond, at - 1) if end else (at + 1, beyond)
            places.append((at, up, down, beside, to))
        move(slots, work, places, weights, scalars)

    for end in range(2):
        for c, value in enumerate(load(slots, work, BLOCK + end * last)):
            ends[end, :, c, :] = value
        at = end * (CHUNKS - 1) * LANES
        copies.append(pltpu.make_async_copy(ends.at[end], out.at[:, :, at : at + LANES], sems.at[end]))
        copies[-1].start()
    for copy in copies:
        copy.wait()


def per_device(fields, target, gradient_matrix, relaxation, interaction):
    slots = fields.shape[0]
    peers = lax.axis_size("loc")
    groups = lax.axis_size("grp")
    cap = (slots + peers - 1) // peers
    chips = peers // 2
    f32 = jnp.float32
    params = pltpu.CompilerParams(vmem_limit_bytes=8 << 20)

    def shape(*dims):
        return pltpu.VMEM(dims, f32)

    def inside(*arrays):
        return [pltpu.with_memory_space_constraint(a, pltpu.VMEM) for a in arrays]

    def cross(array, flip):
        return lax.ppermute(array, "loc", [(i, i ^ flip) for i in range(peers)])

    target = target.reshape(1, slots)
    staged, goals, table = pl.pallas_call(
        stage_kernel,
        out_shape=(shape(*fields.shape), pltpu.VMEM(target.shape, jnp.int32), pltpu.SMEM((TABLE,), f32)),
        in_specs=[VMEM] * 2 + [SMEM] * 3,
        out_specs=(VMEM, VMEM, SMEM),
        name="stage",
    )(fields, target, gradient_matrix, relaxation, interaction)
    table = pltpu.with_memory_space_constraint(table, pltpu.SMEM)
    other_fields, other_target = cross(fields, 1), cross(target, 1)
    entry_count = 2 * peers * cap
    routes = pl.pallas_call(
        lambda *refs: route_kernel(peers, cap, slots, *refs),
        out_shape=(pltpu.SMEM((entry_count,), jnp.int32),) * 2,
        in_specs=[VMEM] * 2,
        out_specs=(SMEM,) * 2,
        scratch_shapes=[pltpu.SMEM((2 * peers,), jnp.int32)],
        name="route",
        compiler_params=params,
    )(*inside(goals, other_target))
    routes = [pltpu.with_memory_space_constraint(a, pltpu.SMEM) for a in routes]

    def pack(flip):
        message = shape(4 * cap * ROWS + 8, LANES)
        extra = () if flip else (pltpu.VMEM((4 * LANES, LANES), jnp.bfloat16),)
        return pl.pallas_call(
            lambda *refs: pack_kernel(peers, cap, flip, *refs),
            out_shape=(message, *extra),
            in_specs=[SMEM] * 2 + [VMEM] * 2,
            out_specs=(VMEM,) * (1 + len(extra)),
            name="pack",
            compiler_params=params,
        )(*routes, *inside(staged, other_fields))

    flips = [2 * j for j in reversed(range(chips))]
    *sent, (own, weights) = [pack(flip) for flip in flips]
    weights = inside(weights)[0]
    got = inside(*[cross(message, flip) for (message,), flip in zip(sent, flips)], own)
    up, down = pl.pallas_call(
        lambda *refs: faces_kernel(cap, slots, *refs),
        out_shape=(shape(slots + slots // 4, HALF, LANES),) * 2,
        in_specs=[VMEM] * chips,
        out_specs=(VMEM,) * 2,
        scratch_shapes=[pltpu.VMEM((slots + 1, HALF, LANES), f32)] * 2,
        name="faces",
        compiler_params=params,
    )(*got)
    forward = [(i, (i + 1) % groups) for i in range(groups)]
    backward = [(j, i) for i, j in forward]
    below = lax.ppermute(up, "grp", forward)
    above = lax.ppermute(down, "grp", backward)
    work = pl.pallas_call(
        lambda *refs: inner_kernel(cap, slots, peers, *refs),
        out_shape=shape(ENTRIES, COMP, DEPTH, LANES),
        in_specs=[VMEM] * chips + [SMEM, VMEM],
        out_specs=VMEM,
        scratch_shapes=[pltpu.VMEM((slots + 1, ROWS, LANES), f32)] * 3,
        name="inner",
        compiler_params=params,
    )(*got, table, weights)
    return pl.pallas_call(
        lambda *refs: outer_kernel(slots, *refs),
        out_shape=(jax.ShapeDtypeStruct(fields.shape, f32), shape(*work.shape)),
        in_specs=[VMEM] * 2 + [SMEM] + [VMEM] * 2,
        out_specs=(pl.BlockSpec(memory_space=pl.ANY), VMEM),
        input_output_aliases={4: 1},
        scratch_shapes=[
            pltpu.VMEM((slots, COMP, 2 * LANES), f32),
            pltpu.VMEM((2, slots, COMP, LANES), f32),
            pltpu.SemaphoreType.DMA((3,)),
        ],
        name="outer",
        compiler_params=params,
    )(*inside(below, above), table, weights, *inside(work))[0]


def solution(mesh):
    placed = (P(("grp", "loc"), None, None), P(("grp", "loc")), P(), P(), P())
    return jax.shard_map(
        per_device,
        mesh=mesh,
        in_specs=placed,
        out_specs=P(("grp", "loc"), None, None),
        check_vma=False,
    )
```

time: 21 us -> 19.7 us (0.938)
  Pallas kernels: 6.56 us -> 4.66 us
  waiting for transfers between devices: 5.41 us -> 5.95 us
    ppermute x1, waiting for transfers between devices: 0.01 us -> 1.32 us  [per_device(): below = lax.ppermute(up, 'grp', forward)]
    pallas_call x1, Pallas kernels: 2.61 us -> 1.38 us  [per_device(): pl.pallas_call(lambda *refs: inner_kernel(cap, slots, peers, *refs), out_...]
    ppermute x5, waiting for transfers between devices: 5.4 us -> 4.27 us  [cross(): return lax.ppermute(array, 'loc', [(i, i ^ flip) for i in range(peers)])]
    pallas_call x3 -> x6, Pallas kernels: 2.73 us -> 2.06 us  [the longest x1 1.48 us: per_device(): pl.pallas_call(lambda *refs: outer_kernel(slots, *refs), out_shape=(jax.S...]
    ppermute x1, waiting for transfers between devices: 0.01 us -> 0.36 us  [per_device(): above = lax.ppermute(down, 'grp', backward)]
  transfers between devices with their start and end apart: 7 -> 7, of which waited for: 4 -> 6; matrix products, arithmetic and copies ran while one was open for 0% -> 0% of each run, Pallas kernels for 21% -> 15%
where the time goes in v3:
time: 19.7 us; the launch traced here: 19.6 us
  starting transfers between devices  8.91 us (45%)
  waiting for transfers between devices  5.95 us (30%)
  Pallas kernels  4.66 us (24%)
    ppermute x5, starting transfers between devices, cross(): return lax.ppermute(array, 'loc', [(i, i ^ flip) for i in range(peers)])  5.04 us
    ppermute x5, waiting for transfers between devices, cross(): return lax.ppermute(array, 'loc', [(i, i ^ flip) for i in range(peers)])  4.27 us
    ppermute x1, starting transfers between devices, per_device(): above = lax.ppermute(down, 'grp', backward)  2.25 us
    ppermute x1, starting transfers between devices, per_device(): below = lax.ppermute(up, 'grp', forward)  1.63 us
    pallas_call x1, Pallas kernels, per_device(): pl.pallas_call(lambda *refs: outer_kernel(slots, *refs), out_shape=(jax.S...  1.48 us
    pallas_call x1, Pallas kernels, per_device(): pl.pallas_call(lambda *refs: inner_kernel(cap, slots, peers, *refs), out_...  1.38 us
    ppermute x1, waiting for transfers between devices, per_device(): below = lax.ppermute(up, 'grp', forward)  1.32 us
    pallas_call x1, Pallas kernels, per_device(): pl.pallas_call(stage_kernel, out_shape=(shape(*fields.shape), pltpu.VMEM(...  0.97 us
  transfers between devices with their start and end apart: 7, of which 6 were waited for; matrix products, arithmetic and copies ran while one was open for 0% of the time, Pallas kernels for 15%

profile of v3, /device:TPU:0, one launch (start us, length us, event | category | flops | bytes accessed | tf_op | source)
XLA Modules:
  0.0 19.6 jit_solution(2671880309650361180)
XLA Ops:
  0.0 0.5 %collective-permute-start.1 = (f32[16,4,512]{2,1,0:T(4,128)}, f32[16,4,512]{2,1,0:T(4,128)S(1)}, u32[]{:S(2)}, u32[]{:S(2)}) collective-permute-start(f32[16,4,512]{2,1,0:T(4,128)} %fields.1), channel_id=1, source_target_pairs={{0,1},{1,0},{2,3},{3,2},{4,5},{5,4},{6,7},{7,6},{8,9},{9,8},{10,11... | collective-permute-start | bytes 393224 | tf_op jit(solution)/shard_map/ppermute | solution.py:331
  0.5 0.1 collective-permute-start
  0.5 1.0 %stage.1 = (f32[16,4,512]{2,1,0:T(4,128)S(1)}, s32[1,16]{1,0:T(1,128)S(1)}, f32[38]{0:T(128)S(4)}) custom-call(f32[16,4,512]{2,1,0:T(4,128)} %fields.1, s32[1,16]{1,0:T(1,128)} %bitcast.2, f32[4,4]{1,0:T(4,128)} %gradient.1, f32[4]{0:T(128)} %relaxation.1, f32[3,4,4]{2,1,0:T(4,128)} %interaction.1), custom_call_target="tpu_custom_call" | custom-call | tf_op jit(solution)/shard_map/stage/pallas_call | solution.py:334
  1.5 0.2 %collective-permute-done.refs_1_ = s32[1,16]{1,0:T(1,128)S(1)} collective-permute-done((s32[1,16]{1,0:T(1,128)}, s32[1,16]{1,0:T(1,128)S(1)}, u32[]{:S(2)}, u32[]{:S(2)}) %collective-permute-start) | collective-permute-done | bytes 96 | tf_op jit(solution)/shard_map/ppermute | solution.py:331
  1.7 0.3 %route.1 = (s32[32]{0:T(128)S(4)}, s32[32]{0:T(128)S(4)}) custom-call(s32[1,16]{1,0:T(1,128)S(1)} %get-tuple-element.15.refs_0_, s32[1,16]{1,0:T(1,128)S(1)} %collective-permute-done.refs_1_), custom_call_target="tpu_custom_call" | custom-call | tf_op jit(solution)/shard_map/route/pallas_call | solution.py:344
  2.0 0.0 collective-permute-done.1.refs_3_
  2.1 3.8 %collective-permute-start.2 = (f32[136,128]{1,0:T(8,128)S(1)}, f32[136,128]{1,0:T(8,128)S(1)}, u32[]{:S(2)}, u32[]{:S(2)}) collective-permute-start(f32[136,128]{1,0:T(8,128)S(1)} %pack.4), channel_id=1, source_target_pairs={{0,6},{1,7},{2,4},{3,5},{4,2},{5,3},{6,0},{7,1},{8,14},{9,15},{10,... | collective-permute-start | bytes 208904 | tf_op jit(solution)/shard_map/ppermute | solution.py:331
  5.9 0.6 %collective-permute-start.3 = (f32[136,128]{1,0:T(8,128)S(1)}, f32[136,128]{1,0:T(8,128)S(1)}, u32[]{:S(2)}, u32[]{:S(2)}) collective-permute-start(f32[136,128]{1,0:T(8,128)S(1)} %pack.5), channel_id=1, source_target_pairs={{0,4},{1,5},{2,6},{3,7},{4,0},{5,1},{6,2},{7,3},{8,12},{9,13},{10,... | collective-permute-start | bytes 208904 | tf_op jit(solution)/shard_map/ppermute | solution.py:331
  6.5 0.1 collective-permute-start.4
  6.7 0.2 pack.7
  6.9 1.6 %collective-permute-done.2.refs_0_ = f32[136,128]{1,0:T(8,128)S(1)} collective-permute-done((f32[136,128]{1,0:T(8,128)S(1)}, f32[136,128]{1,0:T(8,128)S(1)}, u32[]{:S(2)}, u32[]{:S(2)}) %collective-permute-start.2) | collective-permute-done | bytes 69664 | tf_op jit(solution)/shard_map/ppermute | solution.py:331
  8.4 1.9 %collective-permute-done.3.refs_1_ = f32[136,128]{1,0:T(8,128)S(1)} collective-permute-done((f32[136,128]{1,0:T(8,128)S(1)}, f32[136,128]{1,0:T(8,128)S(1)}, u32[]{:S(2)}, u32[]{:S(2)}) %collective-permute-start.3) | collective-permute-done | bytes 69664 | tf_op jit(solution)/shard_map/ppermute | solution.py:331
  10.3 0.6 %collective-permute-done.4.refs_2_ = f32[136,128]{1,0:T(8,128)S(1)} collective-permute-done((f32[136,128]{1,0:T(8,128)S(1)}, f32[136,128]{1,0:T(8,128)S(1)}, u32[]{:S(2)}, u32[]{:S(2)}) %collective-permute-start.4) | collective-permute-done | bytes 69664 | tf_op jit(solution)/shard_map/ppermute | solution.py:331
  10.9 0.2 %faces.1 = (f32[20,8,128]{2,1,0:T(8,128)S(1)}, f32[20,8,128]{2,1,0:T(8,128)S(1)}) custom-call(f32[136,128]{1,0:T(8,128)S(1)} %collective-permute-done.2.refs_0_, f32[136,128]{1,0:T(8,128)S(1)} %collective-permute-done.3.refs_1_, f32[136,128]{1,0:T(8,128)S(1)} %collective-permute-done.4.refs_2_, f32[136,128]{1,0:T(8,128)S(1)} %get-tuple-element.19.refs_3_), custom_call_target="tpu_custom_call" | custom-call | tf_op jit(solution)/shard_map/faces/pallas_call | solution.py:371
  11.2 1.6 %collective-permute-start.5 = (f32[20,8,128]{2,1,0:T(8,128)S(1)}, f32[20,8,128]{2,1,0:T(8,128)S(1)}, u32[]{:S(2)}, u32[]{:S(2)}) collective-permute-start(f32[20,8,128]{2,1,0:T(8,128)S(1)} %get-tuple-element.20), channel_id=1, source_target_pairs={{0,8},{8,16},{16,24},{24,0},{1,9},{9,17},{17,25},{25,1},{2,10},{10... | collective-permute-start | bytes 245768 | tf_op jit(solution)/shard_map/ppermute | solution.py:382
  12.8 2.2 %collective-permute-start.6 = (f32[20,8,128]{2,1,0:T(8,128)S(1)}, f32[20,8,128]{2,1,0:T(8,128)S(1)}, u32[]{:S(2)}, u32[]{:S(2)}) collective-permute-start(f32[20,8,128]{2,1,0:T(8,128)S(1)} %get-tuple-element.21), channel_id=1, source_target_pairs={{8,0},{16,8},{24,16},{0,24},{9,1},{17,9},{25,17},{1,25},{10,2},{18... | collective-permute-start | bytes 245768 | tf_op jit(solution)/shard_map/ppermute | solution.py:383
  15.0 1.4 %inner.1.refs_4_ = f32[28,4,32,128]{3,2,1,0:T(8,128)S(1)} custom-call(f32[136,128]{1,0:T(8,128)S(1)} %collective-permute-done.2.refs_0_, f32[136,128]{1,0:T(8,128)S(1)} %collective-permute-done.3.refs_1_, f32[136,128]{1,0:T(8,128)S(1)} %collective-permute-done.4.refs_2_, f32[136,128]{1,0:T(8,128)S(1)} %get-tuple-element.19.refs_3_, ...), custom_call_target="tpu_custom_call" | custom-call | tf_op jit(solution)/shard_map/inner/pallas_call | solution.py:384
  16.4 1.3 %collective-permute-done.5.refs_0_ = f32[20,8,128]{2,1,0:T(8,128)S(1)} collective-permute-done((f32[20,8,128]{2,1,0:T(8,128)S(1)}, f32[20,8,128]{2,1,0:T(8,128)S(1)}, u32[]{:S(2)}, u32[]{:S(2)}) %collective-permute-start.5) | collective-permute-done | bytes 81952 | tf_op jit(solution)/shard_map/ppermute | solution.py:382
  17.7 0.4 %collective-permute-done.6.refs_1_ = f32[20,8,128]{2,1,0:T(8,128)S(1)} collective-permute-done((f32[20,8,128]{2,1,0:T(8,128)S(1)}, f32[20,8,128]{2,1,0:T(8,128)S(1)}, u32[]{:S(2)}, u32[]{:S(2)}) %collective-permute-start.6) | collective-permute-done | bytes 81952 | tf_op jit(solution)/shard_map/ppermute | solution.py:383
  18.1 1.5 %outer.1 = (f32[16,4,512]{2,1,0:T(4,128)}, f32[28,4,32,128]{3,2,1,0:T(8,128)S(1)}) custom-call(f32[20,8,128]{2,1,0:T(8,128)S(1)} %collective-permute-done.5.refs_0_, f32[20,8,128]{2,1,0:T(8,128)S(1)} %collective-permute-done.6.refs_1_, f32[38]{0:T(128)S(4)} %get-tuple-element.22.refs_4_.refs_2_, ...), custom_call_target="tpu_custom_call", output_to_operand_aliasing={{1}: (4, {})} | custom-call | tf_op jit(solution)/shard_map/outer/pallas_call | solution.py:393
  (3 shorter events, 0.1 us)
Async XLA Ops:
  0.0 2.0 %collective-permute-start.1 = (f32[16,4,512]{2,1,0:T(4,128)}, f32[16,4,512]{2,1,0:T(4,128)S(1)}, u32[]{:S(2)}, u32[]{:S(2)}) collective-permute-start(f32[16,4,512]{2,1,0:T(4,128)} %fields.1), channel_id=1, source_target_pairs={{0,1},{1,0},{2,3},{3,2},{4,5},{5,4},{6,7},{7,6},{8,9},{9,8},{10,11... | collective-permute-start | bytes 393224 | tf_op jit(solution)/shard_map/ppermute | solution.py:331
  0.5 1.3 %collective-permute-start = (s32[1,16]{1,0:T(1,128)}, s32[1,16]{1,0:T(1,128)S(1)}, u32[]{:S(2)}, u32[]{:S(2)}) collective-permute-start(s32[1,16]{1,0:T(1,128)} %bitcast.1), channel_id=1, source_target_pairs={{0,1},{1,0},{2,3},{3,2},{4,5},{5,4},{6,7},{7,6},{8,9},{9,8},{10,11... | collective-permute-start | bytes 200 | tf_op jit(solution)/shard_map/ppermute | solution.py:331
  2.1 6.4 %collective-permute-start.2 = (f32[136,128]{1,0:T(8,128)S(1)}, f32[136,128]{1,0:T(8,128)S(1)}, u32[]{:S(2)}, u32[]{:S(2)}) collective-permute-start(f32[136,128]{1,0:T(8,128)S(1)} %pack.4), channel_id=1, source_target_pairs={{0,6},{1,7},{2,4},{3,5},{4,2},{5,3},{6,0},{7,1},{8,14},{9,15},{10,... | collective-permute-start | bytes 208904 | tf_op jit(solution)/shard_map/ppermute | solution.py:331
  5.9 4.4 %collective-permute-start.3 = (f32[136,128]{1,0:T(8,128)S(1)}, f32[136,128]{1,0:T(8,128)S(1)}, u32[]{:S(2)}, u32[]{:S(2)}) collective-permute-start(f32[136,128]{1,0:T(8,128)S(1)} %pack.5), channel_id=1, source_target_pairs={{0,4},{1,5},{2,6},{3,7},{4,0},{5,1},{6,2},{7,3},{8,12},{9,13},{10,... | collective-permute-start | bytes 208904 | tf_op jit(solution)/shard_map/ppermute | solution.py:331
  6.5 4.4 %collective-permute-start.4 = (f32[136,128]{1,0:T(8,128)S(1)}, f32[136,128]{1,0:T(8,128)S(1)}, u32[]{:S(2)}, u32[]{:S(2)}) collective-permute-start(f32[136,128]{1,0:T(8,128)S(1)} %pack.6), channel_id=1, source_target_pairs={{0,2},{1,3},{2,0},{3,1},{4,6},{5,7},{6,4},{7,5},{8,10},{9,11},{10,... | collective-permute-start | bytes 208904 | tf_op jit(solution)/shard_map/ppermute | solution.py:331
  11.2 6.6 %collective-permute-start.5 = (f32[20,8,128]{2,1,0:T(8,128)S(1)}, f32[20,8,128]{2,1,0:T(8,128)S(1)}, u32[]{:S(2)}, u32[]{:S(2)}) collective-permute-start(f32[20,8,128]{2,1,0:T(8,128)S(1)} %get-tuple-element.20), channel_id=1, source_target_pairs={{0,8},{8,16},{16,24},{24,0},{1,9},{9,17},{17,25},{25,1},{2,10},{10... | collective-permute-start | bytes 245768 | tf_op jit(solution)/shard_map/ppermute | solution.py:382
  12.8 5.3 %collective-permute-start.6 = (f32[20,8,128]{2,1,0:T(8,128)S(1)}, f32[20,8,128]{2,1,0:T(8,128)S(1)}, u32[]{:S(2)}, u32[]{:S(2)}) collective-permute-start(f32[20,8,128]{2,1,0:T(8,128)S(1)} %get-tuple-element.21), channel_id=1, source_target_pairs={{8,0},{16,8},{24,16},{0,24},{9,1},{17,9},{25,17},{1,25},{10,2},{18... | collective-permute-start | bytes 245768 | tf_op jit(solution)/shard_map/ppermute | solution.py:383

commit v4 on v3

--- a/solution.py
+++ b/solution.py
@@ -98,24 +98,84 @@
             yield message, k * ROWS, (2 * cap + k) * ROWS, names[0, k], names[0, 2 * cap + k], names[0, 4 * cap + k]
 
 
-def faces_kernel(cap, slots, *refs):
-    got, (up, down, high, low) = refs[:-4], refs[-4:]
-    _, y, _ = lane_parts((2 * COMP, LANES))
+def squeeze(one, two, y):
+    return jnp.where((y >= 2) & (y < 6), jnp.where(y < 4, turn(two, 16), turn(two, -16)), one)
+
+
+def second_of(both, y):
+    return jnp.where(y < 4, turn(both, -16), turn(both, 16))
+
+
+def bundle_rows(cap, count):
+    corners = 2 * cap * count * HALF
+    names = corners + cap * count * COMP
+    return corners, names, names + 8 * ((count + 7) // 8)
+
+
+def bundle(cap, got, out):
+    corners, names, end = bundle_rows(cap, len(got))
+    _, y, _ = lane_parts((COMP, LANES))
+    out[names:, :] = jnp.zeros((end - names, LANES), out.dtype)
+    for n, message in enumerate(got):
+        for k in range(2 * cap):
+            at = (2 * cap * n + k) * HALF
+            out[at : at + HALF, :] = message[k * ROWS + HALF : (k + 1) * ROWS, :]
+        for k in range(cap):
+            one, two = [message[(2 * cap + e + 1) * ROWS - COMP : (2 * cap + e + 1) * ROWS, :] for e in (k, cap + k)]
+            at = corners + (cap * n + k) * COMP
+            out[at : at + COMP, :] = squeeze(one, two, y)
+        out[names + n : names + n + 1, :] = message[4 * cap * ROWS : 4 * cap * ROWS + 1, :]
+
+
+def put_down(cap, got, down, high, low):
     for message, whole, joined, slot, high_slot, low_slot in entries(cap, got):
         down[slot] = message[whole : whole + HALF, :]
-        up[slot] = message[whole + HALF : whole + ROWS, :]
-        for part, at in ((0, 0), (COMP, ROWS - COMP)):
-            rows = message[joined + at : joined + at + COMP, :]
-            high[high_slot, part : part + COMP, :] = rows
-            low[low_slot, part : part + COMP, :] = rows
+        rows = message[joined : joined + COMP, :]
+        high[high_slot] = rows
+        low[low_slot] = rows
+
+
+def put_sides(slots, faces, high, low):
+    _, y, _ = lane_parts((COMP, LANES))
     pairs = slots // 2
     for q in range(pairs):
         one, two = [jnp.where(y < 4, high[t], low[t]) for t in (q, q + pairs)]
-        two = jnp.where(y < 4, turn(two, 16), turn(two, -16))
-        both = jnp.where((y >= 2) & (y < 6), two, one)
         at = (q % 2) * COMP
-        down[slots + q // 2, at : at + COMP, :] = both[:COMP]
-        up[slots + q // 2, at : at + COMP, :] = both[COMP:]
+        faces[slots + q // 2, at : at + COMP, :] = squeeze(one, two, y)
+
+
+def early_kernel(cap, *refs):
+    got, (up, down, high, low) = refs[:-4], refs[-4:]
+    bundle(cap, got, up)
+    put_down(cap, got, down, high, low)
+
+
+def late_kernel(cap, slots, count, *refs):
+    got, (up, down, high, low) = refs[:count], refs[-4:]
+    bundle(cap, got, up)
+    put_down(cap, got, down, high, low)
+    put_sides(slots, down, high, low)
+
+
+def catch_kernel(cap, slots, counts, *refs):
+    joined, faces, high, low = refs
+    split = bundle_rows(cap, counts[0])[-1]
+    refs = joined.at[:split], joined.at[split:]
+    _, y, _ = lane_parts((COMP, LANES))
+    for ref, count in zip(refs, counts):
+        corners, names, _ = bundle_rows(cap, count)
+        for n in range(count):
+            slot_of = ref[names + n : names + n + 1, :].astype(jnp.int32)
+            for k in range(2 * cap):
+                at = (2 * cap * n + k) * HALF
+                faces[slot_of[0, k]] = ref[at : at + HALF, :]
+                at = corners + (cap * n + k % cap) * COMP
+                rows = ref[at : at + COMP, :]
+                if k >= cap:
+                    rows = second_of(rows, y)
+                high[slot_of[0, 2 * cap + k]] = rows
+                low[slot_of[0, 4 * cap + k]] = rows
+    put_sides(slots, faces, high, low)
 
 
 def stage_kernel(fields, target, gradient, relaxation, interaction, out, goals, table):
@@ -275,7 +335,7 @@
             near.append(column(ref, (1 - end) * COMP + c, slots, HALF))
             distant.append(column(ref, end * COMP + c, slots, HALF))
             both = column(ref, slots * HALF + c, pairs, COMP)
-            side.append(jnp.concatenate([both, jnp.where(y < 4, turn(both, -16), turn(both, 16))], axis=0))
+            side.append(jnp.concatenate([both, second_of(both, y)], axis=0))
         edge = 1 + end * (CHUNKS - 1)
         store(slots, work, BLOCK + end * last, near)
         store(slots, work, BEYOND + end, distant)
@@ -368,19 +428,39 @@
     *sent, (own, weights) = [pack(flip) for flip in flips]
     weights = inside(weights)[0]
     got = inside(*[cross(message, flip) for (message,), flip in zip(sent, flips)], own)
-    up, down = pl.pallas_call(
-        lambda *refs: faces_kernel(cap, slots, *refs),
-        out_shape=(shape(slots + slots // 4, HALF, LANES),) * 2,
-        in_specs=[VMEM] * chips,
-        out_specs=(VMEM,) * 2,
-        scratch_shapes=[pltpu.VMEM((slots + 1, HALF, LANES), f32)] * 2,
-        name="faces",
-        compiler_params=params,
-    )(*got)
+    early, late = got[: chips // 2 - 1] + got[-1:], got[chips // 2 - 1 : -1]
+    counts = len(early), len(late)
+    face, corner = (slots + slots // 4, HALF, LANES), (slots + 1, COMP, LANES)
+    up_early, *down = pl.pallas_call(
+        lambda *refs: early_kernel(cap, *refs),
+        out_shape=(shape(bundle_rows(cap, counts[0])[-1], LANES), shape(*face), shape(*corner), shape(*corner)),
+        in_specs=[VMEM] * counts[0],
+        out_specs=(VMEM,) * 4,
+        name="early",
+        compiler_params=params,
+    )(*early)
+    up_late, down, *_ = pl.pallas_call(
+        lambda *refs: late_kernel(cap, slots, counts[1], *refs),
+        out_shape=(shape(bundle_rows(cap, counts[1])[-1], LANES), shape(*face), shape(*corner), shape(*corner)),
+        in_specs=[VMEM] * (counts[1] + 3),
+        out_specs=(VMEM,) * 4,
+        input_output_aliases={counts[1] + n: 1 + n for n in range(3)},
+        name="late",
+        compiler_params=params,
+    )(*late, *inside(*down))
     forward = [(i, (i + 1) % groups) for i in range(groups)]
     backward = [(j, i) for i, j in forward]
-    below = lax.ppermute(up, "grp", forward)
+    from_below = [lax.ppermute(up, "grp", forward) for up in (up_early, up_late)]
     above = lax.ppermute(down, "grp", backward)
+    below = pl.pallas_call(
+        lambda *refs: catch_kernel(cap, slots, counts, *refs),
+        out_shape=shape(*face),
+        in_specs=[VMEM],
+        out_specs=VMEM,
+        scratch_shapes=[pltpu.VMEM(corner, f32)] * 2,
+        name="catch",
+        compiler_params=params,
+    )(*inside(jnp.concatenate(from_below)))
     work = pl.pallas_call(
         lambda *refs: inner_kernel(cap, slots, peers, *refs),
         out_shape=shape(ENTRIES, COMP, DEPTH, LANES),

time: 19.7 us -> 19.3 us (0.980)
  waiting for transfers between devices: 5.95 us -> 3.28 us
  starting transfers between devices: 8.91 us -> 10.8 us
  Pallas kernels: 4.66 us -> 5.03 us
    ppermute x5, waiting for transfers between devices: 4.27 us -> 2.29 us  [cross(): return lax.ppermute(array, 'loc', [(i, i ^ flip) for i in range(peers)])]
    ppermute x1 -> x2, starting transfers between devices: 1.63 us -> 3.47 us  [per_device(): lax.ppermute(up, 'grp', forward)]
    ppermute x1 -> x2, waiting for transfers between devices: 1.32 us -> 0.84 us  [per_device(): lax.ppermute(up, 'grp', forward)]
    pallas_call x1 -> x3, Pallas kernels: 0.24 us -> 0.59 us  [the longest x1 0.24 us: per_device(): pl.pallas_call(lambda *refs: catch_kernel(cap, slots, counts, *refs), out...]
    ppermute x1, waiting for transfers between devices: 0.36 us -> 0.15 us  [per_device(): above = lax.ppermute(down, 'grp', backward)]
  transfers between devices with their start and end apart: 7 -> 8, of which waited for: 6 -> 5; matrix products, arithmetic and copies ran while one was open for 0% -> 0% of each run, Pallas kernels for 15% -> 18%
where the time goes in v4:
time: 19.3 us; the launch traced here: 19.2 us
  starting transfers between devices  10.8 us (56%)
  Pallas kernels  5.03 us (26%)
  waiting for transfers between devices  3.28 us (17%)
    ppermute x5, starting transfers between devices, cross(): return lax.ppermute(array, 'loc', [(i, i ^ flip) for i in range(peers)])  5.04 us
    ppermute x2, starting transfers between devices, per_device(): lax.ppermute(up, 'grp', forward)  3.47 us
    ppermute x5, waiting for transfers between devices, cross(): return lax.ppermute(array, 'loc', [(i, i ^ flip) for i in range(peers)])  2.29 us
    ppermute x1, starting transfers between devices, per_device(): above = lax.ppermute(down, 'grp', backward)  2.25 us
    pallas_call x1, Pallas kernels, per_device(): pl.pallas_call(lambda *refs: outer_kernel(slots, *refs), out_shape=(jax.S...  1.48 us
    pallas_call x1, Pallas kernels, per_device(): pl.pallas_call(lambda *refs: inner_kernel(cap, slots, peers, *refs), out_...  1.41 us
    pallas_call x1, Pallas kernels, per_device(): pl.pallas_call(stage_kernel, out_shape=(shape(*fields.shape), pltpu.VMEM(...  0.97 us
    ppermute x2, waiting for transfers between devices, per_device(): lax.ppermute(up, 'grp', forward)  0.84 us
  transfers between devices with their start and end apart: 8, of which 5 were waited for; matrix products, arithmetic and copies ran while one was open for 0% of the time, Pallas kernels for 18%

profile of v4, /device:TPU:0, one launch (start us, length us, event | category | flops | bytes accessed | tf_op | source)
XLA Modules:
  0.0 19.2 jit_solution(4272052774428279139)
XLA Ops:
  0.0 0.5 %collective-permute-start.1 = (f32[16,4,512]{2,1,0:T(4,128)}, f32[16,4,512]{2,1,0:T(4,128)S(1)}, u32[]{:S(2)}, u32[]{:S(2)}) collective-permute-start(f32[16,4,512]{2,1,0:T(4,128)} %fields.1), channel_id=1, source_target_pairs={{0,1},{1,0},{2,3},{3,2},{4,5},{5,4},{6,7},{7,6},{8,9},{9,8},{10,11... | collective-permute-start | bytes 393224 | tf_op jit(solution)/shard_map/ppermute | solution.py:391
  0.5 0.1 collective-permute-start
  0.5 1.0 %stage.1 = (f32[16,4,512]{2,1,0:T(4,128)S(1)}, s32[1,16]{1,0:T(1,128)S(1)}, f32[38]{0:T(128)S(4)}) custom-call(f32[16,4,512]{2,1,0:T(4,128)} %fields.1, s32[1,16]{1,0:T(1,128)} %bitcast.2, f32[4,4]{1,0:T(4,128)} %gradient.1, f32[4]{0:T(128)} %relaxation.1, f32[3,4,4]{2,1,0:T(4,128)} %interaction.1), custom_call_target="tpu_custom_call" | custom-call | tf_op jit(solution)/shard_map/stage/pallas_call | solution.py:394
  1.5 0.2 %collective-permute-done.refs_1_ = s32[1,16]{1,0:T(1,128)S(1)} collective-permute-done((s32[1,16]{1,0:T(1,128)}, s32[1,16]{1,0:T(1,128)S(1)}, u32[]{:S(2)}, u32[]{:S(2)}) %collective-permute-start) | collective-permute-done | bytes 96 | tf_op jit(solution)/shard_map/ppermute | solution.py:391
  1.7 0.3 %route.1 = (s32[32]{0:T(128)S(4)}, s32[32]{0:T(128)S(4)}) custom-call(s32[1,16]{1,0:T(1,128)S(1)} %get-tuple-element.19.refs_0_, s32[1,16]{1,0:T(1,128)S(1)} %collective-permute-done.refs_1_), custom_call_target="tpu_custom_call" | custom-call | tf_op jit(solution)/shard_map/route/pallas_call | solution.py:404
  2.0 0.0 collective-permute-done.1.refs_3_
  2.1 3.8 %collective-permute-start.2 = (f32[136,128]{1,0:T(8,128)S(1)}, f32[136,128]{1,0:T(8,128)S(1)}, u32[]{:S(2)}, u32[]{:S(2)}) collective-permute-start(f32[136,128]{1,0:T(8,128)S(1)} %pack.4), channel_id=1, source_target_pairs={{0,6},{1,7},{2,4},{3,5},{4,2},{5,3},{6,0},{7,1},{8,14},{9,15},{10,... | collective-permute-start | bytes 208904 | tf_op jit(solution)/shard_map/ppermute | solution.py:391
  5.9 0.6 %collective-permute-start.4 = (f32[136,128]{1,0:T(8,128)S(1)}, f32[136,128]{1,0:T(8,128)S(1)}, u32[]{:S(2)}, u32[]{:S(2)}) collective-permute-start(f32[136,128]{1,0:T(8,128)S(1)} %pack.6), channel_id=1, source_target_pairs={{0,4},{1,5},{2,6},{3,7},{4,0},{5,1},{6,2},{7,3},{8,12},{9,13},{10,... | collective-permute-start | bytes 208904 | tf_op jit(solution)/shard_map/ppermute | solution.py:391
  6.5 0.1 collective-permute-start.5
  6.7 0.2 pack.5
  6.9 1.6 %collective-permute-done.2.refs_0_ = f32[136,128]{1,0:T(8,128)S(1)} collective-permute-done((f32[136,128]{1,0:T(8,128)S(1)}, f32[136,128]{1,0:T(8,128)S(1)}, u32[]{:S(2)}, u32[]{:S(2)}) %collective-permute-start.2) | collective-permute-done | bytes 69664 | tf_op jit(solution)/shard_map/ppermute | solution.py:391
  8.4 0.1 early.1
  8.6 1.8 %collective-permute-start.3 = (f32[88,128]{1,0:T(8,128)S(1)}, f32[88,128]{1,0:T(8,128)S(1)}, u32[]{:S(2)}, u32[]{:S(2)}) collective-permute-start(f32[88,128]{1,0:T(8,128)S(1)} %get-tuple-element.24), channel_id=1, source_target_pairs={{0,8},{8,16},{16,24},{24,0},{1,9},{9,17},{17,25},{25,1},{2,10},{10... | collective-permute-start | bytes 135176 | tf_op jit(solution)/shard_map/ppermute | solution.py:453
  10.4 0.0 collective-permute-done.4.refs_0_.refs_1_
  10.4 0.5 %collective-permute-done.5.refs_1_.refs_2_ = f32[136,128]{1,0:T(8,128)S(1)} collective-permute-done((f32[136,128]{1,0:T(8,128)S(1)}, f32[136,128]{1,0:T(8,128)S(1)}, u32[]{:S(2)}, u32[]{:S(2)}) %collective-permute-start.5) | collective-permute-done | bytes 69664 | tf_op jit(solution)/shard_map/ppermute | solution.py:391
  10.9 0.2 %late.1 = (f32[88,128]{1,0:T(8,128)S(1)}, f32[20,8,128]{2,1,0:T(8,128)S(1)}, f32[17,4,128]{2,1,0:T(4,128)S(1)}, f32[17,4,128]{2,1,0:T(4,128)S(1)}) custom-call(f32[136,128]{1,0:T(8,128)S(1)} %collective-permute-done.4.refs_0_.refs_1_, ...), custom_call_target="tpu_custom_call", output_to_operand_aliasing={{1}: (2, {}), {2}: (3, {}), {3}: (4, {})} | custom-call | tf_op jit(solution)/shard_map/late/pallas_call | solution.py:442
  11.1 1.6 %collective-permute-start.6 = (f32[88,128]{1,0:T(8,128)S(1)}, f32[88,128]{1,0:T(8,128)S(1)}, u32[]{:S(2)}, u32[]{:S(2)}) collective-permute-start(f32[88,128]{1,0:T(8,128)S(1)} %get-tuple-element.28), channel_id=1, source_target_pairs={{0,8},{8,16},{16,24},{24,0},{1,9},{9,17},{17,25},{25,1},{2,10},{10... | collective-permute-start | bytes 135176 | tf_op jit(solution)/shard_map/ppermute | solution.py:453
  12.8 2.2 %collective-permute-start.7 = (f32[20,8,128]{2,1,0:T(8,128)S(1)}, f32[20,8,128]{2,1,0:T(8,128)S(1)}, u32[]{:S(2)}, u32[]{:S(2)}) collective-permute-start(f32[20,8,128]{2,1,0:T(8,128)S(1)} %get-tuple-element.29), channel_id=1, source_target_pairs={{8,0},{16,8},{24,16},{0,24},{9,1},{17,9},{25,17},{1,25},{10,2},{18... | collective-permute-start | bytes 245768 | tf_op jit(solution)/shard_map/ppermute | solution.py:454
  15.0 1.4 %inner.1.refs_4_ = f32[28,4,32,128]{3,2,1,0:T(8,128)S(1)} custom-call(f32[136,128]{1,0:T(8,128)S(1)} %collective-permute-done.2.refs_0_, f32[136,128]{1,0:T(8,128)S(1)} %collective-permute-done.4.refs_0_.refs_1_, f32[136,128]{1,0:T(8,128)S(1)} %collective-permute-done.5.refs_1_.refs_2_, f32[136,128]{1,0:T(8,128)S(1)} %get-tuple-element.23.refs_1_.refs_3_, ...), custom_call_target="tpu_custom_call" | custom-call | tf_op jit(solution)/shard_map/inner/pallas_call | solution.py:464
  16.4 0.0 collective-permute-done.3
  16.4 0.8 %collective-permute-done.6 = f32[88,128]{1,0:T(8,128)S(1)} collective-permute-done((f32[88,128]{1,0:T(8,128)S(1)}, f32[88,128]{1,0:T(8,128)S(1)}, u32[]{:S(2)}, u32[]{:S(2)}) %collective-permute-start.6) | collective-permute-done | bytes 45088 | tf_op jit(solution)/shard_map/ppermute | solution.py:453
  17.3 0.2 %catch.1.refs_0_ = f32[20,8,128]{2,1,0:T(8,128)S(1)} custom-call(f32[176,128]{1,0:T(8,128)S(1)} %pad_maximum_fusion.refs_0_), custom_call_target="tpu_custom_call" | custom-call | tf_op jit(solution)/shard_map/catch/pallas_call | solution.py:455
  17.5 0.1 collective-permute-done.7.refs_1_
  17.7 1.5 %outer.1 = (f32[16,4,512]{2,1,0:T(4,128)}, f32[28,4,32,128]{3,2,1,0:T(8,128)S(1)}) custom-call(f32[20,8,128]{2,1,0:T(8,128)S(1)} %catch.1.refs_0_, f32[20,8,128]{2,1,0:T(8,128)S(1)} %collective-permute-done.7.refs_1_, f32[38]{0:T(128)S(4)} %get-tuple-element.30.refs_4_.refs_2_, ...), custom_call_target="tpu_custom_call", output_to_operand_aliasing={{1}: (4, {})} | custom-call | tf_op jit(solution)/shard_map/outer/pallas_call | solution.py:473
  (4 shorter events, 0.1 us)
Async XLA Ops:
  0.0 2.0 %collective-permute-start.1 = (f32[16,4,512]{2,1,0:T(4,128)}, f32[16,4,512]{2,1,0:T(4,128)S(1)}, u32[]{:S(2)}, u32[]{:S(2)}) collective-permute-start(f32[16,4,512]{2,1,0:T(4,128)} %fields.1), channel_id=1, source_target_pairs={{0,1},{1,0},{2,3},{3,2},{4,5},{5,4},{6,7},{7,6},{8,9},{9,8},{10,11... | collective-permute-start | bytes 393224 | tf_op jit(solution)/shard_map/ppermute | solution.py:391
  0.5 1.3 %collective-permute-start = (s32[1,16]{1,0:T(1,128)}, s32[1,16]{1,0:T(1,128)S(1)}, u32[]{:S(2)}, u32[]{:S(2)}) collective-permute-start(s32[1,16]{1,0:T(1,128)} %bitcast.1), channel_id=1, source_target_pairs={{0,1},{1,0},{2,3},{3,2},{4,5},{5,4},{6,7},{7,6},{8,9},{9,8},{10,11... | collective-permute-start | bytes 200 | tf_op jit(solution)/shard_map/ppermute | solution.py:391
  2.1 6.4 %collective-permute-start.2 = (f32[136,128]{1,0:T(8,128)S(1)}, f32[136,128]{1,0:T(8,128)S(1)}, u32[]{:S(2)}, u32[]{:S(2)}) collective-permute-start(f32[136,128]{1,0:T(8,128)S(1)} %pack.4), channel_id=1, source_target_pairs={{0,6},{1,7},{2,4},{3,5},{4,2},{5,3},{6,0},{7,1},{8,14},{9,15},{10,... | collective-permute-start | bytes 208904 | tf_op jit(solution)/shard_map/ppermute | solution.py:391
  5.9 4.5 %collective-permute-start.4 = (f32[136,128]{1,0:T(8,128)S(1)}, f32[136,128]{1,0:T(8,128)S(1)}, u32[]{:S(2)}, u32[]{:S(2)}) collective-permute-start(f32[136,128]{1,0:T(8,128)S(1)} %pack.6), channel_id=1, source_target_pairs={{0,4},{1,5},{2,6},{3,7},{4,0},{5,1},{6,2},{7,3},{8,12},{9,13},{10,... | collective-permute-start | bytes 208904 | tf_op jit(solution)/shard_map/ppermute | solution.py:391
  6.5 4.4 %collective-permute-start.5 = (f32[136,128]{1,0:T(8,128)S(1)}, f32[136,128]{1,0:T(8,128)S(1)}, u32[]{:S(2)}, u32[]{:S(2)}) collective-permute-start(f32[136,128]{1,0:T(8,128)S(1)} %pack.7), channel_id=1, source_target_pairs={{0,2},{1,3},{2,0},{3,1},{4,6},{5,7},{6,4},{7,5},{8,10},{9,11},{10,... | collective-permute-start | bytes 208904 | tf_op jit(solution)/shard_map/ppermute | solution.py:391
  8.6 7.8 %collective-permute-start.3 = (f32[88,128]{1,0:T(8,128)S(1)}, f32[88,128]{1,0:T(8,128)S(1)}, u32[]{:S(2)}, u32[]{:S(2)}) collective-permute-start(f32[88,128]{1,0:T(8,128)S(1)} %get-tuple-element.24), channel_id=1, source_target_pairs={{0,8},{8,16},{16,24},{24,0},{1,9},{9,17},{17,25},{25,1},{2,10},{10... | collective-permute-start | bytes 135176 | tf_op jit(solution)/shard_map/ppermute | solution.py:453
  11.1 6.1 %collective-permute-start.6 = (f32[88,128]{1,0:T(8,128)S(1)}, f32[88,128]{1,0:T(8,128)S(1)}, u32[]{:S(2)}, u32[]{:S(2)}) collective-permute-start(f32[88,128]{1,0:T(8,128)S(1)} %get-tuple-element.28), channel_id=1, source_target_pairs={{0,8},{8,16},{16,24},{24,0},{1,9},{9,17},{17,25},{25,1},{2,10},{10... | collective-permute-start | bytes 135176 | tf_op jit(solution)/shard_map/ppermute | solution.py:453
  12.8 4.9 %collective-permute-start.7 = (f32[20,8,128]{2,1,0:T(8,128)S(1)}, f32[20,8,128]{2,1,0:T(8,128)S(1)}, u32[]{:S(2)}, u32[]{:S(2)}) collective-permute-start(f32[20,8,128]{2,1,0:T(8,128)S(1)} %get-tuple-element.29), channel_id=1, source_target_pairs={{8,0},{16,8},{24,16},{0,24},{9,1},{17,9},{25,17},{1,25},{10,2},{18... | collective-permute-start | bytes 245768 | tf_op jit(solution)/shard_map/ppermute | solution.py:454

commit v5 on v4

--- a/solution.py
+++ b/solution.py
@@ -28,34 +28,38 @@
     return pltpu.roll(v, shift % LANES, 1)
 
 
-def route_kernel(peers, cap, slots, target, other_target, held, label, count):
-    for core, goals in enumerate((target[...], other_target[...])):
-        for peer in range(peers):
-            count[core * peers + peer] = 0
-            for k in range(cap):
-                held[(core * peers + peer) * cap + k] = 0
-                label[(core * peers + peer) * cap + k] = slots
-        for i in range(slots):
-            goal = goals[0, i]
-            peer = core * peers + lax.div(goal, slots)
-            k = count[peer]
-            count[peer] = k + 1
-            held[peer * cap + k] = i
-            label[peer * cap + k] = lax.rem(goal, slots)
-
-
-def pack_kernel(peers, cap, flip, held, label, fields, other_fields, out, *weights):
+def route(peers, cap, slots, goal_of, held, label, count):
+    for peer in range(peers):
+        count[peer] = 0
+        for k in range(cap):
+            held[peer * cap + k] = 0
+            label[peer * cap + k] = slots
+    for i in range(slots):
+        goal = goal_of(i)
+        peer = lax.div(goal, slots)
+        k = count[peer]
+        count[peer] = k + 1
+        held[peer * cap + k] = i
+        label[peer * cap + k] = lax.rem(goal, slots)
+
+
+def other_route_kernel(peers, cap, slots, target, held, label, count):
+    goals = target[...]
+    route(peers, cap, slots, lambda i: goals[0, i], held, label, count)
+
+
+def pack_kernel(peers, cap, flip, held, label, other_held, other_label, fields, other_fields, out, *weights):
     _, y, _ = lane_parts((COMP, LANES))
     row = lax.broadcasted_iota(jnp.int32, (8, LANES), 1)
     peer = lax.axis_index("loc") ^ flip
     places = [lax.rem(peer + d, peers) * cap for d in (0, 1, peers - 1)]
     names = jnp.zeros((8, LANES), jnp.int32)
-    for core, source in enumerate((fields, other_fields)):
+    for core, (source, held, label) in enumerate(((fields, held, label), (other_fields, other_held, other_label))):
         for k in range(cap):
-            own, high, low = [held[core * peers * cap + at + k] for at in places]
+            own, high, low = [held[at + k] for at in places]
             entry = core * cap + k
             for n, at in enumerate(places):
-                names = jnp.where(row == 2 * cap * n + entry, label[core * peers * cap + at + k], names)
+                names = jnp.where(row == 2 * cap * n + entry, label[at + k], names)
             for chunk in range(CHUNKS):
                 part = slice(chunk * LANES, (chunk + 1) * LANES)
                 at = entry * ROWS + chunk * COMP
@@ -112,11 +116,12 @@
     return corners, names, names + 8 * ((count + 7) // 8)
 
 
-def bundle(cap, got, out):
-    corners, names, end = bundle_rows(cap, len(got))
+def bundle(cap, count, got, out, before=0):
+    corners, names, end = bundle_rows(cap, count)
     _, y, _ = lane_parts((COMP, LANES))
-    out[names:, :] = jnp.zeros((end - names, LANES), out.dtype)
-    for n, message in enumerate(got):
+    if before == 0:
+        out[names:, :] = jnp.zeros((end - names, LANES), out.dtype)
+    for n, message in enumerate(got, before):
         for k in range(2 * cap):
             at = (2 * cap * n + k) * HALF
             out[at : at + HALF, :] = message[k * ROWS + HALF : (k + 1) * ROWS, :]
@@ -130,30 +135,39 @@
 def put_down(cap, got, down, high, low):
     for message, whole, joined, slot, high_slot, low_slot in entries(cap, got):
         down[slot] = message[whole : whole + HALF, :]
-        rows = message[joined : joined + COMP, :]
-        high[high_slot] = rows
-        low[low_slot] = rows
+        put_corner(message[joined : joined + COMP, :], high, high_slot, low, low_slot)
+
+
+def put_corner(rows, high, high_slot, low, low_slot):
+    high[pl.ds(pl.multiple_of(high_slot * COMP, COMP), COMP), :] = rows
+    low[pl.ds(pl.multiple_of(low_slot * COMP, COMP), COMP), :] = rows
 
 
 def put_sides(slots, faces, high, low):
-    _, y, _ = lane_parts((COMP, LANES))
-    pairs = slots // 2
-    for q in range(pairs):
-        one, two = [jnp.where(y < 4, high[t], low[t]) for t in (q, q + pairs)]
-        at = (q % 2) * COMP
-        faces[slots + q // 2, at : at + COMP, :] = squeeze(one, two, y)
-
-
-def early_kernel(cap, *refs):
+    half = slots // 2 * COMP
+    _, y, _ = lane_parts((half, LANES))
+    one, two = [jnp.where(y < 4, high[at : at + half, :], low[at : at + half, :]) for at in (0, half)]
+    both = squeeze(one, two, y)
+    for n in range(half // HALF):
+        faces[slots + n] = both[n * HALF : (n + 1) * HALF]
+
+
+def early_kernel(cap, count, *refs):
     got, (up, down, high, low) = refs[:-4], refs[-4:]
-    bundle(cap, got, up)
+    bundle(cap, count, got, up)
     put_down(cap, got, down, high, low)
 
 
-def late_kernel(cap, slots, count, *refs):
-    got, (up, down, high, low) = refs[:count], refs[-4:]
-    bundle(cap, got, up)
+def next_kernel(cap, *refs):
+    got, (up, down, high, low) = refs[:-7], refs[-4:]
+    bundle(cap, len(got) + 1, got, up)
     put_down(cap, got, down, high, low)
+
+
+def last_kernel(cap, slots, count, message, *refs):
+    up, down, high, low = refs[-4:]
+    bundle(cap, count, [message], up, count - 1)
+    put_down(cap, [message], down, high, low)
     put_sides(slots, down, high, low)
 
 
@@ -173,14 +187,19 @@
                 rows = ref[at : at + COMP, :]
                 if k >= cap:
                     rows = second_of(rows, y)
-                high[slot_of[0, 2 * cap + k]] = rows
-                low[slot_of[0, 4 * cap + k]] = rows
+                put_corner(rows, high, slot_of[0, 2 * cap + k], low, slot_of[0, 4 * cap + k])
     put_sides(slots, faces, high, low)
 
 
-def stage_kernel(fields, target, gradient, relaxation, interaction, out, goals, table):
-    out[...] = fields[...]
-    goals[...] = target[...]
+def stage_kernel(peers, cap, slots, *refs):
+    arguments, (out, held, label, table), inside, (count, sems) = refs[:5], refs[5:9], refs[9:13], refs[13:]
+    copies = [pltpu.make_async_copy(a, b, sems.at[n]) for n, (a, b) in enumerate(zip(arguments, (out, *inside)))]
+    for copy in copies[1:] + copies[:1]:
+        copy.start()
+    for copy in copies[1:]:
+        copy.wait()
+    target, gradient, relaxation, interaction = inside
+    route(peers, cap, slots, lambda i: target[i], held, label, count)
     for i in range(COMP):
         rate = relaxation[i]
         table[i] = rate
@@ -191,6 +210,7 @@
         for order in range(3):
             table[at] = interaction[order, i, j]
             at += 1
+    copies[0].wait()
 
 
 def coefficients(table):
@@ -390,27 +410,29 @@
     def cross(array, flip):
         return lax.ppermute(array, "loc", [(i, i ^ flip) for i in range(peers)])
 
-    target = target.reshape(1, slots)
-    staged, goals, table = pl.pallas_call(
-        stage_kernel,
-        out_shape=(shape(*fields.shape), pltpu.VMEM(target.shape, jnp.int32), pltpu.SMEM((TABLE,), f32)),
-        in_specs=[VMEM] * 2 + [SMEM] * 3,
-        out_specs=(VMEM, VMEM, SMEM),
+    numbers = pltpu.SMEM((peers * cap,), jnp.int32)
+    arguments = fields, target, gradient_matrix, relaxation, interaction
+    staged, held, label, table = pl.pallas_call(
+        lambda *refs: stage_kernel(peers, cap, slots, *refs),
+        out_shape=(shape(*fields.shape), numbers, numbers, pltpu.SMEM((TABLE,), f32)),
+        in_specs=[pl.BlockSpec(memory_space=pl.ANY)] * 5,
+        out_specs=(VMEM, SMEM, SMEM, SMEM),
+        scratch_shapes=[pltpu.SMEM(a.shape, a.dtype) for a in arguments[1:]]
+        + [pltpu.SMEM((peers,), jnp.int32), pltpu.SemaphoreType.DMA((5,))],
         name="stage",
-    )(fields, target, gradient_matrix, relaxation, interaction)
+    )(*arguments)
     table = pltpu.with_memory_space_constraint(table, pltpu.SMEM)
-    other_fields, other_target = cross(fields, 1), cross(target, 1)
-    entry_count = 2 * peers * cap
-    routes = pl.pallas_call(
-        lambda *refs: route_kernel(peers, cap, slots, *refs),
-        out_shape=(pltpu.SMEM((entry_count,), jnp.int32),) * 2,
-        in_specs=[VMEM] * 2,
+    other_fields, other_target = cross(fields, 1), cross(target.reshape(1, slots), 1)
+    other = pl.pallas_call(
+        lambda *refs: other_route_kernel(peers, cap, slots, *refs),
+        out_shape=(numbers, numbers),
+        in_specs=[VMEM],
         out_specs=(SMEM,) * 2,
-        scratch_shapes=[pltpu.SMEM((2 * peers,), jnp.int32)],
+        scratch_shapes=[pltpu.SMEM((peers,), jnp.int32)],
         name="route",
         compiler_params=params,
-    )(*inside(goals, other_target))
-    routes = [pltpu.with_memory_space_constraint(a, pltpu.SMEM) for a in routes]
+    )(*inside(other_target))
+    routes = [pltpu.with_memory_space_constraint(a, pltpu.SMEM) for a in (held, label, *other)]
 
     def pack(flip):
         message = shape(4 * cap * ROWS + 8, LANES)
@@ -418,7 +440,7 @@
         return pl.pallas_call(
             lambda *refs: pack_kernel(peers, cap, flip, *refs),
             out_shape=(message, *extra),
-            in_specs=[SMEM] * 2 + [VMEM] * 2,
+            in_specs=[SMEM] * 4 + [VMEM] * 2,
             out_specs=(VMEM,) * (1 + len(extra)),
             name="pack",
             compiler_params=params,
@@ -430,24 +452,35 @@
     got = inside(*[cross(message, flip) for (message,), flip in zip(sent, flips)], own)
     early, late = got[: chips // 2 - 1] + got[-1:], got[chips // 2 - 1 : -1]
     counts = len(early), len(late)
-    face, corner = (slots + slots // 4, HALF, LANES), (slots + 1, COMP, LANES)
+    face, corner = (slots + slots // 4, HALF, LANES), ((slots + 2) * COMP, LANES)
+    corners = shape(*face), shape(*corner), shape(*corner)
     up_early, *down = pl.pallas_call(
-        lambda *refs: early_kernel(cap, *refs),
-        out_shape=(shape(bundle_rows(cap, counts[0])[-1], LANES), shape(*face), shape(*corner), shape(*corner)),
+        lambda *refs: early_kernel(cap, counts[0], *refs),
+        out_shape=(shape(bundle_rows(cap, counts[0])[-1], LANES), *corners),
         in_specs=[VMEM] * counts[0],
         out_specs=(VMEM,) * 4,
         name="early",
         compiler_params=params,
     )(*early)
+    up_late = shape(bundle_rows(cap, counts[1])[-1], LANES)
+    going = pl.pallas_call(
+        lambda *refs: next_kernel(cap, *refs),
+        out_shape=(up_late, *corners),
+        in_specs=[VMEM] * (counts[1] + 2),
+        out_specs=(VMEM,) * 4,
+        input_output_aliases={counts[1] - 1 + n: 1 + n for n in range(3)},
+        name="next",
+        compiler_params=params,
+    )(*late[:-1], *inside(*down))
     up_late, down, *_ = pl.pallas_call(
-        lambda *refs: late_kernel(cap, slots, counts[1], *refs),
-        out_shape=(shape(bundle_rows(cap, counts[1])[-1], LANES), shape(*face), shape(*corner), shape(*corner)),
-        in_specs=[VMEM] * (counts[1] + 3),
+        lambda *refs: last_kernel(cap, slots, counts[1], *refs),
+        out_shape=(up_late, *corners),
+        in_specs=[VMEM] * 5,
         out_specs=(VMEM,) * 4,
-        input_output_aliases={counts[1] + n: 1 + n for n in range(3)},
-        name="late",
-        compiler_params=params,
-    )(*late, *inside(*down))
+        input_output_aliases={1 + n: n for n in range(4)},
+        name="last",
+        compiler_params=params,
+    )(late[-1], *inside(*going))
     forward = [(i, (i + 1) % groups) for i in range(groups)]
     backward = [(j, i) for i, j in forward]
     from_below = [lax.ppermute(up, "grp", forward) for up in (up_early, up_late)]

time: 19.3 us -> 19.1 us (0.990)
    pallas_call x4 -> x5, Pallas kernels: 1.62 us -> 1.62 us  [the longest x1 1 us: per_device(): pl.pallas_call(lambda *refs: stage_kernel(peers, cap, slots, *refs), out_...]
  transfers between devices with their start and end apart: 8 -> 8, of which waited for: 5 -> 5; matrix products, arithmetic and copies ran while one was open for 0% -> 0% of each run, Pallas kernels for 18% -> 19%
where the time goes in v5:
time: 19.1 us; the launch traced here: 19 us
  starting transfers between devices  10.7 us (56%)
  Pallas kernels  5.04 us (26%)
  waiting for transfers between devices  3.12 us (16%)
    ppermute x5, starting transfers between devices, cross(): return lax.ppermute(array, 'loc', [(i, i ^ flip) for i in range(peers)])  5.04 us
    ppermute x2, starting transfers between devices, per_device(): lax.ppermute(up, 'grp', forward)  3.43 us
    ppermute x1, starting transfers between devices, per_device(): above = lax.ppermute(down, 'grp', backward)  2.25 us
    ppermute x5, waiting for transfers between devices, cross(): return lax.ppermute(array, 'loc', [(i, i ^ flip) for i in range(peers)])  2.14 us
    pallas_call x1, Pallas kernels, per_device(): pl.pallas_call(lambda *refs: outer_kernel(slots, *refs), out_shape=(jax.S...  1.48 us
    pallas_call x1, Pallas kernels, per_device(): pl.pallas_call(lambda *refs: inner_kernel(cap, slots, peers, *refs), out_...  1.43 us
    pallas_call x1, Pallas kernels, per_device(): pl.pallas_call(lambda *refs: stage_kernel(peers, cap, slots, *refs), out_...  1 us
    ppermute x2, waiting for transfers between devices, per_device(): lax.ppermute(up, 'grp', forward)  0.82 us
  transfers between devices with their start and end apart: 8, of which 5 were waited for; matrix products, arithmetic and copies ran while one was open for 0% of the time, Pallas kernels for 19%

profile of v5, /device:TPU:0, one launch (start us, length us, event | category | flops | bytes accessed | tf_op | source)
XLA Modules:
  0.0 19.0 jit_solution(17462528388050698491)
XLA Ops:
  0.0 0.5 %collective-permute-start.1 = (f32[16,4,512]{2,1,0:T(4,128)}, f32[16,4,512]{2,1,0:T(4,128)S(1)}, u32[]{:S(2)}, u32[]{:S(2)}) collective-permute-start(f32[16,4,512]{2,1,0:T(4,128)} %refs_0_.1), channel_id=1, source_target_pairs={{0,1},{1,0},{2,3},{3,2},{4,5},{5,4},{6,7},{7,6},{8,9},{9,8},{10,11... | collective-permute-start | bytes 393224 | tf_op jit(solution)/shard_map/ppermute | solution.py:411
  0.5 0.1 collective-permute-start
  0.5 1.0 %stage.1 = (f32[16,4,512]{2,1,0:T(4,128)S(1)}, s32[16]{0:T(128)S(4)}, s32[16]{0:T(128)S(4)}, f32[38]{0:T(128)S(4)}) custom-call(f32[16,4,512]{2,1,0:T(4,128)} %refs_0_.1, s32[16]{0:T(128)} %refs_1_.1, f32[4,4]{1,0:T(4,128)} %refs_2_.1, f32[4]{0:T(128)} %refs_3_.1, f32[3,4,4]{2,1,0:T(4,128)} %refs_4_.1), custom_call_target="tpu_custom_call" | custom-call | tf_op jit(solution)/shard_map/stage/pallas_call | solution.py:415
  1.5 0.2 collective-permute-done.refs_0_
  1.7 0.2 route.1
  1.9 0.0 collective-permute-done.1.refs_5_
  2.0 3.8 %collective-permute-start.2 = (f32[136,128]{1,0:T(8,128)S(1)}, f32[136,128]{1,0:T(8,128)S(1)}, u32[]{:S(2)}, u32[]{:S(2)}) collective-permute-start(f32[136,128]{1,0:T(8,128)S(1)} %pack.4), channel_id=1, source_target_pairs={{0,6},{1,7},{2,4},{3,5},{4,2},{5,3},{6,0},{7,1},{8,14},{9,15},{10,... | collective-permute-start | bytes 208904 | tf_op jit(solution)/shard_map/ppermute | solution.py:411
  5.8 0.6 %collective-permute-start.5 = (f32[136,128]{1,0:T(8,128)S(1)}, f32[136,128]{1,0:T(8,128)S(1)}, u32[]{:S(2)}, u32[]{:S(2)}) collective-permute-start(f32[136,128]{1,0:T(8,128)S(1)} %pack.7), channel_id=1, source_target_pairs={{0,4},{1,5},{2,6},{3,7},{4,0},{5,1},{6,2},{7,3},{8,12},{9,13},{10,... | collective-permute-start | bytes 208904 | tf_op jit(solution)/shard_map/ppermute | solution.py:411
  6.4 0.1 collective-permute-start.4
  6.6 0.2 pack.5
  6.7 1.6 %collective-permute-done.2.refs_0_ = f32[136,128]{1,0:T(8,128)S(1)} collective-permute-done((f32[136,128]{1,0:T(8,128)S(1)}, f32[136,128]{1,0:T(8,128)S(1)}, u32[]{:S(2)}, u32[]{:S(2)}) %collective-permute-start.2) | collective-permute-done | bytes 69664 | tf_op jit(solution)/shard_map/ppermute | solution.py:411
  8.3 0.1 early.1
  8.5 1.8 %collective-permute-start.3 = (f32[88,128]{1,0:T(8,128)S(1)}, f32[88,128]{1,0:T(8,128)S(1)}, u32[]{:S(2)}, u32[]{:S(2)}) collective-permute-start(f32[88,128]{1,0:T(8,128)S(1)} %get-tuple-element.30), channel_id=1, source_target_pairs={{0,8},{8,16},{16,24},{24,0},{1,9},{9,17},{17,25},{25,1},{2,10},{10... | collective-permute-start | bytes 135176 | tf_op jit(solution)/shard_map/ppermute | solution.py:486
  10.3 0.0 collective-permute-done.5.refs_0_.refs_1_
  10.3 0.1 next.1
  10.4 0.3 %collective-permute-done.4.refs_0_.refs_2_ = f32[136,128]{1,0:T(8,128)S(1)} collective-permute-done((f32[136,128]{1,0:T(8,128)S(1)}, f32[136,128]{1,0:T(8,128)S(1)}, u32[]{:S(2)}, u32[]{:S(2)}) %collective-permute-start.4) | collective-permute-done | bytes 69664 | tf_op jit(solution)/shard_map/ppermute | solution.py:411
  10.8 0.2 last.1
  11.0 1.6 %collective-permute-start.6 = (f32[88,128]{1,0:T(8,128)S(1)}, f32[88,128]{1,0:T(8,128)S(1)}, u32[]{:S(2)}, u32[]{:S(2)}) collective-permute-start(f32[88,128]{1,0:T(8,128)S(1)} %get-tuple-element.38), channel_id=1, source_target_pairs={{0,8},{8,16},{16,24},{24,0},{1,9},{9,17},{17,25},{25,1},{2,10},{10... | collective-permute-start | bytes 135176 | tf_op jit(solution)/shard_map/ppermute | solution.py:486
  12.6 2.2 %collective-permute-start.7 = (f32[20,8,128]{2,1,0:T(8,128)S(1)}, f32[20,8,128]{2,1,0:T(8,128)S(1)}, u32[]{:S(2)}, u32[]{:S(2)}) collective-permute-start(f32[20,8,128]{2,1,0:T(8,128)S(1)} %get-tuple-element.39), channel_id=1, source_target_pairs={{8,0},{16,8},{24,16},{0,24},{9,1},{17,9},{25,17},{1,25},{10,2},{18... | collective-permute-start | bytes 245768 | tf_op jit(solution)/shard_map/ppermute | solution.py:487
  14.8 1.4 %inner.1.refs_4_ = f32[28,4,32,128]{3,2,1,0:T(8,128)S(1)} custom-call(f32[136,128]{1,0:T(8,128)S(1)} %collective-permute-done.2.refs_0_, f32[136,128]{1,0:T(8,128)S(1)} %collective-permute-done.5.refs_0_.refs_1_, f32[136,128]{1,0:T(8,128)S(1)} %collective-permute-done.4.refs_0_.refs_2_, f32[136,128]{1,0:T(8,128)S(1)} %get-tuple-element.29.refs_1_.refs_3_, ...), custom_call_target="tpu_custom_call" | custom-call | tf_op jit(solution)/shard_map/inner/pallas_call | solution.py:497
  16.2 0.0 collective-permute-done.3
  16.3 0.8 %collective-permute-done.6 = f32[88,128]{1,0:T(8,128)S(1)} collective-permute-done((f32[88,128]{1,0:T(8,128)S(1)}, f32[88,128]{1,0:T(8,128)S(1)}, u32[]{:S(2)}, u32[]{:S(2)}) %collective-permute-start.6) | collective-permute-done | bytes 45088 | tf_op jit(solution)/shard_map/ppermute | solution.py:486
  17.1 0.2 %catch.1.refs_0_ = f32[20,8,128]{2,1,0:T(8,128)S(1)} custom-call(f32[176,128]{1,0:T(8,128)S(1)} %pad_maximum_fusion.refs_0_), custom_call_target="tpu_custom_call" | custom-call | tf_op jit(solution)/shard_map/catch/pallas_call | solution.py:488
  17.3 0.2 collective-permute-done.7.refs_1_
  17.5 1.5 %outer.1 = (f32[16,4,512]{2,1,0:T(4,128)}, f32[28,4,32,128]{3,2,1,0:T(8,128)S(1)}) custom-call(f32[20,8,128]{2,1,0:T(8,128)S(1)} %catch.1.refs_0_, f32[20,8,128]{2,1,0:T(8,128)S(1)} %collective-permute-done.7.refs_1_, f32[38]{0:T(128)S(4)} %get-tuple-element.40.refs_4_.refs_2_, ...), custom_call_target="tpu_custom_call", output_to_operand_aliasing={{1}: (4, {})} | custom-call | tf_op jit(solution)/shard_map/outer/pallas_call | solution.py:506
  (4 shorter events, 0.1 us)
Async XLA Ops:
  0.0 1.9 %collective-permute-start.1 = (f32[16,4,512]{2,1,0:T(4,128)}, f32[16,4,512]{2,1,0:T(4,128)S(1)}, u32[]{:S(2)}, u32[]{:S(2)}) collective-permute-start(f32[16,4,512]{2,1,0:T(4,128)} %refs_0_.1), channel_id=1, source_target_pairs={{0,1},{1,0},{2,3},{3,2},{4,5},{5,4},{6,7},{7,6},{8,9},{9,8},{10,11... | collective-permute-start | bytes 393224 | tf_op jit(solution)/shard_map/ppermute | solution.py:411
  0.5 1.3 %collective-permute-start = (s32[1,16]{1,0:T(1,128)}, s32[1,16]{1,0:T(1,128)S(1)}, u32[]{:S(2)}, u32[]{:S(2)}) collective-permute-start(s32[1,16]{1,0:T(1,128)} %bitcast.1), channel_id=1, source_target_pairs={{0,1},{1,0},{2,3},{3,2},{4,5},{5,4},{6,7},{7,6},{8,9},{9,8},{10,11... | collective-permute-start | bytes 200 | tf_op jit(solution)/shard_map/ppermute | solution.py:411
  2.0 6.4 %collective-permute-start.2 = (f32[136,128]{1,0:T(8,128)S(1)}, f32[136,128]{1,0:T(8,128)S(1)}, u32[]{:S(2)}, u32[]{:S(2)}) collective-permute-start(f32[136,128]{1,0:T(8,128)S(1)} %pack.4), channel_id=1, source_target_pairs={{0,6},{1,7},{2,4},{3,5},{4,2},{5,3},{6,0},{7,1},{8,14},{9,15},{10,... | collective-permute-start | bytes 208904 | tf_op jit(solution)/shard_map/ppermute | solution.py:411
  5.8 4.5 %collective-permute-start.5 = (f32[136,128]{1,0:T(8,128)S(1)}, f32[136,128]{1,0:T(8,128)S(1)}, u32[]{:S(2)}, u32[]{:S(2)}) collective-permute-start(f32[136,128]{1,0:T(8,128)S(1)} %pack.7), channel_id=1, source_target_pairs={{0,4},{1,5},{2,6},{3,7},{4,0},{5,1},{6,2},{7,3},{8,12},{9,13},{10,... | collective-permute-start | bytes 208904 | tf_op jit(solution)/shard_map/ppermute | solution.py:411
  6.4 4.4 %collective-permute-start.4 = (f32[136,128]{1,0:T(8,128)S(1)}, f32[136,128]{1,0:T(8,128)S(1)}, u32[]{:S(2)}, u32[]{:S(2)}) collective-permute-start(f32[136,128]{1,0:T(8,128)S(1)} %pack.6), channel_id=1, source_target_pairs={{0,2},{1,3},{2,0},{3,1},{4,6},{5,7},{6,4},{7,5},{8,10},{9,11},{10,... | collective-permute-start | bytes 208904 | tf_op jit(solution)/shard_map/ppermute | solution.py:411
  8.5 7.8 %collective-permute-start.3 = (f32[88,128]{1,0:T(8,128)S(1)}, f32[88,128]{1,0:T(8,128)S(1)}, u32[]{:S(2)}, u32[]{:S(2)}) collective-permute-start(f32[88,128]{1,0:T(8,128)S(1)} %get-tuple-element.30), channel_id=1, source_target_pairs={{0,8},{8,16},{16,24},{24,0},{1,9},{9,17},{17,25},{25,1},{2,10},{10... | collective-permute-start | bytes 135176 | tf_op jit(solution)/shard_map/ppermute | solution.py:486
  11.0 6.1 %collective-permute-start.6 = (f32[88,128]{1,0:T(8,128)S(1)}, f32[88,128]{1,0:T(8,128)S(1)}, u32[]{:S(2)}, u32[]{:S(2)}) collective-permute-start(f32[88,128]{1,0:T(8,128)S(1)} %get-tuple-element.38), channel_id=1, source_target_pairs={{0,8},{8,16},{16,24},{24,0},{1,9},{9,17},{17,25},{25,1},{2,10},{10... | collective-permute-start | bytes 135176 | tf_op jit(solution)/shard_map/ppermute | solution.py:486
  12.6 4.9 %collective-permute-start.7 = (f32[20,8,128]{2,1,0:T(8,128)S(1)}, f32[20,8,128]{2,1,0:T(8,128)S(1)}, u32[]{:S(2)}, u32[]{:S(2)}) collective-permute-start(f32[20,8,128]{2,1,0:T(8,128)S(1)} %get-tuple-element.39), channel_id=1, source_target_pairs={{8,0},{16,8},{24,16},{0,24},{9,1},{17,9},{25,17},{1,25},{10,2},{18... | collective-permute-start | bytes 245768 | tf_op jit(solution)/shard_map/ppermute | solution.py:487

commit v6 on v5

--- a/solution.py
+++ b/solution.py
@@ -446,7 +446,7 @@
             compiler_params=params,
         )(*routes, *inside(staged, other_fields))
 
-    flips = [2 * j for j in reversed(range(chips))]
+    flips = [2 * j + 1 for j in reversed(range(1, chips))] + [0]
     *sent, (own, weights) = [pack(flip) for flip in flips]
     weights = inside(weights)[0]
     got = inside(*[cross(message, flip) for (message,), flip in zip(sent, flips)], own)

time: 19.1 us -> 18.9 us (0.990)
  starting transfers between devices: 10.7 us -> 10.5 us
    ppermute x1, waiting for transfers between devices: 0.16 us -> 0.59 us  [per_device(): above = lax.ppermute(down, 'grp', backward)]
    ppermute x5, starting transfers between devices: 5.04 us -> 4.76 us  [cross(): return lax.ppermute(array, 'loc', [(i, i ^ flip) for i in range(peers)])]
    ppermute x5, waiting for transfers between devices: 2.14 us -> 1.94 us  [cross(): return lax.ppermute(array, 'loc', [(i, i ^ flip) for i in range(peers)])]
where the time goes in v6:
time: 18.9 us; the launch traced here: 18.8 us
  starting transfers between devices  10.5 us (56%)
  Pallas kernels  5.02 us (27%)
  waiting for transfers between devices  3.18 us (17%)
    ppermute x5, starting transfers between devices, cross(): return lax.ppermute(array, 'loc', [(i, i ^ flip) for i in range(peers)])  4.76 us
    ppermute x2, starting transfers between devices, per_device(): lax.ppermute(up, 'grp', forward)  3.5 us
    ppermute x1, starting transfers between devices, per_device(): above = lax.ppermute(down, 'grp', backward)  2.25 us
    ppermute x5, waiting for transfers between devices, cross(): return lax.ppermute(array, 'loc', [(i, i ^ flip) for i in range(peers)])  1.94 us
    pallas_call x1, Pallas kernels, per_device(): pl.pallas_call(lambda *refs: outer_kernel(slots, *refs), out_shape=(jax.S...  1.48 us
    pallas_call x1, Pallas kernels, per_device(): pl.pallas_call(lambda *refs: inner_kernel(cap, slots, peers, *refs), out_...  1.41 us
    pallas_call x1, Pallas kernels, per_device(): pl.pallas_call(lambda *refs: stage_kernel(peers, cap, slots, *refs), out_...  1 us
    ppermute x2, waiting for transfers between devices, per_device(): lax.ppermute(up, 'grp', forward)  0.65 us
  transfers between devices with their start and end apart: 8, of which 5 were waited for; matrix products, arithmetic and copies ran while one was open for 0% of the time, Pallas kernels for 19%

profile of v6, /device:TPU:0, one launch (start us, length us, event | category | flops | bytes accessed | tf_op | source)
XLA Modules:
  0.0 18.8 jit_solution(821457225721648648)
XLA Ops:
  0.0 0.5 %collective-permute-start.1 = (f32[16,4,512]{2,1,0:T(4,128)}, f32[16,4,512]{2,1,0:T(4,128)S(1)}, u32[]{:S(2)}, u32[]{:S(2)}) collective-permute-start(f32[16,4,512]{2,1,0:T(4,128)} %refs_0_.1), channel_id=1, source_target_pairs={{0,1},{1,0},{2,3},{3,2},{4,5},{5,4},{6,7},{7,6},{8,9},{9,8},{10,11... | collective-permute-start | bytes 393224 | tf_op jit(solution)/shard_map/ppermute | solution.py:411
  0.5 0.1 collective-permute-start
  0.5 1.0 %stage.1 = (f32[16,4,512]{2,1,0:T(4,128)S(1)}, s32[16]{0:T(128)S(4)}, s32[16]{0:T(128)S(4)}, f32[38]{0:T(128)S(4)}) custom-call(f32[16,4,512]{2,1,0:T(4,128)} %refs_0_.1, s32[16]{0:T(128)} %refs_1_.1, f32[4,4]{1,0:T(4,128)} %refs_2_.1, f32[4]{0:T(128)} %refs_3_.1, f32[3,4,4]{2,1,0:T(4,128)} %refs_4_.1), custom_call_target="tpu_custom_call" | custom-call | tf_op jit(solution)/shard_map/stage/pallas_call | solution.py:415
  1.5 0.2 %collective-permute-done.refs_0_ = s32[1,16]{1,0:T(1,128)S(1)} collective-permute-done((s32[1,16]{1,0:T(1,128)}, s32[1,16]{1,0:T(1,128)S(1)}, u32[]{:S(2)}, u32[]{:S(2)}) %collective-permute-start) | collective-permute-done | bytes 96 | tf_op jit(solution)/shard_map/ppermute | solution.py:411
  1.7 0.2 %route.1 = (s32[16]{0:T(128)S(4)}, s32[16]{0:T(128)S(4)}) custom-call(s32[1,16]{1,0:T(1,128)S(1)} %collective-permute-done.refs_0_), custom_call_target="tpu_custom_call" | custom-call | tf_op jit(solution)/shard_map/route/pallas_call | solution.py:426
  1.9 0.0 collective-permute-done.1.refs_5_
  2.0 3.6 %collective-permute-start.2 = (f32[136,128]{1,0:T(8,128)S(1)}, f32[136,128]{1,0:T(8,128)S(1)}, u32[]{:S(2)}, u32[]{:S(2)}) collective-permute-start(f32[136,128]{1,0:T(8,128)S(1)} %pack.4), channel_id=1, source_target_pairs={{0,7},{1,6},{2,5},{3,4},{4,3},{5,2},{6,1},{7,0},{8,15},{9,14},{10,... | collective-permute-start | bytes 208904 | tf_op jit(solution)/shard_map/ppermute | solution.py:411
  5.6 0.5 %collective-permute-start.5 = (f32[136,128]{1,0:T(8,128)S(1)}, f32[136,128]{1,0:T(8,128)S(1)}, u32[]{:S(2)}, u32[]{:S(2)}) collective-permute-start(f32[136,128]{1,0:T(8,128)S(1)} %pack.7), channel_id=1, source_target_pairs={{0,5},{1,4},{2,7},{3,6},{4,1},{5,0},{6,3},{7,2},{8,13},{9,12},{10,... | collective-permute-start | bytes 208904 | tf_op jit(solution)/shard_map/ppermute | solution.py:411
  6.1 0.1 collective-permute-start.4
  6.3 0.2 pack.5
  6.4 1.7 %collective-permute-done.2.refs_0_ = f32[136,128]{1,0:T(8,128)S(1)} collective-permute-done((f32[136,128]{1,0:T(8,128)S(1)}, f32[136,128]{1,0:T(8,128)S(1)}, u32[]{:S(2)}, u32[]{:S(2)}) %collective-permute-start.2) | collective-permute-done | bytes 69664 | tf_op jit(solution)/shard_map/ppermute | solution.py:411
  8.1 0.1 early.1
  8.2 1.9 %collective-permute-start.3 = (f32[88,128]{1,0:T(8,128)S(1)}, f32[88,128]{1,0:T(8,128)S(1)}, u32[]{:S(2)}, u32[]{:S(2)}) collective-permute-start(f32[88,128]{1,0:T(8,128)S(1)} %get-tuple-element.30), channel_id=1, source_target_pairs={{0,8},{8,16},{16,24},{24,0},{1,9},{9,17},{17,25},{25,1},{2,10},{10... | collective-permute-start | bytes 135176 | tf_op jit(solution)/shard_map/ppermute | solution.py:486
  10.2 0.0 collective-permute-done.5.refs_0_.refs_1_
  10.2 0.1 next.1
  10.3 0.1 collective-permute-done.4.refs_0_.refs_2_
  10.4 0.2 %last.1 = (f32[88,128]{1,0:T(8,128)S(1)}, f32[20,8,128]{2,1,0:T(8,128)S(1)}, f32[72,128]{1,0:T(8,128)S(1)}, f32[72,128]{1,0:T(8,128)S(1)}) custom-call(f32[136,128]{1,0:T(8,128)S(1)} %collective-permute-done.4.refs_0_.refs_2_, f32[88,128]{1,0:T(8,128)S(1)} %get-tuple-element.34.refs_1_, ...), custom_call_target="tpu_custom_call", output_to_operand_aliasing={{0}: (1, {}), {1}: (2, {}), {2}: (3, {}), {3}: (4, {})} | custom-call | tf_op jit(solution)/shard_map/last/pallas_call | solution.py:475
  10.6 1.6 %collective-permute-start.6 = (f32[88,128]{1,0:T(8,128)S(1)}, f32[88,128]{1,0:T(8,128)S(1)}, u32[]{:S(2)}, u32[]{:S(2)}) collective-permute-start(f32[88,128]{1,0:T(8,128)S(1)} %get-tuple-element.38), channel_id=1, source_target_pairs={{0,8},{8,16},{16,24},{24,0},{1,9},{9,17},{17,25},{25,1},{2,10},{10... | collective-permute-start | bytes 135176 | tf_op jit(solution)/shard_map/ppermute | solution.py:486
  12.1 2.2 %collective-permute-start.7 = (f32[20,8,128]{2,1,0:T(8,128)S(1)}, f32[20,8,128]{2,1,0:T(8,128)S(1)}, u32[]{:S(2)}, u32[]{:S(2)}) collective-permute-start(f32[20,8,128]{2,1,0:T(8,128)S(1)} %get-tuple-element.39), channel_id=1, source_target_pairs={{8,0},{16,8},{24,16},{0,24},{9,1},{17,9},{25,17},{1,25},{10,2},{18... | collective-permute-start | bytes 245768 | tf_op jit(solution)/shard_map/ppermute | solution.py:487
  14.4 1.4 %inner.1.refs_4_ = f32[28,4,32,128]{3,2,1,0:T(8,128)S(1)} custom-call(f32[136,128]{1,0:T(8,128)S(1)} %collective-permute-done.2.refs_0_, f32[136,128]{1,0:T(8,128)S(1)} %collective-permute-done.5.refs_0_.refs_1_, f32[136,128]{1,0:T(8,128)S(1)} %collective-permute-done.4.refs_0_.refs_2_, f32[136,128]{1,0:T(8,128)S(1)} %get-tuple-element.29.refs_1_.refs_3_, ...), custom_call_target="tpu_custom_call" | custom-call | tf_op jit(solution)/shard_map/inner/pallas_call | solution.py:497
  15.8 0.0 collective-permute-done.3
  15.8 0.6 %collective-permute-done.6 = f32[88,128]{1,0:T(8,128)S(1)} collective-permute-done((f32[88,128]{1,0:T(8,128)S(1)}, f32[88,128]{1,0:T(8,128)S(1)}, u32[]{:S(2)}, u32[]{:S(2)}) %collective-permute-start.6) | collective-permute-done | bytes 45088 | tf_op jit(solution)/shard_map/ppermute | solution.py:486
  16.5 0.2 %catch.1.refs_0_ = f32[20,8,128]{2,1,0:T(8,128)S(1)} custom-call(f32[176,128]{1,0:T(8,128)S(1)} %pad_maximum_fusion.refs_0_), custom_call_target="tpu_custom_call" | custom-call | tf_op jit(solution)/shard_map/catch/pallas_call | solution.py:488
  16.7 0.6 %collective-permute-done.7.refs_1_ = f32[20,8,128]{2,1,0:T(8,128)S(1)} collective-permute-done((f32[20,8,128]{2,1,0:T(8,128)S(1)}, f32[20,8,128]{2,1,0:T(8,128)S(1)}, u32[]{:S(2)}, u32[]{:S(2)}) %collective-permute-start.7) | collective-permute-done | bytes 81952 | tf_op jit(solution)/shard_map/ppermute | solution.py:487
  17.3 1.5 %outer.1 = (f32[16,4,512]{2,1,0:T(4,128)}, f32[28,4,32,128]{3,2,1,0:T(8,128)S(1)}) custom-call(f32[20,8,128]{2,1,0:T(8,128)S(1)} %catch.1.refs_0_, f32[20,8,128]{2,1,0:T(8,128)S(1)} %collective-permute-done.7.refs_1_, f32[38]{0:T(128)S(4)} %get-tuple-element.40.refs_4_.refs_2_, ...), custom_call_target="tpu_custom_call", output_to_operand_aliasing={{1}: (4, {})} | custom-call | tf_op jit(solution)/shard_map/outer/pallas_call | solution.py:506
  (4 shorter events, 0.1 us)
Async XLA Ops:
  0.0 1.9 %collective-permute-start.1 = (f32[16,4,512]{2,1,0:T(4,128)}, f32[16,4,512]{2,1,0:T(4,128)S(1)}, u32[]{:S(2)}, u32[]{:S(2)}) collective-permute-start(f32[16,4,512]{2,1,0:T(4,128)} %refs_0_.1), channel_id=1, source_target_pairs={{0,1},{1,0},{2,3},{3,2},{4,5},{5,4},{6,7},{7,6},{8,9},{9,8},{10,11... | collective-permute-start | bytes 393224 | tf_op jit(solution)/shard_map/ppermute | solution.py:411
  0.5 1.3 %collective-permute-start = (s32[1,16]{1,0:T(1,128)}, s32[1,16]{1,0:T(1,128)S(1)}, u32[]{:S(2)}, u32[]{:S(2)}) collective-permute-start(s32[1,16]{1,0:T(1,128)} %bitcast.1), channel_id=1, source_target_pairs={{0,1},{1,0},{2,3},{3,2},{4,5},{5,4},{6,7},{7,6},{8,9},{9,8},{10,11... | collective-permute-start | bytes 200 | tf_op jit(solution)/shard_map/ppermute | solution.py:411
  2.0 6.2 %collective-permute-start.2 = (f32[136,128]{1,0:T(8,128)S(1)}, f32[136,128]{1,0:T(8,128)S(1)}, u32[]{:S(2)}, u32[]{:S(2)}) collective-permute-start(f32[136,128]{1,0:T(8,128)S(1)} %pack.4), channel_id=1, source_target_pairs={{0,7},{1,6},{2,5},{3,4},{4,3},{5,2},{6,1},{7,0},{8,15},{9,14},{10,... | collective-permute-start | bytes 208904 | tf_op jit(solution)/shard_map/ppermute | solution.py:411
  5.6 4.6 %collective-permute-start.5 = (f32[136,128]{1,0:T(8,128)S(1)}, f32[136,128]{1,0:T(8,128)S(1)}, u32[]{:S(2)}, u32[]{:S(2)}) collective-permute-start(f32[136,128]{1,0:T(8,128)S(1)} %pack.7), channel_id=1, source_target_pairs={{0,5},{1,4},{2,7},{3,6},{4,1},{5,0},{6,3},{7,2},{8,13},{9,12},{10,... | collective-permute-start | bytes 208904 | tf_op jit(solution)/shard_map/ppermute | solution.py:411
  6.1 4.2 %collective-permute-start.4 = (f32[136,128]{1,0:T(8,128)S(1)}, f32[136,128]{1,0:T(8,128)S(1)}, u32[]{:S(2)}, u32[]{:S(2)}) collective-permute-start(f32[136,128]{1,0:T(8,128)S(1)} %pack.6), channel_id=1, source_target_pairs={{0,3},{1,2},{2,1},{3,0},{4,7},{5,6},{6,5},{7,4},{8,11},{9,10},{10,... | collective-permute-start | bytes 208904 | tf_op jit(solution)/shard_map/ppermute | solution.py:411
  8.2 7.6 %collective-permute-start.3 = (f32[88,128]{1,0:T(8,128)S(1)}, f32[88,128]{1,0:T(8,128)S(1)}, u32[]{:S(2)}, u32[]{:S(2)}) collective-permute-start(f32[88,128]{1,0:T(8,128)S(1)} %get-tuple-element.30), channel_id=1, source_target_pairs={{0,8},{8,16},{16,24},{24,0},{1,9},{9,17},{17,25},{25,1},{2,10},{10... | collective-permute-start | bytes 135176 | tf_op jit(solution)/shard_map/ppermute | solution.py:486
  10.6 5.9 %collective-permute-start.6 = (f32[88,128]{1,0:T(8,128)S(1)}, f32[88,128]{1,0:T(8,128)S(1)}, u32[]{:S(2)}, u32[]{:S(2)}) collective-permute-start(f32[88,128]{1,0:T(8,128)S(1)} %get-tuple-element.38), channel_id=1, source_target_pairs={{0,8},{8,16},{16,24},{24,0},{1,9},{9,17},{17,25},{25,1},{2,10},{10... | collective-permute-start | bytes 135176 | tf_op jit(solution)/shard_map/ppermute | solution.py:486
  12.1 5.2 %collective-permute-start.7 = (f32[20,8,128]{2,1,0:T(8,128)S(1)}, f32[20,8,128]{2,1,0:T(8,128)S(1)}, u32[]{:S(2)}, u32[]{:S(2)}) collective-permute-start(f32[20,8,128]{2,1,0:T(8,128)S(1)} %get-tuple-element.39), channel_id=1, source_target_pairs={{8,0},{16,8},{24,16},{0,24},{9,1},{17,9},{25,17},{1,25},{10,2},{18... | collective-permute-start | bytes 245768 | tf_op jit(solution)/shard_map/ppermute | solution.py:487

commit v7 on v6

--- a/solution.py
+++ b/solution.py
@@ -30,22 +30,23 @@
 
 def route(peers, cap, slots, goal_of, held, label, count):
     for peer in range(peers):
-        count[peer] = 0
-        for k in range(cap):
-            held[peer * cap + k] = 0
-            label[peer * cap + k] = slots
+        count[peer] = peer * cap
+        if peers * cap > slots:
+            for k in range(cap):
+                held[peer * cap + k] = 0
+                label[peer * cap + k] = slots
     for i in range(slots):
-        goal = goal_of(i)
-        peer = lax.div(goal, slots)
-        k = count[peer]
-        count[peer] = k + 1
-        held[peer * cap + k] = i
-        label[peer * cap + k] = lax.rem(goal, slots)
+        peer, slot = goal_of(i)
+        at = count[peer]
+        count[peer] = at + 1
+        held[at] = i
+        label[at] = slot
 
 
 def other_route_kernel(peers, cap, slots, target, held, label, count):
     goals = target[...]
-    route(peers, cap, slots, lambda i: goals[0, i], held, label, count)
+    homes, places = lax.div(goals, slots), lax.rem(goals, slots)
+    route(peers, cap, slots, lambda i: (homes[0, i], places[0, i]), held, label, count)
 
 
 def pack_kernel(peers, cap, flip, held, label, other_held, other_label, fields, other_fields, out, *weights):
@@ -199,7 +200,7 @@
     for copy in copies[1:]:
         copy.wait()
     target, gradient, relaxation, interaction = inside
-    route(peers, cap, slots, lambda i: target[i], held, label, count)
+    route(peers, cap, slots, lambda i: (lax.div(target[i], slots), lax.rem(target[i], slots)), held, label, count)
     for i in range(COMP):
         rate = relaxation[i]
         table[i] = rate

time: 18.9 us -> 18.9 us (level)
  transfers between devices with their start and end apart: 8 -> 8, of which waited for: 5 -> 5; matrix products, arithmetic and copies ran while one was open for 0% -> 0% of each run, Pallas kernels for 19% -> 18%
where the time goes in v7:
time: 18.9 us; the launch traced here: 18.8 us
  starting transfers between devices  10.5 us (56%)
  Pallas kernels  4.98 us (26%)
  waiting for transfers between devices  3.2 us (17%)
    ppermute x5, starting transfers between devices, cross(): return lax.ppermute(array, 'loc', [(i, i ^ flip) for i in range(peers)])  4.76 us
    ppermute x2, starting transfers between devices, per_device(): lax.ppermute(up, 'grp', forward)  3.5 us
    ppermute x1, starting transfers between devices, per_device(): above = lax.ppermute(down, 'grp', backward)  2.25 us
    ppermute x5, waiting for transfers between devices, cross(): return lax.ppermute(array, 'loc', [(i, i ^ flip) for i in range(peers)])  1.96 us
    pallas_call x1, Pallas kernels, per_device(): pl.pallas_call(lambda *refs: outer_kernel(slots, *refs), out_shape=(jax.S...  1.48 us
    pallas_call x1, Pallas kernels, per_device(): pl.pallas_call(lambda *refs: inner_kernel(cap, slots, peers, *refs), out_...  1.41 us
    pallas_call x1, Pallas kernels, per_device(): pl.pallas_call(lambda *refs: stage_kernel(peers, cap, slots, *refs), out_...  0.98 us
    ppermute x2, waiting for transfers between devices, per_device(): lax.ppermute(up, 'grp', forward)  0.65 us
  transfers between devices with their start and end apart: 8, of which 5 were waited for; matrix products, arithmetic and copies ran while one was open for 0% of the time, Pallas kernels for 18%

profile of v7, /device:TPU:0, one launch (start us, length us, event | category | flops | bytes accessed | tf_op | source)
XLA Modules:
  0.0 18.8 jit_solution(8849984383601796178)
XLA Ops:
  0.0 0.5 %collective-permute-start.1 = (f32[16,4,512]{2,1,0:T(4,128)}, f32[16,4,512]{2,1,0:T(4,128)S(1)}, u32[]{:S(2)}, u32[]{:S(2)}) collective-permute-start(f32[16,4,512]{2,1,0:T(4,128)} %refs_0_.1), channel_id=1, source_target_pairs={{0,1},{1,0},{2,3},{3,2},{4,5},{5,4},{6,7},{7,6},{8,9},{9,8},{10,11... | collective-permute-start | bytes 393224 | tf_op jit(solution)/shard_map/ppermute | solution.py:412
  0.5 0.1 collective-permute-start
  0.5 1.0 %stage.1 = (f32[16,4,512]{2,1,0:T(4,128)S(1)}, s32[16]{0:T(128)S(4)}, s32[16]{0:T(128)S(4)}, f32[38]{0:T(128)S(4)}) custom-call(f32[16,4,512]{2,1,0:T(4,128)} %refs_0_.1, s32[16]{0:T(128)} %refs_1_.1, f32[4,4]{1,0:T(4,128)} %refs_2_.1, f32[4]{0:T(128)} %refs_3_.1, f32[3,4,4]{2,1,0:T(4,128)} %refs_4_.1), custom_call_target="tpu_custom_call" | custom-call | tf_op jit(solution)/shard_map/stage/pallas_call | solution.py:416
  1.5 0.2 %collective-permute-done.refs_0_ = s32[1,16]{1,0:T(1,128)S(1)} collective-permute-done((s32[1,16]{1,0:T(1,128)}, s32[1,16]{1,0:T(1,128)S(1)}, u32[]{:S(2)}, u32[]{:S(2)}) %collective-permute-start) | collective-permute-done | bytes 96 | tf_op jit(solution)/shard_map/ppermute | solution.py:412
  1.7 0.2 route.1
  1.9 0.0 collective-permute-done.1.refs_5_
  2.0 3.6 %collective-permute-start.2 = (f32[136,128]{1,0:T(8,128)S(1)}, f32[136,128]{1,0:T(8,128)S(1)}, u32[]{:S(2)}, u32[]{:S(2)}) collective-permute-start(f32[136,128]{1,0:T(8,128)S(1)} %pack.4), channel_id=1, source_target_pairs={{0,7},{1,6},{2,5},{3,4},{4,3},{5,2},{6,1},{7,0},{8,15},{9,14},{10,... | collective-permute-start | bytes 208904 | tf_op jit(solution)/shard_map/ppermute | solution.py:412
  5.6 0.5 %collective-permute-start.5 = (f32[136,128]{1,0:T(8,128)S(1)}, f32[136,128]{1,0:T(8,128)S(1)}, u32[]{:S(2)}, u32[]{:S(2)}) collective-permute-start(f32[136,128]{1,0:T(8,128)S(1)} %pack.7), channel_id=1, source_target_pairs={{0,5},{1,4},{2,7},{3,6},{4,1},{5,0},{6,3},{7,2},{8,13},{9,12},{10,... | collective-permute-start | bytes 208904 | tf_op jit(solution)/shard_map/ppermute | solution.py:412
  6.1 0.1 collective-permute-start.4
  6.3 0.2 pack.5
  6.4 1.7 %collective-permute-done.2.refs_0_ = f32[136,128]{1,0:T(8,128)S(1)} collective-permute-done((f32[136,128]{1,0:T(8,128)S(1)}, f32[136,128]{1,0:T(8,128)S(1)}, u32[]{:S(2)}, u32[]{:S(2)}) %collective-permute-start.2) | collective-permute-done | bytes 69664 | tf_op jit(solution)/shard_map/ppermute | solution.py:412
  8.1 0.1 early.1
  8.2 1.9 %collective-permute-start.3 = (f32[88,128]{1,0:T(8,128)S(1)}, f32[88,128]{1,0:T(8,128)S(1)}, u32[]{:S(2)}, u32[]{:S(2)}) collective-permute-start(f32[88,128]{1,0:T(8,128)S(1)} %get-tuple-element.30), channel_id=1, source_target_pairs={{0,8},{8,16},{16,24},{24,0},{1,9},{9,17},{17,25},{25,1},{2,10},{10... | collective-permute-start | bytes 135176 | tf_op jit(solution)/shard_map/ppermute | solution.py:487
  10.2 0.0 collective-permute-done.5.refs_0_.refs_1_
  10.2 0.1 next.1
  10.3 0.1 collective-permute-done.4.refs_0_.refs_2_
  10.4 0.2 %last.1 = (f32[88,128]{1,0:T(8,128)S(1)}, f32[20,8,128]{2,1,0:T(8,128)S(1)}, f32[72,128]{1,0:T(8,128)S(1)}, f32[72,128]{1,0:T(8,128)S(1)}) custom-call(f32[136,128]{1,0:T(8,128)S(1)} %collective-permute-done.4.refs_0_.refs_2_, f32[88,128]{1,0:T(8,128)S(1)} %get-tuple-element.34.refs_1_, ...), custom_call_target="tpu_custom_call", output_to_operand_aliasing={{0}: (1, {}), {1}: (2, {}), {2}: (3, {}), {3}: (4, {})} | custom-call | tf_op jit(solution)/shard_map/last/pallas_call | solution.py:476
  10.6 1.6 %collective-permute-start.6 = (f32[88,128]{1,0:T(8,128)S(1)}, f32[88,128]{1,0:T(8,128)S(1)}, u32[]{:S(2)}, u32[]{:S(2)}) collective-permute-start(f32[88,128]{1,0:T(8,128)S(1)} %get-tuple-element.38), channel_id=1, source_target_pairs={{0,8},{8,16},{16,24},{24,0},{1,9},{9,17},{17,25},{25,1},{2,10},{10... | collective-permute-start | bytes 135176 | tf_op jit(solution)/shard_map/ppermute | solution.py:487
  12.1 2.2 %collective-permute-start.7 = (f32[20,8,128]{2,1,0:T(8,128)S(1)}, f32[20,8,128]{2,1,0:T(8,128)S(1)}, u32[]{:S(2)}, u32[]{:S(2)}) collective-permute-start(f32[20,8,128]{2,1,0:T(8,128)S(1)} %get-tuple-element.39), channel_id=1, source_target_pairs={{8,0},{16,8},{24,16},{0,24},{9,1},{17,9},{25,17},{1,25},{10,2},{18... | collective-permute-start | bytes 245768 | tf_op jit(solution)/shard_map/ppermute | solution.py:488
  14.4 1.4 %inner.1.refs_4_ = f32[28,4,32,128]{3,2,1,0:T(8,128)S(1)} custom-call(f32[136,128]{1,0:T(8,128)S(1)} %collective-permute-done.2.refs_0_, f32[136,128]{1,0:T(8,128)S(1)} %collective-permute-done.5.refs_0_.refs_1_, f32[136,128]{1,0:T(8,128)S(1)} %collective-permute-done.4.refs_0_.refs_2_, f32[136,128]{1,0:T(8,128)S(1)} %get-tuple-element.29.refs_1_.refs_3_, ...), custom_call_target="tpu_custom_call" | custom-call | tf_op jit(solution)/shard_map/inner/pallas_call | solution.py:498
  15.8 0.0 collective-permute-done.3
  15.8 0.6 %collective-permute-done.6 = f32[88,128]{1,0:T(8,128)S(1)} collective-permute-done((f32[88,128]{1,0:T(8,128)S(1)}, f32[88,128]{1,0:T(8,128)S(1)}, u32[]{:S(2)}, u32[]{:S(2)}) %collective-permute-start.6) | collective-permute-done | bytes 45088 | tf_op jit(solution)/shard_map/ppermute | solution.py:487
  16.5 0.2 %catch.1.refs_0_ = f32[20,8,128]{2,1,0:T(8,128)S(1)} custom-call(f32[176,128]{1,0:T(8,128)S(1)} %pad_maximum_fusion.refs_0_), custom_call_target="tpu_custom_call" | custom-call | tf_op jit(solution)/shard_map/catch/pallas_call | solution.py:489
  16.7 0.6 %collective-permute-done.7.refs_1_ = f32[20,8,128]{2,1,0:T(8,128)S(1)} collective-permute-done((f32[20,8,128]{2,1,0:T(8,128)S(1)}, f32[20,8,128]{2,1,0:T(8,128)S(1)}, u32[]{:S(2)}, u32[]{:S(2)}) %collective-permute-start.7) | collective-permute-done | bytes 81952 | tf_op jit(solution)/shard_map/ppermute | solution.py:488
  17.3 1.5 %outer.1 = (f32[16,4,512]{2,1,0:T(4,128)}, f32[28,4,32,128]{3,2,1,0:T(8,128)S(1)}) custom-call(f32[20,8,128]{2,1,0:T(8,128)S(1)} %catch.1.refs_0_, f32[20,8,128]{2,1,0:T(8,128)S(1)} %collective-permute-done.7.refs_1_, f32[38]{0:T(128)S(4)} %get-tuple-element.40.refs_4_.refs_2_, ...), custom_call_target="tpu_custom_call", output_to_operand_aliasing={{1}: (4, {})} | custom-call | tf_op jit(solution)/shard_map/outer/pallas_call | solution.py:507
  (4 shorter events, 0.1 us)
Async XLA Ops:
  0.0 1.9 %collective-permute-start.1 = (f32[16,4,512]{2,1,0:T(4,128)}, f32[16,4,512]{2,1,0:T(4,128)S(1)}, u32[]{:S(2)}, u32[]{:S(2)}) collective-permute-start(f32[16,4,512]{2,1,0:T(4,128)} %refs_0_.1), channel_id=1, source_target_pairs={{0,1},{1,0},{2,3},{3,2},{4,5},{5,4},{6,7},{7,6},{8,9},{9,8},{10,11... | collective-permute-start | bytes 393224 | tf_op jit(solution)/shard_map/ppermute | solution.py:412
  0.5 1.3 %collective-permute-start = (s32[1,16]{1,0:T(1,128)}, s32[1,16]{1,0:T(1,128)S(1)}, u32[]{:S(2)}, u32[]{:S(2)}) collective-permute-start(s32[1,16]{1,0:T(1,128)} %bitcast.1), channel_id=1, source_target_pairs={{0,1},{1,0},{2,3},{3,2},{4,5},{5,4},{6,7},{7,6},{8,9},{9,8},{10,11... | collective-permute-start | bytes 200 | tf_op jit(solution)/shard_map/ppermute | solution.py:412
  2.0 6.2 %collective-permute-start.2 = (f32[136,128]{1,0:T(8,128)S(1)}, f32[136,128]{1,0:T(8,128)S(1)}, u32[]{:S(2)}, u32[]{:S(2)}) collective-permute-start(f32[136,128]{1,0:T(8,128)S(1)} %pack.4), channel_id=1, source_target_pairs={{0,7},{1,6},{2,5},{3,4},{4,3},{5,2},{6,1},{7,0},{8,15},{9,14},{10,... | collective-permute-start | bytes 208904 | tf_op jit(solution)/shard_map/ppermute | solution.py:412
  5.6 4.6 %collective-permute-start.5 = (f32[136,128]{1,0:T(8,128)S(1)}, f32[136,128]{1,0:T(8,128)S(1)}, u32[]{:S(2)}, u32[]{:S(2)}) collective-permute-start(f32[136,128]{1,0:T(8,128)S(1)} %pack.7), channel_id=1, source_target_pairs={{0,5},{1,4},{2,7},{3,6},{4,1},{5,0},{6,3},{7,2},{8,13},{9,12},{10,... | collective-permute-start | bytes 208904 | tf_op jit(solution)/shard_map/ppermute | solution.py:412
  6.1 4.2 %collective-permute-start.4 = (f32[136,128]{1,0:T(8,128)S(1)}, f32[136,128]{1,0:T(8,128)S(1)}, u32[]{:S(2)}, u32[]{:S(2)}) collective-permute-start(f32[136,128]{1,0:T(8,128)S(1)} %pack.6), channel_id=1, source_target_pairs={{0,3},{1,2},{2,1},{3,0},{4,7},{5,6},{6,5},{7,4},{8,11},{9,10},{10,... | collective-permute-start | bytes 208904 | tf_op jit(solution)/shard_map/ppermute | solution.py:412
  8.2 7.6 %collective-permute-start.3 = (f32[88,128]{1,0:T(8,128)S(1)}, f32[88,128]{1,0:T(8,128)S(1)}, u32[]{:S(2)}, u32[]{:S(2)}) collective-permute-start(f32[88,128]{1,0:T(8,128)S(1)} %get-tuple-element.30), channel_id=1, source_target_pairs={{0,8},{8,16},{16,24},{24,0},{1,9},{9,17},{17,25},{25,1},{2,10},{10... | collective-permute-start | bytes 135176 | tf_op jit(solution)/shard_map/ppermute | solution.py:487
  10.6 5.9 %collective-permute-start.6 = (f32[88,128]{1,0:T(8,128)S(1)}, f32[88,128]{1,0:T(8,128)S(1)}, u32[]{:S(2)}, u32[]{:S(2)}) collective-permute-start(f32[88,128]{1,0:T(8,128)S(1)} %get-tuple-element.38), channel_id=1, source_target_pairs={{0,8},{8,16},{16,24},{24,0},{1,9},{9,17},{17,25},{25,1},{2,10},{10... | collective-permute-start | bytes 135176 | tf_op jit(solution)/shard_map/ppermute | solution.py:487
  12.1 5.2 %collective-permute-start.7 = (f32[20,8,128]{2,1,0:T(8,128)S(1)}, f32[20,8,128]{2,1,0:T(8,128)S(1)}, u32[]{:S(2)}, u32[]{:S(2)}) collective-permute-start(f32[20,8,128]{2,1,0:T(8,128)S(1)} %get-tuple-element.39), channel_id=1, source_target_pairs={{8,0},{16,8},{24,16},{0,24},{9,1},{17,9},{25,17},{1,25},{10,2},{18... | collective-permute-start | bytes 245768 | tf_op jit(solution)/shard_map/ppermute | solution.py:488

commit v8 on v7

--- a/solution.py
+++ b/solution.py
@@ -370,15 +370,14 @@
     copies = [pltpu.make_async_copy(middle, out.at[:, :, LANES : 3 * LANES], sems.at[2])]
     copies[0].start()
 
-    @pl.loop(0, 2)
-    def _(late):
+    for late in range(2):
         places = []
         for end in range(2):
             outside = end * last
-            at = jnp.where(late == 1, BLOCK_NEXT + 1 + end * (CHUNKS - 1), BLOCK + outside)
-            beyond = jnp.where(late == 1, BLOCK_NEXT + outside, BEYOND + end)
-            beside = jnp.where(late == 1, SIDE_NEXT + 1 + end * (CHUNKS - 1), SIDE + outside)
-            to = jnp.where(late == 1, BLOCK, BLOCK_NEXT) + outside
+            at = BLOCK_NEXT + 1 + end * (CHUNKS - 1) if late else BLOCK + outside
+            beyond = BLOCK_NEXT + outside if late else BEYOND + end
+            beside = SIDE_NEXT + 1 + end * (CHUNKS - 1) if late else SIDE + outside
+            to = (BLOCK if late else BLOCK_NEXT) + outside
             up, down = (beyond, at - 1) if end else (at + 1, beyond)
             places.append((at, up, down, beside, to))
         move(slots, work, places, weights, scalars)

time: 18.9 us -> 18.7 us (0.989)
  Pallas kernels: 4.98 us -> 4.76 us
    pallas_call x1, Pallas kernels: 1.48 us -> 1.25 us  [per_device(): pl.pallas_call(lambda *refs: outer_kernel(slots, *refs), out_shape=(jax.S...]
  transfers between devices with their start and end apart: 8 -> 8, of which waited for: 5 -> 5; matrix products, arithmetic and copies ran while one was open for 0% -> 0% of each run, Pallas kernels for 18% -> 19%
where the time goes in v8:
time: 18.7 us; the launch traced here: 18.6 us
  starting transfers between devices  10.5 us (56%)
  Pallas kernels  4.76 us (25%)
  waiting for transfers between devices  3.2 us (17%)
    ppermute x5, starting transfers between devices, cross(): return lax.ppermute(array, 'loc', [(i, i ^ flip) for i in range(peers)])  4.76 us
    ppermute x2, starting transfers between devices, per_device(): lax.ppermute(up, 'grp', forward)  3.5 us
    ppermute x1, starting transfers between devices, per_device(): above = lax.ppermute(down, 'grp', backward)  2.25 us
    ppermute x5, waiting for transfers between devices, cross(): return lax.ppermute(array, 'loc', [(i, i ^ flip) for i in range(peers)])  1.96 us
    pallas_call x1, Pallas kernels, per_device(): pl.pallas_call(lambda *refs: inner_kernel(cap, slots, peers, *refs), out_...  1.41 us
    pallas_call x1, Pallas kernels, per_device(): pl.pallas_call(lambda *refs: outer_kernel(slots, *refs), out_shape=(jax.S...  1.25 us
    pallas_call x1, Pallas kernels, per_device(): pl.pallas_call(lambda *refs: stage_kernel(peers, cap, slots, *refs), out_...  0.98 us
    ppermute x2, waiting for transfers between devices, per_device(): lax.ppermute(up, 'grp', forward)  0.65 us
  transfers between devices with their start and end apart: 8, of which 5 were waited for; matrix products, arithmetic and copies ran while one was open for 0% of the time, Pallas kernels for 19%

profile of v8, /device:TPU:0, one launch (start us, length us, event | category | flops | bytes accessed | tf_op | source)
XLA Modules:
  0.0 18.6 jit_solution(9753939616420876545)
XLA Ops:
  0.0 0.5 %collective-permute-start.1 = (f32[16,4,512]{2,1,0:T(4,128)}, f32[16,4,512]{2,1,0:T(4,128)S(1)}, u32[]{:S(2)}, u32[]{:S(2)}) collective-permute-start(f32[16,4,512]{2,1,0:T(4,128)} %refs_0_.1), channel_id=1, source_target_pairs={{0,1},{1,0},{2,3},{3,2},{4,5},{5,4},{6,7},{7,6},{8,9},{9,8},{10,11... | collective-permute-start | bytes 393224 | tf_op jit(solution)/shard_map/ppermute | solution.py:411
  0.5 0.1 collective-permute-start
  0.5 1.0 %stage.1 = (f32[16,4,512]{2,1,0:T(4,128)S(1)}, s32[16]{0:T(128)S(4)}, s32[16]{0:T(128)S(4)}, f32[38]{0:T(128)S(4)}) custom-call(f32[16,4,512]{2,1,0:T(4,128)} %refs_0_.1, s32[16]{0:T(128)} %refs_1_.1, f32[4,4]{1,0:T(4,128)} %refs_2_.1, f32[4]{0:T(128)} %refs_3_.1, f32[3,4,4]{2,1,0:T(4,128)} %refs_4_.1), custom_call_target="tpu_custom_call" | custom-call | tf_op jit(solution)/shard_map/stage/pallas_call | solution.py:415
  1.5 0.2 %collective-permute-done.refs_0_ = s32[1,16]{1,0:T(1,128)S(1)} collective-permute-done((s32[1,16]{1,0:T(1,128)}, s32[1,16]{1,0:T(1,128)S(1)}, u32[]{:S(2)}, u32[]{:S(2)}) %collective-permute-start) | collective-permute-done | bytes 96 | tf_op jit(solution)/shard_map/ppermute | solution.py:411
  1.7 0.2 route.1
  1.9 0.0 collective-permute-done.1.refs_5_
  2.0 3.6 %collective-permute-start.2 = (f32[136,128]{1,0:T(8,128)S(1)}, f32[136,128]{1,0:T(8,128)S(1)}, u32[]{:S(2)}, u32[]{:S(2)}) collective-permute-start(f32[136,128]{1,0:T(8,128)S(1)} %pack.4), channel_id=1, source_target_pairs={{0,7},{1,6},{2,5},{3,4},{4,3},{5,2},{6,1},{7,0},{8,15},{9,14},{10,... | collective-permute-start | bytes 208904 | tf_op jit(solution)/shard_map/ppermute | solution.py:411
  5.6 0.5 %collective-permute-start.5 = (f32[136,128]{1,0:T(8,128)S(1)}, f32[136,128]{1,0:T(8,128)S(1)}, u32[]{:S(2)}, u32[]{:S(2)}) collective-permute-start(f32[136,128]{1,0:T(8,128)S(1)} %pack.7), channel_id=1, source_target_pairs={{0,5},{1,4},{2,7},{3,6},{4,1},{5,0},{6,3},{7,2},{8,13},{9,12},{10,... | collective-permute-start | bytes 208904 | tf_op jit(solution)/shard_map/ppermute | solution.py:411
  6.1 0.1 collective-permute-start.4
  6.3 0.2 pack.5
  6.4 1.7 %collective-permute-done.2.refs_0_ = f32[136,128]{1,0:T(8,128)S(1)} collective-permute-done((f32[136,128]{1,0:T(8,128)S(1)}, f32[136,128]{1,0:T(8,128)S(1)}, u32[]{:S(2)}, u32[]{:S(2)}) %collective-permute-start.2) | collective-permute-done | bytes 69664 | tf_op jit(solution)/shard_map/ppermute | solution.py:411
  8.1 0.1 early.1
  8.2 1.9 %collective-permute-start.3 = (f32[88,128]{1,0:T(8,128)S(1)}, f32[88,128]{1,0:T(8,128)S(1)}, u32[]{:S(2)}, u32[]{:S(2)}) collective-permute-start(f32[88,128]{1,0:T(8,128)S(1)} %get-tuple-element.30), channel_id=1, source_target_pairs={{0,8},{8,16},{16,24},{24,0},{1,9},{9,17},{17,25},{25,1},{2,10},{10... | collective-permute-start | bytes 135176 | tf_op jit(solution)/shard_map/ppermute | solution.py:486
  10.2 0.0 collective-permute-done.5.refs_0_.refs_1_
  10.2 0.1 next.1
  10.3 0.1 collective-permute-done.4.refs_0_.refs_2_
  10.4 0.2 %last.1 = (f32[88,128]{1,0:T(8,128)S(1)}, f32[20,8,128]{2,1,0:T(8,128)S(1)}, f32[72,128]{1,0:T(8,128)S(1)}, f32[72,128]{1,0:T(8,128)S(1)}) custom-call(f32[136,128]{1,0:T(8,128)S(1)} %collective-permute-done.4.refs_0_.refs_2_, f32[88,128]{1,0:T(8,128)S(1)} %get-tuple-element.34.refs_1_, ...), custom_call_target="tpu_custom_call", output_to_operand_aliasing={{0}: (1, {}), {1}: (2, {}), {2}: (3, {}), {3}: (4, {})} | custom-call | tf_op jit(solution)/shard_map/last/pallas_call | solution.py:475
  10.6 1.6 %collective-permute-start.6 = (f32[88,128]{1,0:T(8,128)S(1)}, f32[88,128]{1,0:T(8,128)S(1)}, u32[]{:S(2)}, u32[]{:S(2)}) collective-permute-start(f32[88,128]{1,0:T(8,128)S(1)} %get-tuple-element.38), channel_id=1, source_target_pairs={{0,8},{8,16},{16,24},{24,0},{1,9},{9,17},{17,25},{25,1},{2,10},{10... | collective-permute-start | bytes 135176 | tf_op jit(solution)/shard_map/ppermute | solution.py:486
  12.1 2.2 %collective-permute-start.7 = (f32[20,8,128]{2,1,0:T(8,128)S(1)}, f32[20,8,128]{2,1,0:T(8,128)S(1)}, u32[]{:S(2)}, u32[]{:S(2)}) collective-permute-start(f32[20,8,128]{2,1,0:T(8,128)S(1)} %get-tuple-element.39), channel_id=1, source_target_pairs={{8,0},{16,8},{24,16},{0,24},{9,1},{17,9},{25,17},{1,25},{10,2},{18... | collective-permute-start | bytes 245768 | tf_op jit(solution)/shard_map/ppermute | solution.py:487
  14.4 1.4 %inner.1.refs_4_ = f32[28,4,32,128]{3,2,1,0:T(8,128)S(1)} custom-call(f32[136,128]{1,0:T(8,128)S(1)} %collective-permute-done.2.refs_0_, f32[136,128]{1,0:T(8,128)S(1)} %collective-permute-done.5.refs_0_.refs_1_, f32[136,128]{1,0:T(8,128)S(1)} %collective-permute-done.4.refs_0_.refs_2_, f32[136,128]{1,0:T(8,128)S(1)} %get-tuple-element.29.refs_1_.refs_3_, ...), custom_call_target="tpu_custom_call" | custom-call | tf_op jit(solution)/shard_map/inner/pallas_call | solution.py:497
  15.8 0.0 collective-permute-done.3
  15.8 0.6 %collective-permute-done.6 = f32[88,128]{1,0:T(8,128)S(1)} collective-permute-done((f32[88,128]{1,0:T(8,128)S(1)}, f32[88,128]{1,0:T(8,128)S(1)}, u32[]{:S(2)}, u32[]{:S(2)}) %collective-permute-start.6) | collective-permute-done | bytes 45088 | tf_op jit(solution)/shard_map/ppermute | solution.py:486
  16.5 0.2 %catch.1.refs_0_ = f32[20,8,128]{2,1,0:T(8,128)S(1)} custom-call(f32[176,128]{1,0:T(8,128)S(1)} %pad_maximum_fusion.refs_0_), custom_call_target="tpu_custom_call" | custom-call | tf_op jit(solution)/shard_map/catch/pallas_call | solution.py:488
  16.7 0.6 %collective-permute-done.7.refs_1_ = f32[20,8,128]{2,1,0:T(8,128)S(1)} collective-permute-done((f32[20,8,128]{2,1,0:T(8,128)S(1)}, f32[20,8,128]{2,1,0:T(8,128)S(1)}, u32[]{:S(2)}, u32[]{:S(2)}) %collective-permute-start.7) | collective-permute-done | bytes 81952 | tf_op jit(solution)/shard_map/ppermute | solution.py:487
  17.3 1.3 %outer.1 = (f32[16,4,512]{2,1,0:T(4,128)}, f32[28,4,32,128]{3,2,1,0:T(8,128)S(1)}) custom-call(f32[20,8,128]{2,1,0:T(8,128)S(1)} %catch.1.refs_0_, f32[20,8,128]{2,1,0:T(8,128)S(1)} %collective-permute-done.7.refs_1_, f32[38]{0:T(128)S(4)} %get-tuple-element.40.refs_4_.refs_2_, ...), custom_call_target="tpu_custom_call", output_to_operand_aliasing={{1}: (4, {})} | custom-call | tf_op jit(solution)/shard_map/outer/pallas_call | solution.py:506
  (4 shorter events, 0.1 us)
Async XLA Ops:
  0.0 1.9 %collective-permute-start.1 = (f32[16,4,512]{2,1,0:T(4,128)}, f32[16,4,512]{2,1,0:T(4,128)S(1)}, u32[]{:S(2)}, u32[]{:S(2)}) collective-permute-start(f32[16,4,512]{2,1,0:T(4,128)} %refs_0_.1), channel_id=1, source_target_pairs={{0,1},{1,0},{2,3},{3,2},{4,5},{5,4},{6,7},{7,6},{8,9},{9,8},{10,11... | collective-permute-start | bytes 393224 | tf_op jit(solution)/shard_map/ppermute | solution.py:411
  0.5 1.3 %collective-permute-start = (s32[1,16]{1,0:T(1,128)}, s32[1,16]{1,0:T(1,128)S(1)}, u32[]{:S(2)}, u32[]{:S(2)}) collective-permute-start(s32[1,16]{1,0:T(1,128)} %bitcast.1), channel_id=1, source_target_pairs={{0,1},{1,0},{2,3},{3,2},{4,5},{5,4},{6,7},{7,6},{8,9},{9,8},{10,11... | collective-permute-start | bytes 200 | tf_op jit(solution)/shard_map/ppermute | solution.py:411
  2.0 6.2 %collective-permute-start.2 = (f32[136,128]{1,0:T(8,128)S(1)}, f32[136,128]{1,0:T(8,128)S(1)}, u32[]{:S(2)}, u32[]{:S(2)}) collective-permute-start(f32[136,128]{1,0:T(8,128)S(1)} %pack.4), channel_id=1, source_target_pairs={{0,7},{1,6},{2,5},{3,4},{4,3},{5,2},{6,1},{7,0},{8,15},{9,14},{10,... | collective-permute-start | bytes 208904 | tf_op jit(solution)/shard_map/ppermute | solution.py:411
  5.6 4.6 %collective-permute-start.5 = (f32[136,128]{1,0:T(8,128)S(1)}, f32[136,128]{1,0:T(8,128)S(1)}, u32[]{:S(2)}, u32[]{:S(2)}) collective-permute-start(f32[136,128]{1,0:T(8,128)S(1)} %pack.7), channel_id=1, source_target_pairs={{0,5},{1,4},{2,7},{3,6},{4,1},{5,0},{6,3},{7,2},{8,13},{9,12},{10,... | collective-permute-start | bytes 208904 | tf_op jit(solution)/shard_map/ppermute | solution.py:411
  6.1 4.2 %collective-permute-start.4 = (f32[136,128]{1,0:T(8,128)S(1)}, f32[136,128]{1,0:T(8,128)S(1)}, u32[]{:S(2)}, u32[]{:S(2)}) collective-permute-start(f32[136,128]{1,0:T(8,128)S(1)} %pack.6), channel_id=1, source_target_pairs={{0,3},{1,2},{2,1},{3,0},{4,7},{5,6},{6,5},{7,4},{8,11},{9,10},{10,... | collective-permute-start | bytes 208904 | tf_op jit(solution)/shard_map/ppermute | solution.py:411
  8.2 7.6 %collective-permute-start.3 = (f32[88,128]{1,0:T(8,128)S(1)}, f32[88,128]{1,0:T(8,128)S(1)}, u32[]{:S(2)}, u32[]{:S(2)}) collective-permute-start(f32[88,128]{1,0:T(8,128)S(1)} %get-tuple-element.30), channel_id=1, source_target_pairs={{0,8},{8,16},{16,24},{24,0},{1,9},{9,17},{17,25},{25,1},{2,10},{10... | collective-permute-start | bytes 135176 | tf_op jit(solution)/shard_map/ppermute | solution.py:486
  10.6 5.9 %collective-permute-start.6 = (f32[88,128]{1,0:T(8,128)S(1)}, f32[88,128]{1,0:T(8,128)S(1)}, u32[]{:S(2)}, u32[]{:S(2)}) collective-permute-start(f32[88,128]{1,0:T(8,128)S(1)} %get-tuple-element.38), channel_id=1, source_target_pairs={{0,8},{8,16},{16,24},{24,0},{1,9},{9,17},{17,25},{25,1},{2,10},{10... | collective-permute-start | bytes 135176 | tf_op jit(solution)/shard_map/ppermute | solution.py:486
  12.1 5.2 %collective-permute-start.7 = (f32[20,8,128]{2,1,0:T(8,128)S(1)}, f32[20,8,128]{2,1,0:T(8,128)S(1)}, u32[]{:S(2)}, u32[]{:S(2)}) collective-permute-start(f32[20,8,128]{2,1,0:T(8,128)S(1)} %get-tuple-element.39), channel_id=1, source_target_pairs={{8,0},{16,8},{24,16},{0,24},{9,1},{17,9},{25,17},{1,25},{10,2},{18... | collective-permute-start | bytes 245768 | tf_op jit(solution)/shard_map/ppermute | solution.py:487
